TPU v7x, 512 devices: a whole 4x4x16 slice. The times are simulated.
512 devices in a mesh: ctx: 256 (over z, y_lo, x, core), mp: 2 (over y_hi).
Axes of the slice: x: 4, y: 4 (y_hi: 2, y_lo: 2; y = y_hi * 2 + y_lo), z: 16, core: 2. Of those that a mesh axis runs over, the one named last changes fastest.
Arguments:
- queries: bfloat16 [32768, 1024], P('ctx', 'mp'), may hold values from -6 to 6
- keys: bfloat16 [32768, 1024], P('ctx', 'mp'), may hold values from -6 to 6
- values: bfloat16 [3, 32768, 1024], P(None, 'ctx', 'mp'), may hold values from -6 to 6
- tile_mask: int32 [256, 15, 1, 1], P('ctx'), may hold values 0 or 1
Outputs:
- attended: bfloat16 [3, 32768, 1024], P(None, 'ctx', 'mp')
All inputs are finite; a program needn't handle non-finite values. No bound on the sum of `tile_mask` on one device may be relied on, other than what follows from the above.
Results may differ from a plain program's by a relative error of at most 0.0049.
Values may be sent and summed in bfloat16 or wider, within the bound.
No kernel may reach another device: no remote copies, remote signals or barrier semaphores. Data moves between devices by JAX's collectives and lax.ppermute only.
A program may use at most 64 MiB of HBM per device.

v0:
```python
import math

import jax
import jax.numpy as jnp
from jax import lax
from jax.sharding import PartitionSpec as P

TILE = 128
HD = 128


def from_behind(array, axis, by):
    size = lax.axis_size(axis)
    return lax.ppermute(array, axis, [(i, (i + by) % size) for i in range(size)])


def expand_live(mask_block):
    offset_ids = lax.broadcasted_iota(jnp.int32, mask_block.shape, 0)
    query_tiles = lax.broadcasted_iota(jnp.int32, mask_block.shape, 1)
    key_tiles = lax.broadcasted_iota(jnp.int32, mask_block.shape, 2)
    live = (mask_block != 0) | (offset_ids == 0) & (query_tiles == key_tiles)
    return jnp.transpose(live, (1, 0, 2))[:, None, :, :, None]


def move_first(blocks, stride):
    return from_behind(blocks, "ctx", stride)


def move_later(blocks, stride):
    return from_behind(blocks, "ctx", stride)


def collect(blocks, mover, loop_size, levels):
    gathered = [blocks]
    for degree in range(levels):
        distance = 2**degree
        gathered.append(mover(blocks, loop_size - distance))
        gathered.append(mover(blocks, distance))
    return jnp.stack(gathered)


def attend(queries, key_stack, value_stack, live):
    scale = 1.0 / math.sqrt(HD)
    head_count = queries.shape[1] // HD
    block_rows = queries.shape[0]
    tile_count = block_rows // TILE
    offset_count = key_stack.shape[0]
    outputs = []
    for head_index in range(head_count):
        window = slice(head_index * HD, (head_index + 1) * HD)
        scores = (
            jnp.einsum(
                "qd,okd->qok",
                queries[:, window],
                key_stack[:, :, window],
                preferred_element_type=jnp.float32,
            )
            * scale
        )
        shaped = scores.reshape(tile_count, TILE, offset_count, tile_count, TILE)
        masked = jnp.where(live, shaped, -1e30)
        largest = jnp.max(masked, axis=(2, 3, 4), keepdims=True)
        expval = jnp.where(live, jnp.exp(masked - largest), 0.0)
        totals = jnp.sum(expval, axis=(2, 3, 4), keepdims=True)
        weights = (
            (expval / totals).astype(jnp.bfloat16).reshape(block_rows, offset_count, block_rows)
        )
        outputs.append(
            jnp.einsum(
                "qok,olkd->lqd",
                weights,
                value_stack[:, :, :, window],
                preferred_element_type=jnp.float32,
            )
        )
    return jnp.concatenate(outputs, axis=2).astype(jnp.bfloat16)


def body(queries, keys, values, tile_mask):
    loop_size = lax.axis_size("ctx")
    levels = loop_size.bit_length() - 2
    live = expand_live(tile_mask[0])
    first = jnp.concatenate([keys[None], values[:1]], axis=0)
    first_stack = collect(first, move_first, loop_size, levels)
    later_stack = collect(values[1:], move_later, loop_size, levels)
    key_stack = first_stack[:, 0]
    value_stack = jnp.concatenate([first_stack[:, 1:], later_stack], axis=1)
    return attend(queries, key_stack, value_stack, live)


def solution(mesh):
    in_specs = (P("ctx", "mp"), P("ctx", "mp"), P(None, "ctx", "mp"), P("ctx", None, None, None))
    out_specs = P(None, "ctx", "mp")
    return jax.shard_map(body, mesh=mesh, in_specs=in_specs, out_specs=out_specs, check_vma=False)
```

profile of v0, /device:TPU:127, one launch (start us, length us, event | category | flops | bytes accessed | tf_op | source)
XLA Modules:
  0.0 217.4 jit_solution(6849644946856028024)
XLA Ops:
  0.0 1.0 slice.50
  1.1 2.6 %collective-permute-start.14 = (bf16[2,128,512]{1,2,0:T(8,128)(2,1)S(1)}, bf16[2,128,512]{1,2,0:T(8,128)(2,1)S(1)}, u32[]{:S(2)}, u32[]{:S(2)}) collective-permute-start(bf16[2,128,512]{1,2,0:T(8,128)(2,1)S(1)} %copy.52), channel_id=1, source_target_pairs={{0,510},{2,0},{4,2},{6,4},{8,6},{10,8},{12,10},{14,12},{16,14},{18... | collective-permute-start | bytes 786440 | tf_op jit(solution)/shard_map/ppermute | solution.py:14
  3.7 7.2 %collective-permute-start.15 = (bf16[2,128,512]{1,2,0:T(8,128)(2,1)S(1)}, bf16[2,128,512]{1,2,0:T(8,128)(2,1)S(1)}, u32[]{:S(2)}, u32[]{:S(2)}) collective-permute-start(bf16[2,128,512]{1,2,0:T(8,128)(2,1)S(1)} %copy.52), channel_id=1, source_target_pairs={{0,2},{2,4},{4,6},{6,8},{8,10},{10,12},{12,14},{14,16},{16,18},{18... | collective-permute-start | bytes 786440 | tf_op jit(solution)/shard_map/ppermute | solution.py:14
  10.9 1.9 collective-permute-start.16
  12.9 0.9 slice.48
  13.8 0.9 pad_maximum_fusion.9
  14.7 1.9 collective-permute-start
  16.7 7.9 %collective-permute-start.1 = (bf16[2,128,512]{2,1,0:T(8,128)(2,1)S(1)}, bf16[2,128,512]{2,1,0:T(8,128)(2,1)S(1)}, u32[]{:S(2)}, u32[]{:S(2)}) collective-permute-start(bf16[2,128,512]{2,1,0:T(8,128)(2,1)S(1)} %pad_maximum_fusion.9), channel_id=1, source_target_pairs={{0,2},{2,4},{4,6},{6,8},{8,10},{10,12},{12,14},{14,16},{16,18},{18... | collective-permute-start | bytes 786440 | tf_op jit(solution)/shard_map/ppermute | solution.py:14
  24.5 0.7 bitcast_dynamic-update-slice_fusion.13
  25.9 0.9 bitcast_dynamic-update-slice_fusion.27
  26.8 1.9 collective-permute-start.2
  28.8 7.6 %collective-permute-start.3 = (bf16[2,128,512]{2,1,0:T(8,128)(2,1)S(1)}, bf16[2,128,512]{2,1,0:T(8,128)(2,1)S(1)}, u32[]{:S(2)}, u32[]{:S(2)}) collective-permute-start(bf16[2,128,512]{2,1,0:T(8,128)(2,1)S(1)} %pad_maximum_fusion.9), channel_id=1, source_target_pairs={{0,4},{2,6},{4,8},{6,10},{8,12},{10,14},{12,16},{14,18},{16,20},{1... | collective-permute-start | bytes 786440 | tf_op jit(solution)/shard_map/ppermute | solution.py:14
  36.4 1.8 collective-permute-done.2
  38.2 1.9 collective-permute-start.4
  40.1 3.9 %collective-permute-done.3 = bf16[2,128,512]{2,1,0:T(8,128)(2,1)S(1)} collective-permute-done((bf16[2,128,512]{2,1,0:T(8,128)(2,1)S(1)}, bf16[2,128,512]{2,1,0:T(8,128)(2,1)S(1)}, u32[]{:S(2)}, u32[]{:S(2)}) %collective-permute-start.3) | collective-permute-done | bytes 262176 | tf_op jit(solution)/shard_map/ppermute | solution.py:14
  44.0 7.6 %collective-permute-start.5 = (bf16[2,128,512]{2,1,0:T(8,128)(2,1)S(1)}, bf16[2,128,512]{2,1,0:T(8,128)(2,1)S(1)}, u32[]{:S(2)}, u32[]{:S(2)}) collective-permute-start(bf16[2,128,512]{2,1,0:T(8,128)(2,1)S(1)} %pad_maximum_fusion.9), channel_id=1, source_target_pairs={{0,8},{2,10},{4,12},{6,14},{8,16},{10,18},{12,20},{14,22},{16,24},... | collective-permute-start | bytes 786440 | tf_op jit(solution)/shard_map/ppermute | solution.py:14
  51.9 1.9 collective-permute-start.6
  53.8 2.7 %collective-permute-done.5 = bf16[2,128,512]{2,1,0:T(8,128)(2,1)S(1)} collective-permute-done((bf16[2,128,512]{2,1,0:T(8,128)(2,1)S(1)}, bf16[2,128,512]{2,1,0:T(8,128)(2,1)S(1)}, u32[]{:S(2)}, u32[]{:S(2)}) %collective-permute-start.5) | collective-permute-done | bytes 262176 | tf_op jit(solution)/shard_map/ppermute | solution.py:14
  56.5 3.2 %collective-permute-start.7 = (bf16[2,128,512]{2,1,0:T(8,128)(2,1)S(1)}, bf16[2,128,512]{2,1,0:T(8,128)(2,1)S(1)}, u32[]{:S(2)}, u32[]{:S(2)}) collective-permute-start(bf16[2,128,512]{2,1,0:T(8,128)(2,1)S(1)} %pad_maximum_fusion.9), channel_id=1, source_target_pairs={{0,16},{2,18},{4,20},{6,22},{8,24},{10,26},{12,28},{14,30},{16,32}... | collective-permute-start | bytes 786440 | tf_op jit(solution)/shard_map/ppermute | solution.py:14
  59.8 4.7 %collective-permute-done.6 = bf16[2,128,512]{2,1,0:T(8,128)(2,1)S(1)} collective-permute-done((bf16[2,128,512]{2,1,0:T(8,128)(2,1)S(1)}, bf16[2,128,512]{2,1,0:T(8,128)(2,1)S(1)}, u32[]{:S(2)}, u32[]{:S(2)}) %collective-permute-start.6) | collective-permute-done | bytes 262176 | tf_op jit(solution)/shard_map/ppermute | solution.py:14
  64.5 1.9 collective-permute-start.8
  66.5 3.2 %collective-permute-done.7 = bf16[2,128,512]{2,1,0:T(8,128)(2,1)S(1)} collective-permute-done((bf16[2,128,512]{2,1,0:T(8,128)(2,1)S(1)}, bf16[2,128,512]{2,1,0:T(8,128)(2,1)S(1)}, u32[]{:S(2)}, u32[]{:S(2)}) %collective-permute-start.7) | collective-permute-done | bytes 262176 | tf_op jit(solution)/shard_map/ppermute | solution.py:14
  69.7 1.9 collective-permute-start.9
  71.7 2.4 %collective-permute-done.8 = bf16[2,128,512]{2,1,0:T(8,128)(2,1)S(1)} collective-permute-done((bf16[2,128,512]{2,1,0:T(8,128)(2,1)S(1)}, bf16[2,128,512]{2,1,0:T(8,128)(2,1)S(1)}, u32[]{:S(2)}, u32[]{:S(2)}) %collective-permute-start.8) | collective-permute-done | bytes 262176 | tf_op jit(solution)/shard_map/ppermute | solution.py:14
  74.1 1.9 collective-permute-start.10
  76.0 3.0 %collective-permute-done.9 = bf16[2,128,512]{2,1,0:T(8,128)(2,1)S(1)} collective-permute-done((bf16[2,128,512]{2,1,0:T(8,128)(2,1)S(1)}, bf16[2,128,512]{2,1,0:T(8,128)(2,1)S(1)}, u32[]{:S(2)}, u32[]{:S(2)}) %collective-permute-start.9) | collective-permute-done | bytes 262176 | tf_op jit(solution)/shard_map/ppermute | solution.py:14
  79.0 2.5 %collective-permute-start.11 = (bf16[2,128,512]{2,1,0:T(8,128)(2,1)S(1)}, bf16[2,128,512]{2,1,0:T(8,128)(2,1)S(1)}, u32[]{:S(2)}, u32[]{:S(2)}) collective-permute-start(bf16[2,128,512]{2,1,0:T(8,128)(2,1)S(1)} %pad_maximum_fusion.9), channel_id=1, source_target_pairs={{0,64},{2,66},{4,68},{6,70},{8,72},{10,74},{12,76},{14,78},{16,80}... | collective-permute-start | bytes 786440 | tf_op jit(solution)/shard_map/ppermute | solution.py:14
  81.5 9.2 %collective-permute-done.10 = bf16[2,128,512]{2,1,0:T(8,128)(2,1)S(1)} collective-permute-done((bf16[2,128,512]{2,1,0:T(8,128)(2,1)S(1)}, bf16[2,128,512]{2,1,0:T(8,128)(2,1)S(1)}, u32[]{:S(2)}, u32[]{:S(2)}) %collective-permute-start.10) | collective-permute-done | bytes 262176 | tf_op jit(solution)/shard_map/ppermute | solution.py:14
  90.7 8.5 %collective-permute-start.12 = (bf16[2,128,512]{2,1,0:T(8,128)(2,1)S(1)}, bf16[2,128,512]{2,1,0:T(8,128)(2,1)S(1)}, u32[]{:S(2)}, u32[]{:S(2)}) collective-permute-start(bf16[2,128,512]{2,1,0:T(8,128)(2,1)S(1)} %pad_maximum_fusion.9), channel_id=1, source_target_pairs={{0,384},{2,386},{4,388},{6,390},{8,392},{10,394},{12,396},{14,398}... | collective-permute-start | bytes 786440 | tf_op jit(solution)/shard_map/ppermute | solution.py:14
  99.2 4.2 %collective-permute-start.13 = (bf16[2,128,512]{2,1,0:T(8,128)(2,1)S(1)}, bf16[2,128,512]{2,1,0:T(8,128)(2,1)S(1)}, u32[]{:S(2)}, u32[]{:S(2)}) collective-permute-start(bf16[2,128,512]{2,1,0:T(8,128)(2,1)S(1)} %pad_maximum_fusion.9), channel_id=1, source_target_pairs={{0,128},{2,130},{4,132},{6,134},{8,136},{10,138},{12,140},{14,142}... | collective-permute-start | bytes 786440 | tf_op jit(solution)/shard_map/ppermute | solution.py:14
  103.4 18.5 %collective-permute-done.12 = bf16[2,128,512]{2,1,0:T(8,128)(2,1)S(1)} collective-permute-done((bf16[2,128,512]{2,1,0:T(8,128)(2,1)S(1)}, bf16[2,128,512]{2,1,0:T(8,128)(2,1)S(1)}, u32[]{:S(2)}, u32[]{:S(2)}) %collective-permute-start.12) | collective-permute-done | bytes 262176 | tf_op jit(solution)/shard_map/ppermute | solution.py:14
  121.9 5.3 %collective-permute-start.17 = (bf16[2,128,512]{1,2,0:T(8,128)(2,1)S(1)}, bf16[2,128,512]{1,2,0:T(8,128)(2,1)S(1)}, u32[]{:S(2)}, u32[]{:S(2)}) collective-permute-start(bf16[2,128,512]{1,2,0:T(8,128)(2,1)S(1)} %copy.52), channel_id=1, source_target_pairs={{0,4},{2,6},{4,8},{6,10},{8,12},{10,14},{12,16},{14,18},{16,20},{1... | collective-permute-start | bytes 786440 | tf_op jit(solution)/shard_map/ppermute | solution.py:14
  127.3 6.5 %collective-permute-start.18 = (bf16[2,128,512]{1,2,0:T(8,128)(2,1)S(1)}, bf16[2,128,512]{1,2,0:T(8,128)(2,1)S(1)}, u32[]{:S(2)}, u32[]{:S(2)}) collective-permute-start(bf16[2,128,512]{1,2,0:T(8,128)(2,1)S(1)} %copy.52), channel_id=1, source_target_pairs={{0,504},{2,506},{4,508},{6,510},{8,0},{10,2},{12,4},{14,6},{16,8},... | collective-permute-start | bytes 786440 | tf_op jit(solution)/shard_map/ppermute | solution.py:14
  137.2 3.3 %collective-permute-start.19 = (bf16[2,128,512]{1,2,0:T(8,128)(2,1)S(1)}, bf16[2,128,512]{1,2,0:T(8,128)(2,1)S(1)}, u32[]{:S(2)}, u32[]{:S(2)}) collective-permute-start(bf16[2,128,512]{1,2,0:T(8,128)(2,1)S(1)} %copy.52), channel_id=1, source_target_pairs={{0,8},{2,10},{4,12},{6,14},{8,16},{10,18},{12,20},{14,22},{16,24},... | collective-permute-start | bytes 786440 | tf_op jit(solution)/shard_map/ppermute | solution.py:14
  140.5 0.7 bitcast_dynamic-update-slice_fusion.12
  141.2 1.9 collective-permute-start.20
  143.1 0.7 bitcast_dynamic-update-slice_fusion.11
  143.9 5.5 %collective-permute-start.21 = (bf16[2,128,512]{1,2,0:T(8,128)(2,1)S(1)}, bf16[2,128,512]{1,2,0:T(8,128)(2,1)S(1)}, u32[]{:S(2)}, u32[]{:S(2)}) collective-permute-start(bf16[2,128,512]{1,2,0:T(8,128)(2,1)S(1)} %copy.52), channel_id=1, source_target_pairs={{0,16},{2,18},{4,20},{6,22},{8,24},{10,26},{12,28},{14,30},{16,32}... | collective-permute-start | bytes 786440 | tf_op jit(solution)/shard_map/ppermute | solution.py:14
  149.3 0.7 bitcast_dynamic-update-slice_fusion.10
  150.1 1.9 collective-permute-start.22
  152.0 0.7 bitcast_dynamic-update-slice_fusion.9
  152.7 4.6 %collective-permute-start.23 = (bf16[2,128,512]{1,2,0:T(8,128)(2,1)S(1)}, bf16[2,128,512]{1,2,0:T(8,128)(2,1)S(1)}, u32[]{:S(2)}, u32[]{:S(2)}) collective-permute-start(bf16[2,128,512]{1,2,0:T(8,128)(2,1)S(1)} %copy.52), channel_id=1, source_target_pairs={{0,32},{2,34},{4,36},{6,38},{8,40},{10,42},{12,44},{14,46},{16,48}... | collective-permute-start | bytes 786440 | tf_op jit(solution)/shard_map/ppermute | solution.py:14
  157.3 0.7 bitcast_dynamic-update-slice_fusion.8
  158.0 1.9 collective-permute-start.24
  159.9 0.7 bitcast_dynamic-update-slice_fusion.7
  160.7 5.5 %collective-permute-start.25 = (bf16[2,128,512]{1,2,0:T(8,128)(2,1)S(1)}, bf16[2,128,512]{1,2,0:T(8,128)(2,1)S(1)}, u32[]{:S(2)}, u32[]{:S(2)}) collective-permute-start(bf16[2,128,512]{1,2,0:T(8,128)(2,1)S(1)} %copy.52), channel_id=1, source_target_pairs={{0,64},{2,66},{4,68},{6,70},{8,72},{10,74},{12,76},{14,78},{16,80}... | collective-permute-start | bytes 786440 | tf_op jit(solution)/shard_map/ppermute | solution.py:14
  166.1 0.7 bitcast_dynamic-update-slice_fusion.6
  166.9 8.0 %collective-permute-start.26 = (bf16[2,128,512]{1,2,0:T(8,128)(2,1)S(1)}, bf16[2,128,512]{1,2,0:T(8,128)(2,1)S(1)}, u32[]{:S(2)}, u32[]{:S(2)}) collective-permute-start(bf16[2,128,512]{1,2,0:T(8,128)(2,1)S(1)} %copy.52), channel_id=1, source_target_pairs={{0,384},{2,386},{4,388},{6,390},{8,392},{10,394},{12,396},{14,398}... | collective-permute-start | bytes 786440 | tf_op jit(solution)/shard_map/ppermute | solution.py:14
  174.9 0.7 bitcast_dynamic-update-slice_fusion.5
  175.6 1.9 collective-permute-start.27
  177.6 0.7 bitcast_dynamic-update-slice_fusion.4
  178.3 0.7 bitcast_dynamic-update-slice_fusion.3
  179.0 0.7 bitcast_dynamic-update-slice_fusion.2
  180.1 0.7 bitcast_dynamic-update-slice_fusion.1
  180.8 2.3 %copy.34 = bf16[15,1,128,512]{2,3,0,1:T(8,128)(2,1)} copy(bf16[15,1,128,512]{3,2,0,1:T(8,128)(2,1)S(1)} %get-tuple-element.10) | data formatting | bytes 3932160 | tf_op jit(solution)/shard_map/slice | solution.py:87
  183.1 13.4 %collective-permute-done.26 = bf16[2,128,512]{1,2,0:T(8,128)(2,1)S(1)} collective-permute-done((bf16[2,128,512]{1,2,0:T(8,128)(2,1)S(1)}, bf16[2,128,512]{1,2,0:T(8,128)(2,1)S(1)}, u32[]{:S(2)}, u32[]{:S(2)}) %collective-permute-start.26) | collective-permute-done | bytes 262176 | tf_op jit(solution)/shard_map/ppermute | solution.py:14
  196.5 0.7 bitcast_dynamic-update-slice_fusion
  197.3 9.6 %collective-permute-done.27 = bf16[2,128,512]{1,2,0:T(8,128)(2,1)} collective-permute-done((bf16[2,128,512]{1,2,0:T(8,128)(2,1)S(1)}, bf16[2,128,512]{1,2,0:T(8,128)(2,1)}, u32[]{:S(2)}, u32[]{:S(2)}) %collective-permute-start.27) | collective-permute-done | bytes 262176 | tf_op jit(solution)/shard_map/ppermute | solution.py:14
  206.8 1.7 bitcast_dynamic-update-slice_fusion.28
  208.5 2.3 %fusion.44 = bf16[3,128,128]{1,2,0:T(8,128)(2,1)S(1)} fusion(bf16[15,2,128,512]{2,3,0,1:T(8,128)(2,1)} %bitcast_dynamic-update-slice_fusion.28, bf16[15,1,128,512]{2,3,0,1:T(8,128)(2,1)} %copy.34, f32[15,128,128]{2,1,0:T(8,128)} %copy-done.3, f32[128]{0:T(128)S(1)} %get-tuple-element.8, f32[128]{0:T(128)S(1)} %get-tuple-element.17, ...), kind=kOutput, calls=%fused_computation.35 | convolution fusion | flops 192724992 | bytes 6980623 | tf_op jit(solution)/shard_map/qok,olkd->lqd/dot_general | solution.py:69
  210.8 1.9 fusion.35
  212.8 1.8 fusion.41
  214.6 1.8 fusion.38
  216.5 0.9 copy.39
  (54 shorter events, 5.1 us)
Async XLA Ops:
  1.1 136.1 %collective-permute-start.14 = (bf16[2,128,512]{1,2,0:T(8,128)(2,1)S(1)}, bf16[2,128,512]{1,2,0:T(8,128)(2,1)S(1)}, u32[]{:S(2)}, u32[]{:S(2)}) collective-permute-start(bf16[2,128,512]{1,2,0:T(8,128)(2,1)S(1)} %copy.52), channel_id=1, source_target_pairs={{0,510},{2,0},{4,2},{6,4},{8,6},{10,8},{12,10},{14,12},{16,14},{18... | collective-permute-start | bytes 786440 | tf_op jit(solution)/shard_map/ppermute | solution.py:14
  3.7 137.5 %collective-permute-start.15 = (bf16[2,128,512]{1,2,0:T(8,128)(2,1)S(1)}, bf16[2,128,512]{1,2,0:T(8,128)(2,1)S(1)}, u32[]{:S(2)}, u32[]{:S(2)}) collective-permute-start(bf16[2,128,512]{1,2,0:T(8,128)(2,1)S(1)} %copy.52), channel_id=1, source_target_pairs={{0,2},{2,4},{4,6},{6,8},{8,10},{10,12},{12,14},{14,16},{16,18},{18... | collective-permute-start | bytes 786440 | tf_op jit(solution)/shard_map/ppermute | solution.py:14
  10.9 132.9 %collective-permute-start.16 = (bf16[2,128,512]{1,2,0:T(8,128)(2,1)S(1)}, bf16[2,128,512]{1,2,0:T(8,128)(2,1)S(1)}, u32[]{:S(2)}, u32[]{:S(2)}) collective-permute-start(bf16[2,128,512]{1,2,0:T(8,128)(2,1)S(1)} %copy.52), channel_id=1, source_target_pairs={{0,508},{2,510},{4,0},{6,2},{8,4},{10,6},{12,8},{14,10},{16,12},{1... | collective-permute-start | bytes 786440 | tf_op jit(solution)/shard_map/ppermute | solution.py:14
  14.7 12.1 %collective-permute-start = (bf16[2,128,512]{2,1,0:T(8,128)(2,1)S(1)}, bf16[2,128,512]{2,1,0:T(8,128)(2,1)S(1)}, u32[]{:S(2)}, u32[]{:S(2)}) collective-permute-start(bf16[2,128,512]{2,1,0:T(8,128)(2,1)S(1)} %pad_maximum_fusion.9), channel_id=1, source_target_pairs={{0,510},{2,0},{4,2},{6,4},{8,6},{10,8},{12,10},{14,12},{16,14},{18... | collective-permute-start | bytes 786440 | tf_op jit(solution)/shard_map/ppermute | solution.py:14
  16.7 12.1 %collective-permute-start.1 = (bf16[2,128,512]{2,1,0:T(8,128)(2,1)S(1)}, bf16[2,128,512]{2,1,0:T(8,128)(2,1)S(1)}, u32[]{:S(2)}, u32[]{:S(2)}) collective-permute-start(bf16[2,128,512]{2,1,0:T(8,128)(2,1)S(1)} %pad_maximum_fusion.9), channel_id=1, source_target_pairs={{0,2},{2,4},{4,6},{6,8},{8,10},{10,12},{12,14},{14,16},{16,18},{18... | collective-permute-start | bytes 786440 | tf_op jit(solution)/shard_map/ppermute | solution.py:14
  26.8 11.3 %collective-permute-start.2 = (bf16[2,128,512]{2,1,0:T(8,128)(2,1)S(1)}, bf16[2,128,512]{2,1,0:T(8,128)(2,1)S(1)}, u32[]{:S(2)}, u32[]{:S(2)}) collective-permute-start(bf16[2,128,512]{2,1,0:T(8,128)(2,1)S(1)} %pad_maximum_fusion.9), channel_id=1, source_target_pairs={{0,508},{2,510},{4,0},{6,2},{8,4},{10,6},{12,8},{14,10},{16,12},{1... | collective-permute-start | bytes 786440 | tf_op jit(solution)/shard_map/ppermute | solution.py:14
  28.8 15.2 %collective-permute-start.3 = (bf16[2,128,512]{2,1,0:T(8,128)(2,1)S(1)}, bf16[2,128,512]{2,1,0:T(8,128)(2,1)S(1)}, u32[]{:S(2)}, u32[]{:S(2)}) collective-permute-start(bf16[2,128,512]{2,1,0:T(8,128)(2,1)S(1)} %pad_maximum_fusion.9), channel_id=1, source_target_pairs={{0,4},{2,6},{4,8},{6,10},{8,12},{10,14},{12,16},{14,18},{16,20},{1... | collective-permute-start | bytes 786440 | tf_op jit(solution)/shard_map/ppermute | solution.py:14
  38.2 13.7 %collective-permute-start.4 = (bf16[2,128,512]{2,1,0:T(8,128)(2,1)S(1)}, bf16[2,128,512]{2,1,0:T(8,128)(2,1)S(1)}, u32[]{:S(2)}, u32[]{:S(2)}) collective-permute-start(bf16[2,128,512]{2,1,0:T(8,128)(2,1)S(1)} %pad_maximum_fusion.9), channel_id=1, source_target_pairs={{0,504},{2,506},{4,508},{6,510},{8,0},{10,2},{12,4},{14,6},{16,8},... | collective-permute-start | bytes 786440 | tf_op jit(solution)/shard_map/ppermute | solution.py:14
  44.0 12.5 %collective-permute-start.5 = (bf16[2,128,512]{2,1,0:T(8,128)(2,1)S(1)}, bf16[2,128,512]{2,1,0:T(8,128)(2,1)S(1)}, u32[]{:S(2)}, u32[]{:S(2)}) collective-permute-start(bf16[2,128,512]{2,1,0:T(8,128)(2,1)S(1)} %pad_maximum_fusion.9), channel_id=1, source_target_pairs={{0,8},{2,10},{4,12},{6,14},{8,16},{10,18},{12,20},{14,22},{16,24},... | collective-permute-start | bytes 786440 | tf_op jit(solution)/shard_map/ppermute | solution.py:14
  51.9 12.7 %collective-permute-start.6 = (bf16[2,128,512]{2,1,0:T(8,128)(2,1)S(1)}, bf16[2,128,512]{2,1,0:T(8,128)(2,1)S(1)}, u32[]{:S(2)}, u32[]{:S(2)}) collective-permute-start(bf16[2,128,512]{2,1,0:T(8,128)(2,1)S(1)} %pad_maximum_fusion.9), channel_id=1, source_target_pairs={{0,496},{2,498},{4,500},{6,502},{8,504},{10,506},{12,508},{14,510}... | collective-permute-start | bytes 786440 | tf_op jit(solution)/shard_map/ppermute | solution.py:14
  56.5 13.2 %collective-permute-start.7 = (bf16[2,128,512]{2,1,0:T(8,128)(2,1)S(1)}, bf16[2,128,512]{2,1,0:T(8,128)(2,1)S(1)}, u32[]{:S(2)}, u32[]{:S(2)}) collective-permute-start(bf16[2,128,512]{2,1,0:T(8,128)(2,1)S(1)} %pad_maximum_fusion.9), channel_id=1, source_target_pairs={{0,16},{2,18},{4,20},{6,22},{8,24},{10,26},{12,28},{14,30},{16,32}... | collective-permute-start | bytes 786440 | tf_op jit(solution)/shard_map/ppermute | solution.py:14
  64.5 9.5 %collective-permute-start.8 = (bf16[2,128,512]{2,1,0:T(8,128)(2,1)S(1)}, bf16[2,128,512]{2,1,0:T(8,128)(2,1)S(1)}, u32[]{:S(2)}, u32[]{:S(2)}) collective-permute-start(bf16[2,128,512]{2,1,0:T(8,128)(2,1)S(1)} %pad_maximum_fusion.9), channel_id=1, source_target_pairs={{0,480},{2,482},{4,484},{6,486},{8,488},{10,490},{12,492},{14,494}... | collective-permute-start | bytes 786440 | tf_op jit(solution)/shard_map/ppermute | solution.py:14
  69.7 9.3 %collective-permute-start.9 = (bf16[2,128,512]{2,1,0:T(8,128)(2,1)S(1)}, bf16[2,128,512]{2,1,0:T(8,128)(2,1)S(1)}, u32[]{:S(2)}, u32[]{:S(2)}) collective-permute-start(bf16[2,128,512]{2,1,0:T(8,128)(2,1)S(1)} %pad_maximum_fusion.9), channel_id=1, source_target_pairs={{0,32},{2,34},{4,36},{6,38},{8,40},{10,42},{12,44},{14,46},{16,48}... | collective-permute-start | bytes 786440 | tf_op jit(solution)/shard_map/ppermute | solution.py:14
  74.1 16.7 %collective-permute-start.10 = (bf16[2,128,512]{2,1,0:T(8,128)(2,1)S(1)}, bf16[2,128,512]{2,1,0:T(8,128)(2,1)S(1)}, u32[]{:S(2)}, u32[]{:S(2)}) collective-permute-start(bf16[2,128,512]{2,1,0:T(8,128)(2,1)S(1)} %pad_maximum_fusion.9), channel_id=1, source_target_pairs={{0,448},{2,450},{4,452},{6,454},{8,456},{10,458},{12,460},{14,462}... | collective-permute-start | bytes 786440 | tf_op jit(solution)/shard_map/ppermute | solution.py:14
  79.0 20.2 %collective-permute-start.11 = (bf16[2,128,512]{2,1,0:T(8,128)(2,1)S(1)}, bf16[2,128,512]{2,1,0:T(8,128)(2,1)S(1)}, u32[]{:S(2)}, u32[]{:S(2)}) collective-permute-start(bf16[2,128,512]{2,1,0:T(8,128)(2,1)S(1)} %pad_maximum_fusion.9), channel_id=1, source_target_pairs={{0,64},{2,66},{4,68},{6,70},{8,72},{10,74},{12,76},{14,78},{16,80}... | collective-permute-start | bytes 786440 | tf_op jit(solution)/shard_map/ppermute | solution.py:14
  90.7 31.2 %collective-permute-start.12 = (bf16[2,128,512]{2,1,0:T(8,128)(2,1)S(1)}, bf16[2,128,512]{2,1,0:T(8,128)(2,1)S(1)}, u32[]{:S(2)}, u32[]{:S(2)}) collective-permute-start(bf16[2,128,512]{2,1,0:T(8,128)(2,1)S(1)} %pad_maximum_fusion.9), channel_id=1, source_target_pairs={{0,384},{2,386},{4,388},{6,390},{8,392},{10,394},{12,396},{14,398}... | collective-permute-start | bytes 786440 | tf_op jit(solution)/shard_map/ppermute | solution.py:14
  99.2 28.1 %collective-permute-start.13 = (bf16[2,128,512]{2,1,0:T(8,128)(2,1)S(1)}, bf16[2,128,512]{2,1,0:T(8,128)(2,1)S(1)}, u32[]{:S(2)}, u32[]{:S(2)}) collective-permute-start(bf16[2,128,512]{2,1,0:T(8,128)(2,1)S(1)} %pad_maximum_fusion.9), channel_id=1, source_target_pairs={{0,128},{2,130},{4,132},{6,134},{8,136},{10,138},{12,140},{14,142}... | collective-permute-start | bytes 786440 | tf_op jit(solution)/shard_map/ppermute | solution.py:14
  121.9 28.1 %collective-permute-start.17 = (bf16[2,128,512]{1,2,0:T(8,128)(2,1)S(1)}, bf16[2,128,512]{1,2,0:T(8,128)(2,1)S(1)}, u32[]{:S(2)}, u32[]{:S(2)}) collective-permute-start(bf16[2,128,512]{1,2,0:T(8,128)(2,1)S(1)} %copy.52), channel_id=1, source_target_pairs={{0,4},{2,6},{4,8},{6,10},{8,12},{10,14},{12,16},{14,18},{16,20},{1... | collective-permute-start | bytes 786440 | tf_op jit(solution)/shard_map/ppermute | solution.py:14
  127.3 25.4 %collective-permute-start.18 = (bf16[2,128,512]{1,2,0:T(8,128)(2,1)S(1)}, bf16[2,128,512]{1,2,0:T(8,128)(2,1)S(1)}, u32[]{:S(2)}, u32[]{:S(2)}) collective-permute-start(bf16[2,128,512]{1,2,0:T(8,128)(2,1)S(1)} %copy.52), channel_id=1, source_target_pairs={{0,504},{2,506},{4,508},{6,510},{8,0},{10,2},{12,4},{14,6},{16,8},... | collective-permute-start | bytes 786440 | tf_op jit(solution)/shard_map/ppermute | solution.py:14
  133.9 0.9 copy-start.6
  135.2 2.0 copy-start.3
  136.1 21.9 %copy-start.1 = (f32[15,128,128]{2,1,0:T(8,128)}, f32[15,128,128]{2,1,0:T(8,128)S(1)}, u32[]{:S(2)}) copy-start(f32[15,128,128]{2,1,0:T(8,128)S(1)} %get-tuple-element.14) | copy-start | bytes 2949124
  136.5 39.1 %copy-start.4 = (f32[15,128,128]{2,1,0:T(8,128)}, f32[15,128,128]{2,1,0:T(8,128)S(1)}, u32[]{:S(2)}) copy-start(f32[15,128,128]{2,1,0:T(8,128)S(1)} %get-tuple-element.16) | copy-start | bytes 2949124
  137.2 20.8 %collective-permute-start.19 = (bf16[2,128,512]{1,2,0:T(8,128)(2,1)S(1)}, bf16[2,128,512]{1,2,0:T(8,128)(2,1)S(1)}, u32[]{:S(2)}, u32[]{:S(2)}) collective-permute-start(bf16[2,128,512]{1,2,0:T(8,128)(2,1)S(1)} %copy.52), channel_id=1, source_target_pairs={{0,8},{2,10},{4,12},{6,14},{8,16},{10,18},{12,20},{14,22},{16,24},... | collective-permute-start | bytes 786440 | tf_op jit(solution)/shard_map/ppermute | solution.py:14
  141.2 19.4 %collective-permute-start.20 = (bf16[2,128,512]{1,2,0:T(8,128)(2,1)S(1)}, bf16[2,128,512]{1,2,0:T(8,128)(2,1)S(1)}, u32[]{:S(2)}, u32[]{:S(2)}) collective-permute-start(bf16[2,128,512]{1,2,0:T(8,128)(2,1)S(1)} %copy.52), channel_id=1, source_target_pairs={{0,496},{2,498},{4,500},{6,502},{8,504},{10,506},{12,508},{14,510}... | collective-permute-start | bytes 786440 | tf_op jit(solution)/shard_map/ppermute | solution.py:14
  143.9 23.0 %collective-permute-start.21 = (bf16[2,128,512]{1,2,0:T(8,128)(2,1)S(1)}, bf16[2,128,512]{1,2,0:T(8,128)(2,1)S(1)}, u32[]{:S(2)}, u32[]{:S(2)}) collective-permute-start(bf16[2,128,512]{1,2,0:T(8,128)(2,1)S(1)} %copy.52), channel_id=1, source_target_pairs={{0,16},{2,18},{4,20},{6,22},{8,24},{10,26},{12,28},{14,30},{16,32}... | collective-permute-start | bytes 786440 | tf_op jit(solution)/shard_map/ppermute | solution.py:14
  150.1 25.6 %collective-permute-start.22 = (bf16[2,128,512]{1,2,0:T(8,128)(2,1)S(1)}, bf16[2,128,512]{1,2,0:T(8,128)(2,1)S(1)}, u32[]{:S(2)}, u32[]{:S(2)}) collective-permute-start(bf16[2,128,512]{1,2,0:T(8,128)(2,1)S(1)} %copy.52), channel_id=1, source_target_pairs={{0,480},{2,482},{4,484},{6,486},{8,488},{10,490},{12,492},{14,494}... | collective-permute-start | bytes 786440 | tf_op jit(solution)/shard_map/ppermute | solution.py:14
  152.7 25.6 %collective-permute-start.23 = (bf16[2,128,512]{1,2,0:T(8,128)(2,1)S(1)}, bf16[2,128,512]{1,2,0:T(8,128)(2,1)S(1)}, u32[]{:S(2)}, u32[]{:S(2)}) collective-permute-start(bf16[2,128,512]{1,2,0:T(8,128)(2,1)S(1)} %copy.52), channel_id=1, source_target_pairs={{0,32},{2,34},{4,36},{6,38},{8,40},{10,42},{12,44},{14,46},{16,48}... | collective-permute-start | bytes 786440 | tf_op jit(solution)/shard_map/ppermute | solution.py:14
  158.0 21.0 %collective-permute-start.24 = (bf16[2,128,512]{1,2,0:T(8,128)(2,1)S(1)}, bf16[2,128,512]{1,2,0:T(8,128)(2,1)S(1)}, u32[]{:S(2)}, u32[]{:S(2)}) collective-permute-start(bf16[2,128,512]{1,2,0:T(8,128)(2,1)S(1)} %copy.52), channel_id=1, source_target_pairs={{0,448},{2,450},{4,452},{6,454},{8,456},{10,458},{12,460},{14,462}... | collective-permute-start | bytes 786440 | tf_op jit(solution)/shard_map/ppermute | solution.py:14
  160.7 19.4 %collective-permute-start.25 = (bf16[2,128,512]{1,2,0:T(8,128)(2,1)S(1)}, bf16[2,128,512]{1,2,0:T(8,128)(2,1)S(1)}, u32[]{:S(2)}, u32[]{:S(2)}) collective-permute-start(bf16[2,128,512]{1,2,0:T(8,128)(2,1)S(1)} %copy.52), channel_id=1, source_target_pairs={{0,64},{2,66},{4,68},{6,70},{8,72},{10,74},{12,76},{14,78},{16,80}... | collective-permute-start | bytes 786440 | tf_op jit(solution)/shard_map/ppermute | solution.py:14
  166.9 29.7 %collective-permute-start.26 = (bf16[2,128,512]{1,2,0:T(8,128)(2,1)S(1)}, bf16[2,128,512]{1,2,0:T(8,128)(2,1)S(1)}, u32[]{:S(2)}, u32[]{:S(2)}) collective-permute-start(bf16[2,128,512]{1,2,0:T(8,128)(2,1)S(1)} %copy.52), channel_id=1, source_target_pairs={{0,384},{2,386},{4,388},{6,390},{8,392},{10,394},{12,396},{14,398}... | collective-permute-start | bytes 786440 | tf_op jit(solution)/shard_map/ppermute | solution.py:14
  175.6 31.2 %collective-permute-start.27 = (bf16[2,128,512]{1,2,0:T(8,128)(2,1)S(1)}, bf16[2,128,512]{1,2,0:T(8,128)(2,1)}, u32[]{:S(2)}, u32[]{:S(2)}) collective-permute-start(bf16[2,128,512]{1,2,0:T(8,128)(2,1)S(1)} %copy.52), channel_id=1, source_target_pairs={{0,128},{2,130},{4,132},{6,134},{8,136},{10,138},{12,140},{14,142}... | collective-permute-start | bytes 786440 | tf_op jit(solution)/shard_map/ppermute | solution.py:14
  197.3 13.5 %copy-start = (bf16[15,1,128,512]{2,3,0,1:T(8,128)(2,1)S(1)}, bf16[15,1,128,512]{2,3,0,1:T(8,128)(2,1)}, u32[]{:S(2)}) copy-start(bf16[15,1,128,512]{2,3,0,1:T(8,128)(2,1)} %copy.34) | copy-start | bytes 5898244
  197.3 13.6 %copy-start.5 = (f32[15,128,128]{2,1,0:T(8,128)S(1)}, f32[15,128,128]{2,1,0:T(8,128)}, u32[]{:S(2)}) copy-start(f32[15,128,128]{2,1,0:T(8,128)} %copy-done.4) | copy-start | bytes 2949124
  210.8 1.9 copy-start.2
where the time goes:
time: 219 us; the launch traced here: 217 us
  starting transfers between devices  113 us (52%)
  waiting for transfers between devices  73 us (33%)
  local copies, waits for them, and re-layouts  18.3 us (8%)
  matrix products  9.63 us (4%)
  other arithmetic  3.24 us (1%)
    ppermute x28, starting transfers between devices, from_behind(): lax.ppermute(array, axis, [(i, (i + by) % size) for i in range(size)])  113 us
    ppermute x28, waiting for transfers between devices, from_behind(): lax.ppermute(array, axis, [(i, (i + by) % size) for i in range(size)])  73 us
    unnamed x42, local copies, waits for them, and re-layouts  11.2 us
    dot_general x4, matrix products, attend(): jnp.einsum('qok,olkd->lqd', weights, value_stack[:, :, :, window], prefer...  7.89 us
  transfers between devices with their start and end apart: 28, of which 13 were waited for; matrix products, arithmetic and copies ran while one was open for 9% of the time, Pallas kernels for 0%

commit v1 on v0

v1 whole, which is shorter than its diff:
```python
import functools
import math

import jax
import jax.numpy as jnp
from jax import lax
from jax.experimental import pallas as pl
from jax.experimental.pallas import tpu as pltpu
from jax.sharding import PartitionSpec as P

HD = 128
DEAD = -1e30
ZS, YS, XS, CS = 16, 2, 4, 2


def place(z, y, x, c):
    return (((z % ZS) * YS + y % YS) * XS + x % XS) * CS + c % CS


def send(block, target):
    pairs = []
    for z in range(ZS):
        for y in range(YS):
            for x in range(XS):
                for c in range(CS):
                    goal = target(z, y, x, c)
                    if goal is not None:
                        pairs.append((place(z, y, x, c), place(*goal)))
    return lax.ppermute(block, "ctx", pairs)


def part_kernel(count, first, last, q_ref, live_ref, *refs):
    blocks = refs[:count]
    rest = refs[count:]
    if not first:
        acc_in, max_in, sum_in = rest[:3]
        rest = rest[3:]
    if last:
        (out_ref,) = rest
    else:
        acc_out, max_out, sum_out = rest
    layers = blocks[0].shape[0] - 1
    rows = q_ref.shape[0]
    factor = math.log2(math.e) / math.sqrt(HD)
    for head in range(q_ref.shape[1] // HD):
        window = slice(head * HD, (head + 1) * HD)
        q = q_ref[:, window]
        scores = []
        for j in range(count):
            s = lax.dot_general(
                q, blocks[j][0, :, window], (((1,), (1,)), ((), ())),
                preferred_element_type=jnp.float32,
            ) * factor
            scores.append(jnp.where(live_ref[j] != 0, s, DEAD))
        top = functools.reduce(jnp.maximum, scores)
        largest = jnp.max(top, axis=1, keepdims=True)
        if not first:
            before = max_in[head, :, :1]
            largest = jnp.maximum(largest, before)
            shrink = jnp.exp2(before - largest)
        probs = [jnp.exp2(s - largest) for s in scores]
        total = jnp.sum(functools.reduce(jnp.add, probs), axis=1, keepdims=True)
        if not first:
            total = total + sum_in[head, :, :1] * shrink
        probs = [p.astype(jnp.bfloat16) for p in probs]
        for layer in range(layers):
            acc = functools.reduce(jnp.add, [
                jnp.dot(probs[j], blocks[j][1 + layer, :, window], preferred_element_type=jnp.float32)
                for j in range(count)
            ])
            if not first:
                acc = acc + acc_in[layer, :, window] * shrink
            if last:
                out_ref[layer, :, window] = (acc / total).astype(out_ref.dtype)
            else:
                acc_out[layer, :, window] = acc
        if not last:
            max_out[head] = jnp.broadcast_to(largest, (rows, HD))
            sum_out[head] = jnp.broadcast_to(total, (rows, HD))


def attend(queries, blocks, live, state=None, last=False):
    rows, width = queries.shape
    layers = blocks[0].shape[0] - 1
    heads = width // HD
    vmem = pl.BlockSpec(memory_space=pltpu.VMEM)
    smem = pl.BlockSpec(memory_space=pltpu.SMEM)
    if last:
        shapes = jax.ShapeDtypeStruct((layers, rows, width), jnp.bfloat16)
        out_specs = vmem
    else:
        shapes = (
            jax.ShapeDtypeStruct((layers, rows, width), jnp.float32),
            jax.ShapeDtypeStruct((heads, rows, HD), jnp.float32),
            jax.ShapeDtypeStruct((heads, rows, HD), jnp.float32),
        )
        out_specs = (vmem,) * 3
    state = () if state is None else tuple(state)
    count = len(blocks)
    work = 2 * rows * rows * width * count
    return pl.pallas_call(
        functools.partial(part_kernel, count, not state, last),
        out_shape=shapes,
        in_specs=[vmem, smem] + [vmem] * (count + len(state)),
        out_specs=out_specs,
        compiler_params=pltpu.CompilerParams(vmem_limit_bytes=32 * 1024 * 1024),
        cost_estimate=pl.CostEstimate(
            flops=work * (1 + layers),
            bytes_accessed=2 * rows * width * (1 + layers) * count,
            transcendentals=rows * rows * heads * count,
        ),
    )(queries, jnp.stack(live), *blocks, *state)


def body(queries, keys, values, tile_mask):
    here = lax.axis_index("ctx")
    c = here % CS
    x = here // CS % XS
    y = here // (CS * XS) % YS
    mask = tile_mask[0, :, 0, 0]

    def live(level, ahead):
        return jnp.where(ahead, mask[2 * level + 1], mask[2 * level + 2])

    own = jnp.concatenate([keys[None], values], axis=0)
    sign = lambda c: 1 if c else -1
    a1 = send(own, lambda z, y, x, c: (z + sign(c), y, x, c))
    yn = send(own, lambda z, y, x, c: (z, y + 1, x, c))
    x2n = send(own, lambda z, y, x, c: (z, y, x + 2, c))
    b1 = send(own, lambda z, y, x, c: (z - sign(c), y, x, c))
    cn = send(own, lambda z, y, x, c: (z, y, x, c + 1))
    a2 = send(a1, lambda z, y, x, c: (z + sign(c), y, x, c))
    b2 = send(b1, lambda z, y, x, c: (z - sign(c), y, x, c))
    yc = send(jnp.where((y == 0) == (c == 0), a1, b1), lambda z, y, x, c: (z, y + 1, x, c))
    a4 = send(a2, lambda z, y, x, c: (z + 2 * sign(c), y, x, c))
    b4 = send(b2, lambda z, y, x, c: (z - 2 * sign(c), y, x, c))
    above = jnp.where(y == 0, yn, yc)
    below = jnp.where(y == 0, yc, yn)
    x1u = send(jnp.where(x == XS - 1, below, own), lambda z, y, x, c: (z, y, x + 1, c))
    x1d = send(jnp.where(x == 0, above, own), lambda z, y, x, c: (z, y, x - 1, c))
    x2c = send(jnp.where(x < 2, above, below), lambda z, y, x, c: (z, y, x + 2, c))
    cc = send(jnp.where(c == 0, x1d, x1u), lambda z, y, x, c: (z, y, x, c + 1))

    up = c == 0
    state = attend(
        queries,
        [own, cn, yn, x2n, a1, b1, a2, b2, yc],
        [jnp.ones((), jnp.int32), live(0, up), live(3, y == 0), live(2, x < 2),
         live(4, up), live(4, ~up), live(5, up), live(5, ~up), live(3, y != 0)],
    )
    return attend(
        queries,
        [x1u, x1d, x2c, cc, a4, b4],
        [mask[4], mask[3], live(2, x >= 2), live(0, ~up), live(6, up), live(6, ~up)],
        state,
        last=True,
    )


def solution(mesh):
    in_specs = (P("ctx", "mp"), P("ctx", "mp"), P(None, "ctx", "mp"), P("ctx", None, None, None))
    out_specs = P(None, "ctx", "mp")
    return jax.shard_map(body, mesh=mesh, in_specs=in_specs, out_specs=out_specs, check_vma=False)
```

time: 219 us -> 123 us (0.56)
  the two profiles are of different devices: /device:TPU:127 before, /device:TPU:1 now
where the time goes in v1:
time: 123 us; the launch traced here: 122 us
  starting transfers between devices  75.5 us (61%)
  between operations  15.6 us (13%)
  waiting for transfers between devices  12.8 us (10%)
  Pallas kernels  9.25 us (8%)
  local copies, waits for them, and re-layouts  4.95 us (4%)
  other arithmetic  3.76 us (3%)
    ppermute x14, starting transfers between devices, send(): return lax.ppermute(block, 'ctx', pairs)  75.5 us
    ppermute x14, waiting for transfers between devices, send(): return lax.ppermute(block, 'ctx', pairs)  12.8 us
    pallas_call x2, Pallas kernels, attend(): pl.pallas_call(functools.partial(part_kernel, count, not state, last), ou...  9.25 us
    unnamed x16, local copies, waits for them, and re-layouts  2.9 us
  transfers between devices with their start and end apart: 14, of which 3 were waited for; matrix products, arithmetic and copies ran while one was open for 4% of the time, Pallas kernels for 4%

profile of v1, /device:TPU:1, one launch (start us, length us, event | category | flops | bytes accessed | tf_op | source)
XLA Modules:
  0.0 121.8 jit_solution(12216705466368651217)
XLA Ops:
  0.0 1.1 pad_maximum_fusion.refs_0_
  1.1 4.4 %collective-permute-start = (bf16[4,128,512]{2,1,0:T(8,128)(2,1)S(1)}, bf16[4,128,512]{2,1,0:T(8,128)(2,1)S(1)}, u32[]{:S(2)}, u32[]{:S(2)}) collective-permute-start(bf16[4,128,512]{2,1,0:T(8,128)(2,1)S(1)} %pad_maximum_fusion.refs_0_), channel_id=1, source_target_pairs={{0,480},{2,34},{4,484},{6,38},{8,488},{10,42},{12,492},{14,46},{16... | collective-permute-start | bytes 1572872 | tf_op jit(solution)/shard_map/ppermute | solution.py:29
  5.5 9.5 %collective-permute-start.1 = (bf16[4,128,512]{2,1,0:T(8,128)(2,1)S(1)}, bf16[4,128,512]{2,1,0:T(8,128)(2,1)S(1)}, u32[]{:S(2)}, u32[]{:S(2)}) collective-permute-start(bf16[4,128,512]{2,1,0:T(8,128)(2,1)S(1)} %pad_maximum_fusion.refs_0_), channel_id=1, source_target_pairs={{0,32},{2,482},{4,36},{6,486},{8,40},{10,490},{12,44},{14,494},{16... | collective-permute-start | bytes 1572872 | tf_op jit(solution)/shard_map/ppermute | solution.py:29
  15.0 3.2 %collective-permute-start.3 = (bf16[4,128,512]{2,1,0:T(8,128)(2,1)S(1)}, bf16[4,128,512]{2,1,0:T(8,128)(2,1)S(1)}, u32[]{:S(2)}, u32[]{:S(2)}) collective-permute-start(bf16[4,128,512]{2,1,0:T(8,128)(2,1)S(1)} %pad_maximum_fusion.refs_0_), channel_id=1, source_target_pairs={{0,16},{2,18},{4,20},{6,22},{8,24},{10,26},{12,28},{14,30},{16,0},... | collective-permute-start | bytes 1572872 | tf_op jit(solution)/shard_map/ppermute | solution.py:29
  18.2 0.0 copy-start.5
  18.2 0.0 copy-start.6
  18.2 1.3 %collective-permute-done.refs_4_ = bf16[4,128,512]{2,1,0:T(8,128)(2,1)S(1)} collective-permute-done((bf16[4,128,512]{2,1,0:T(8,128)(2,1)S(1)}, bf16[4,128,512]{2,1,0:T(8,128)(2,1)S(1)}, u32[]{:S(2)}, u32[]{:S(2)}) %collective-permute-start) | collective-permute-done | bytes 524320 | tf_op jit(solution)/shard_map/ppermute | solution.py:29
  19.6 6.3 %collective-permute-done.1.refs_5_ = bf16[4,128,512]{2,1,0:T(8,128)(2,1)S(1)} collective-permute-done((bf16[4,128,512]{2,1,0:T(8,128)(2,1)S(1)}, bf16[4,128,512]{2,1,0:T(8,128)(2,1)S(1)}, u32[]{:S(2)}, u32[]{:S(2)}) %collective-permute-start.1) | collective-permute-done | bytes 524320 | tf_op jit(solution)/shard_map/ppermute | solution.py:29
  25.9 0.8 broadcast_select_fusion.3
  26.7 3.2 %collective-permute-start.2 = (bf16[4,128,512]{2,1,0:T(8,128)(2,1)}, bf16[4,128,512]{2,1,0:T(8,128)(2,1)S(1)}, u32[]{:S(2)}, u32[]{:S(2)}) collective-permute-start(bf16[4,128,512]{2,1,0:T(8,128)(2,1)} %broadcast_select_fusion.3), channel_id=1, source_target_pairs={{0,16},{2,18},{4,20},{6,22},{8,24},{10,26},{12,28},{14,30},{16,0},... | collective-permute-start | bytes 1572872 | tf_op jit(solution)/shard_map/ppermute | solution.py:29
  30.0 5.0 %collective-permute-start.10 = (bf16[4,128,512]{2,1,0:T(8,128)(2,1)S(1)}, bf16[4,128,512]{2,1,0:T(8,128)(2,1)}, u32[]{:S(2)}, u32[]{:S(2)}) collective-permute-start(bf16[4,128,512]{2,1,0:T(8,128)(2,1)S(1)} %collective-permute-done.1.refs_5_), channel_id=1, source_target_pairs={{0,32},{2,482},{4,36},{6,486},{8,40},{10,490},{12,44},{14,494},{16... | collective-permute-start | bytes 1572872 | tf_op jit(solution)/shard_map/ppermute | solution.py:29
  35.0 1.9 %collective-permute-start.8 = (bf16[4,128,512]{2,1,0:T(8,128)(2,1)S(1)}, bf16[4,128,512]{2,1,0:T(8,128)(2,1)}, u32[]{:S(2)}, u32[]{:S(2)}) collective-permute-start(bf16[4,128,512]{2,1,0:T(8,128)(2,1)S(1)} %collective-permute-done.refs_4_), channel_id=1, source_target_pairs={{0,480},{2,34},{4,484},{6,38},{8,488},{10,42},{12,492},{14,46},{16... | collective-permute-start | bytes 1572872 | tf_op jit(solution)/shard_map/ppermute | solution.py:29
  36.9 0.0 collective-permute-done.3.refs_2_
  36.9 5.1 %collective-permute-done.2.refs_8_ = bf16[4,128,512]{2,1,0:T(8,128)(2,1)S(1)} collective-permute-done((bf16[4,128,512]{2,1,0:T(8,128)(2,1)}, bf16[4,128,512]{2,1,0:T(8,128)(2,1)S(1)}, u32[]{:S(2)}, u32[]{:S(2)}) %collective-permute-start.2) | collective-permute-done | bytes 524320 | tf_op jit(solution)/shard_map/ppermute | solution.py:29
  42.1 0.0 copy-done.5
  42.1 0.0 copy-done.6
  42.1 0.0 copy-start
  42.1 1.0 broadcast_select_fusion.2
  43.1 0.0 copy-done
  43.1 3.1 %collective-permute-start.4 = (bf16[4,128,512]{2,1,0:T(8,128)(2,1)S(1)}, bf16[4,128,512]{2,1,0:T(8,128)(2,1)S(1)}, u32[]{:S(2)}, u32[]{:S(2)}) collective-permute-start(bf16[4,128,512]{2,1,0:T(8,128)(2,1)S(1)} %get-tuple-element.12), channel_id=1, source_target_pairs={{0,4},{2,6},{4,8},{6,10},{8,12},{10,14},{12,0},{14,2},{16,20},{18,... | collective-permute-start | bytes 1572872 | tf_op jit(solution)/shard_map/ppermute | solution.py:29
  46.2 3.4 %collective-permute-start.5 = (bf16[4,128,512]{2,1,0:T(8,128)(2,1)S(1)}, bf16[4,128,512]{2,1,0:T(8,128)(2,1)S(1)}, u32[]{:S(2)}, u32[]{:S(2)}) collective-permute-start(bf16[4,128,512]{2,1,0:T(8,128)(2,1)S(1)} %get-tuple-element.11), channel_id=1, source_target_pairs={{0,12},{2,14},{4,0},{6,2},{8,4},{10,6},{12,8},{14,10},{16,28},{18,... | collective-permute-start | bytes 1572872 | tf_op jit(solution)/shard_map/ppermute | solution.py:29
  49.6 3.6 %collective-permute-start.12 = (bf16[4,128,512]{2,1,0:T(8,128)(2,1)S(1)}, bf16[4,128,512]{2,1,0:T(8,128)(2,1)S(1)}, u32[]{:S(2)}, u32[]{:S(2)}) collective-permute-start(bf16[4,128,512]{2,1,0:T(8,128)(2,1)S(1)} %pad_maximum_fusion.refs_0_), channel_id=1, source_target_pairs={{0,2},{2,0},{4,6},{6,4},{8,10},{10,8},{12,14},{14,12},{16,18},{18,... | collective-permute-start | bytes 1572872 | tf_op jit(solution)/shard_map/ppermute | solution.py:29
  53.1 0.0 collective-permute-done.10.refs_7_
  53.2 3.4 %collective-permute-start.13 = (bf16[4,128,512]{2,1,0:T(8,128)(2,1)S(1)}, bf16[4,128,512]{2,1,0:T(8,128)(2,1)}, u32[]{:S(2)}, u32[]{:S(2)}) collective-permute-start(bf16[4,128,512]{2,1,0:T(8,128)(2,1)S(1)} %pad_maximum_fusion.refs_0_), channel_id=1, source_target_pairs={{0,8},{2,10},{4,12},{6,14},{8,0},{10,2},{12,4},{14,6},{16,24},{18,... | collective-permute-start | bytes 1572872 | tf_op jit(solution)/shard_map/ppermute | solution.py:29
  56.6 0.0 collective-permute-done.8.refs_6_
  56.6 3.3 %collective-permute-start.6 = (bf16[4,128,512]{2,1,0:T(8,128)(2,1)}, bf16[4,128,512]{2,1,0:T(8,128)(2,1)}, u32[]{:S(2)}, u32[]{:S(2)}) collective-permute-start(bf16[4,128,512]{2,1,0:T(8,128)(2,1)} %get-tuple-element.13), channel_id=1, source_target_pairs={{0,8},{2,10},{4,12},{6,14},{8,0},{10,2},{12,4},{14,6},{16,24},{18,... | collective-permute-start | bytes 1572872 | tf_op jit(solution)/shard_map/ppermute | solution.py:29
  60.0 0.0 collective-permute-done.4.refs_0_
  60.0 4.8 %collective-permute-start.11 = (bf16[4,128,512]{2,1,0:T(8,128)(2,1)}, bf16[4,128,512]{2,1,0:T(8,128)(2,1)}, u32[]{:S(2)}, u32[]{:S(2)}) collective-permute-start(bf16[4,128,512]{2,1,0:T(8,128)(2,1)} %collective-permute-done.10.refs_7_), channel_id=1, source_target_pairs={{0,64},{2,450},{4,68},{6,454},{8,72},{10,458},{12,76},{14,462},{16... | collective-permute-start | bytes 1572872 | tf_op jit(solution)/shard_map/ppermute | solution.py:29
  64.8 0.0 collective-permute-done.5.refs_1_
  64.8 1.9 %collective-permute-start.9 = (bf16[4,128,512]{2,1,0:T(8,128)(2,1)}, bf16[4,128,512]{2,1,0:T(8,128)(2,1)}, u32[]{:S(2)}, u32[]{:S(2)}) collective-permute-start(bf16[4,128,512]{2,1,0:T(8,128)(2,1)} %collective-permute-done.8.refs_6_), channel_id=1, source_target_pairs={{0,448},{2,66},{4,452},{6,70},{8,456},{10,74},{12,460},{14,78},{16... | collective-permute-start | bytes 1572872 | tf_op jit(solution)/shard_map/ppermute | solution.py:29
  66.7 0.0 copy-start.4
  66.8 0.8 broadcast_select_fusion
  67.6 0.0 copy-start.7
  67.6 0.0 collective-permute-done.12.refs_1_
  67.6 0.0 copy-start.2
  67.6 0.8 copy-done.2
  68.4 24.7 %collective-permute-start.7 = (bf16[4,128,512]{2,1,0:T(8,128)(2,1)}, bf16[4,128,512]{2,1,0:T(8,128)(2,1)}, u32[]{:S(2)}, u32[]{:S(2)}) collective-permute-start(bf16[4,128,512]{2,1,0:T(8,128)(2,1)} %broadcast_select_fusion), channel_id=1, source_target_pairs={{0,2},{2,0},{4,6},{6,4},{8,10},{10,8},{12,14},{14,12},{16,18},{18,... | collective-permute-start | bytes 1572872 | tf_op jit(solution)/shard_map/ppermute | solution.py:29
  93.1 0.0 copy-done.7
  93.1 0.7 fusion
  109.1 1.3 %stack.46.live_ref = s32[6]{0:T(128)S(1)} concatenate(s32[1]{0:T(128)} %bitcast, s32[1]{0:T(128)} %bitcast.1, s32[1]{0:T(128)} %bitcast.4, s32[1]{0:T(128)} %bitcast.7, s32[1]{0:T(128)} %bitcast.10, s32[1]{0:T(128)} %bitcast.11), dimensions={0} | concatenate | bytes 48 | tf_op jit(solution)/shard_map/stack | solution.py:112
  110.4 0.1 stack.55.live_ref
  110.4 0.0 collective-permute-done.13.refs_3_
  110.4 0.0 copy-done.4
  110.5 0.0 copy-start.1
  110.5 1.0 copy-done.1
  111.5 0.0 copy-start.3
  111.5 1.0 copy-done.3
  112.5 4.3 %shard_map.46 = (f32[3,128,512]{2,1,0:T(8,128)S(1)}, f32[4,128,128]{2,1,0:T(8,128)S(1)}, f32[4,128,128]{2,1,0:T(8,128)S(1)}) custom-call(bf16[128,512]{1,0:T(8,128)(2,1)S(1)} %copy-done.4, s32[9]{0:T(128)S(1)} %stack.55.live_ref, bf16[4,128,512]{2,1,0:T(8,128)(2,1)S(1)} %pad_maximum_fusion.refs_0_, bf16[4,128,512]{2,1,0:T(8,128)(2,1)S(1)} %copy-done.3, ...), custom_call_target="tpu_custom_call" | custom-call | flops 603979776 | bytes 4718592 | tf_op jit(solution)/shard_map/pallas_call | solution.py:101
  116.9 0.0 collective-permute-done.6.refs_2_
  116.9 0.0 collective-permute-done.11.refs_5_
  116.9 0.0 collective-permute-done.9.refs_4_
  116.9 0.0 collective-permute-done.7.refs_3_
  116.9 4.9 %shard_map.47 = bf16[3,128,512]{2,1,0:T(8,128)(2,1)} custom-call(bf16[128,512]{1,0:T(8,128)(2,1)S(1)} %copy-done.4, s32[6]{0:T(128)S(1)} %stack.46.live_ref, bf16[4,128,512]{2,1,0:T(8,128)(2,1)S(1)} %collective-permute-done.4.refs_0_, bf16[4,128,512]{2,1,0:T(8,128)(2,1)S(1)} %collective-permute-done.5.refs_1_, ...), custom_call_target="tpu_custom_call" | custom-call | flops 402653184 | bytes 3145728 | tf_op jit(solution)/shard_map/pallas_call | solution.py:101
Async XLA Ops:
  1.1 18.5 %collective-permute-start = (bf16[4,128,512]{2,1,0:T(8,128)(2,1)S(1)}, bf16[4,128,512]{2,1,0:T(8,128)(2,1)S(1)}, u32[]{:S(2)}, u32[]{:S(2)}) collective-permute-start(bf16[4,128,512]{2,1,0:T(8,128)(2,1)S(1)} %pad_maximum_fusion.refs_0_), channel_id=1, source_target_pairs={{0,480},{2,34},{4,484},{6,38},{8,488},{10,42},{12,492},{14,46},{16... | collective-permute-start | bytes 1572872 | tf_op jit(solution)/shard_map/ppermute | solution.py:29
  5.5 20.4 %collective-permute-start.1 = (bf16[4,128,512]{2,1,0:T(8,128)(2,1)S(1)}, bf16[4,128,512]{2,1,0:T(8,128)(2,1)S(1)}, u32[]{:S(2)}, u32[]{:S(2)}) collective-permute-start(bf16[4,128,512]{2,1,0:T(8,128)(2,1)S(1)} %pad_maximum_fusion.refs_0_), channel_id=1, source_target_pairs={{0,32},{2,482},{4,36},{6,486},{8,40},{10,490},{12,44},{14,494},{16... | collective-permute-start | bytes 1572872 | tf_op jit(solution)/shard_map/ppermute | solution.py:29
  15.0 22.0 %collective-permute-start.3 = (bf16[4,128,512]{2,1,0:T(8,128)(2,1)S(1)}, bf16[4,128,512]{2,1,0:T(8,128)(2,1)S(1)}, u32[]{:S(2)}, u32[]{:S(2)}) collective-permute-start(bf16[4,128,512]{2,1,0:T(8,128)(2,1)S(1)} %pad_maximum_fusion.refs_0_), channel_id=1, source_target_pairs={{0,16},{2,18},{4,20},{6,22},{8,24},{10,26},{12,28},{14,30},{16,0},... | collective-permute-start | bytes 1572872 | tf_op jit(solution)/shard_map/ppermute | solution.py:29
  18.2 23.8 %copy-start.5 = (bf16[3,128,512]{2,1,0:T(8,128)(2,1)S(1)}, bf16[3,128,512]{2,1,0:T(8,128)(2,1)}, u32[]{:S(2)}) copy-start(bf16[3,128,512]{2,1,0:T(8,128)(2,1)} %param.6) | copy-start | bytes 1179652
  18.2 23.8 %copy-start.6 = (bf16[128,512]{1,0:T(8,128)(2,1)S(1)}, bf16[128,512]{1,0:T(8,128)(2,1)}, u32[]{:S(2)}) copy-start(bf16[128,512]{1,0:T(8,128)(2,1)} %param.5) | copy-start | bytes 393220
  26.7 15.3 %collective-permute-start.2 = (bf16[4,128,512]{2,1,0:T(8,128)(2,1)}, bf16[4,128,512]{2,1,0:T(8,128)(2,1)S(1)}, u32[]{:S(2)}, u32[]{:S(2)}) collective-permute-start(bf16[4,128,512]{2,1,0:T(8,128)(2,1)} %broadcast_select_fusion.3), channel_id=1, source_target_pairs={{0,16},{2,18},{4,20},{6,22},{8,24},{10,26},{12,28},{14,30},{16,0},... | collective-permute-start | bytes 1572872 | tf_op jit(solution)/shard_map/ppermute | solution.py:29
  30.0 23.2 %collective-permute-start.10 = (bf16[4,128,512]{2,1,0:T(8,128)(2,1)S(1)}, bf16[4,128,512]{2,1,0:T(8,128)(2,1)}, u32[]{:S(2)}, u32[]{:S(2)}) collective-permute-start(bf16[4,128,512]{2,1,0:T(8,128)(2,1)S(1)} %collective-permute-done.1.refs_5_), channel_id=1, source_target_pairs={{0,32},{2,482},{4,36},{6,486},{8,40},{10,490},{12,44},{14,494},{16... | collective-permute-start | bytes 1572872 | tf_op jit(solution)/shard_map/ppermute | solution.py:29
  35.0 21.6 %collective-permute-start.8 = (bf16[4,128,512]{2,1,0:T(8,128)(2,1)S(1)}, bf16[4,128,512]{2,1,0:T(8,128)(2,1)}, u32[]{:S(2)}, u32[]{:S(2)}) collective-permute-start(bf16[4,128,512]{2,1,0:T(8,128)(2,1)S(1)} %collective-permute-done.refs_4_), channel_id=1, source_target_pairs={{0,480},{2,34},{4,484},{6,38},{8,488},{10,42},{12,492},{14,46},{16... | collective-permute-start | bytes 1572872 | tf_op jit(solution)/shard_map/ppermute | solution.py:29
  42.1 1.0 copy-start
  43.1 16.9 %collective-permute-start.4 = (bf16[4,128,512]{2,1,0:T(8,128)(2,1)S(1)}, bf16[4,128,512]{2,1,0:T(8,128)(2,1)S(1)}, u32[]{:S(2)}, u32[]{:S(2)}) collective-permute-start(bf16[4,128,512]{2,1,0:T(8,128)(2,1)S(1)} %get-tuple-element.12), channel_id=1, source_target_pairs={{0,4},{2,6},{4,8},{6,10},{8,12},{10,14},{12,0},{14,2},{16,20},{18,... | collective-permute-start | bytes 1572872 | tf_op jit(solution)/shard_map/ppermute | solution.py:29
  46.2 18.6 %collective-permute-start.5 = (bf16[4,128,512]{2,1,0:T(8,128)(2,1)S(1)}, bf16[4,128,512]{2,1,0:T(8,128)(2,1)S(1)}, u32[]{:S(2)}, u32[]{:S(2)}) collective-permute-start(bf16[4,128,512]{2,1,0:T(8,128)(2,1)S(1)} %get-tuple-element.11), channel_id=1, source_target_pairs={{0,12},{2,14},{4,0},{6,2},{8,4},{10,6},{12,8},{14,10},{16,28},{18,... | collective-permute-start | bytes 1572872 | tf_op jit(solution)/shard_map/ppermute | solution.py:29
  49.6 18.0 %collective-permute-start.12 = (bf16[4,128,512]{2,1,0:T(8,128)(2,1)S(1)}, bf16[4,128,512]{2,1,0:T(8,128)(2,1)S(1)}, u32[]{:S(2)}, u32[]{:S(2)}) collective-permute-start(bf16[4,128,512]{2,1,0:T(8,128)(2,1)S(1)} %pad_maximum_fusion.refs_0_), channel_id=1, source_target_pairs={{0,2},{2,0},{4,6},{6,4},{8,10},{10,8},{12,14},{14,12},{16,18},{18,... | collective-permute-start | bytes 1572872 | tf_op jit(solution)/shard_map/ppermute | solution.py:29
  53.2 57.3 %collective-permute-start.13 = (bf16[4,128,512]{2,1,0:T(8,128)(2,1)S(1)}, bf16[4,128,512]{2,1,0:T(8,128)(2,1)}, u32[]{:S(2)}, u32[]{:S(2)}) collective-permute-start(bf16[4,128,512]{2,1,0:T(8,128)(2,1)S(1)} %pad_maximum_fusion.refs_0_), channel_id=1, source_target_pairs={{0,8},{2,10},{4,12},{6,14},{8,0},{10,2},{12,4},{14,6},{16,24},{18,... | collective-permute-start | bytes 1572872 | tf_op jit(solution)/shard_map/ppermute | solution.py:29
  56.6 60.3 %collective-permute-start.6 = (bf16[4,128,512]{2,1,0:T(8,128)(2,1)}, bf16[4,128,512]{2,1,0:T(8,128)(2,1)}, u32[]{:S(2)}, u32[]{:S(2)}) collective-permute-start(bf16[4,128,512]{2,1,0:T(8,128)(2,1)} %get-tuple-element.13), channel_id=1, source_target_pairs={{0,8},{2,10},{4,12},{6,14},{8,0},{10,2},{12,4},{14,6},{16,24},{18,... | collective-permute-start | bytes 1572872 | tf_op jit(solution)/shard_map/ppermute | solution.py:29
  60.0 56.9 %collective-permute-start.11 = (bf16[4,128,512]{2,1,0:T(8,128)(2,1)}, bf16[4,128,512]{2,1,0:T(8,128)(2,1)}, u32[]{:S(2)}, u32[]{:S(2)}) collective-permute-start(bf16[4,128,512]{2,1,0:T(8,128)(2,1)} %collective-permute-done.10.refs_7_), channel_id=1, source_target_pairs={{0,64},{2,450},{4,68},{6,454},{8,72},{10,458},{12,76},{14,462},{16... | collective-permute-start | bytes 1572872 | tf_op jit(solution)/shard_map/ppermute | solution.py:29
  64.8 52.1 %collective-permute-start.9 = (bf16[4,128,512]{2,1,0:T(8,128)(2,1)}, bf16[4,128,512]{2,1,0:T(8,128)(2,1)}, u32[]{:S(2)}, u32[]{:S(2)}) collective-permute-start(bf16[4,128,512]{2,1,0:T(8,128)(2,1)} %collective-permute-done.8.refs_6_), channel_id=1, source_target_pairs={{0,448},{2,66},{4,452},{6,70},{8,456},{10,74},{12,460},{14,78},{16... | collective-permute-start | bytes 1572872 | tf_op jit(solution)/shard_map/ppermute | solution.py:29
  66.7 43.7 %copy-start.4 = (bf16[128,512]{1,0:T(8,128)(2,1)S(1)}, bf16[128,512]{1,0:T(8,128)(2,1)}, u32[]{:S(2)}) copy-start(bf16[128,512]{1,0:T(8,128)(2,1)} %q_ref.3) | copy-start | bytes 393220
  67.6 25.5 %copy-start.7 = (s32[1,15,1,1]{1,3,2,0:T(1,128)S(1)}, s32[1,15,1,1]{1,3,2,0:T(1,128)}, u32[]{:S(2)}) copy-start(s32[1,15,1,1]{1,3,2,0:T(1,128)} %param.7) | copy-start | bytes 184
  67.6 0.8 copy-start.2
  68.4 48.5 %collective-permute-start.7 = (bf16[4,128,512]{2,1,0:T(8,128)(2,1)}, bf16[4,128,512]{2,1,0:T(8,128)(2,1)}, u32[]{:S(2)}, u32[]{:S(2)}) collective-permute-start(bf16[4,128,512]{2,1,0:T(8,128)(2,1)} %broadcast_select_fusion), channel_id=1, source_target_pairs={{0,2},{2,0},{4,6},{6,4},{8,10},{10,8},{12,14},{14,12},{16,18},{18,... | collective-permute-start | bytes 1572872 | tf_op jit(solution)/shard_map/ppermute | solution.py:29
  110.5 1.0 copy-start.1
  111.5 1.0 copy-start.3

commit v2 on v1

v2 whole, which is shorter than its diff:
```python
import functools
import math

import jax
import jax.numpy as jnp
from jax import lax
from jax.experimental import pallas as pl
from jax.experimental.pallas import tpu as pltpu
from jax.sharding import PartitionSpec as P

HD = 128
DEAD = -1e30
MIB = 1024 * 1024
SPREAD = 1_000_000
GATE1, GATE2 = 20.0, 3.0
FIRST, LAST = 1, 1
ZS, YS, XS, CS = 16, 2, 4, 2


def place(z, y, x, c):
    return (((z % ZS) * YS + y % YS) * XS + x % XS) * CS + c % CS


def coordinates():
    here = lax.axis_index("ctx")
    return (here >> 3) & 1, (here >> 1) & 3, here & 1


ROWS = [
    [place(z, y, x, c) for x in range(XS)] for z in range(ZS) for y in range(YS) for c in range(CS)
]


def send(block, target):
    pairs = []
    for z in range(ZS):
        for y in range(YS):
            for x in range(XS):
                for c in range(CS):
                    goal = target(z, y, x, c)
                    if goal is not None:
                        pairs.append((place(z, y, x, c), place(*goal)))
    return lax.ppermute(block, "ctx", pairs)


def after(block, *others):
    return lax.optimization_barrier((block, *others))[0]


def attend_head(q_ref, blocks, biases, window, before=None):
    rows = q_ref.shape[0]
    layers = blocks[0].shape[0] - 1
    keys = jnp.concatenate([b[0, :, window] for b in blocks], axis=0)
    scores = lax.dot_general(
        q_ref[:, window], keys, (((1,), (1,)), ((), ())), preferred_element_type=jnp.float32
    ) * (math.log2(math.e) / math.sqrt(HD))
    parts = [
        scores[:, j * rows:(j + 1) * rows] + biases[j][...] for j in range(len(blocks))
    ]
    largest = jnp.max(functools.reduce(jnp.maximum, parts), axis=1, keepdims=True)
    if before is not None:
        largest = jnp.maximum(largest, before)
    probs = [jnp.exp2(s - largest) for s in parts]
    total = jnp.sum(functools.reduce(jnp.add, probs), axis=1, keepdims=True)
    weights = jnp.concatenate([p.astype(jnp.bfloat16) for p in probs], axis=1)
    values = jnp.concatenate(
        [jnp.concatenate([b[1 + layer, :, window] for layer in range(layers)], axis=1) for b in blocks],
        axis=0,
    )
    return largest, total, jnp.dot(weights, values, preferred_element_type=jnp.float32)


def first_kernel(stacked, rules, later, q_ref, mask_ref, *refs):
    blocks = []
    for ref, depth in zip(refs, stacked):
        blocks += [ref] if depth is None else [ref.at[j] for j in range(depth)]
    acc_ref, max_ref, sum_ref, later_ref, now_ref = refs[-5:]
    where = coordinates()
    row = (1, HD)
    for j, rule in enumerate(later):
        later_ref[j:j + 1] = jnp.where(rule(mask_ref, *where), jnp.zeros(row, jnp.float32), DEAD)
    for j, rule in enumerate(rules):
        now_ref[j:j + 1] = jnp.where(rule(mask_ref, *where), jnp.zeros(row, jnp.float32), DEAD)
    biases = [now_ref.at[j:j + 1] for j in range(len(rules))]
    for head in range(q_ref.shape[1] // HD):
        window = slice(head * HD, (head + 1) * HD)
        largest, total, acc = attend_head(q_ref, blocks, biases, window)
        max_ref[head] = jnp.broadcast_to(largest, max_ref.shape[1:])
        sum_ref[head] = jnp.broadcast_to(total, sum_ref.shape[1:])
        acc_ref[head] = acc


def last_kernel(count, q_ref, *refs):
    blocks = refs[:count]
    acc_ref, max_ref, sum_ref, bias_ref = refs[count:count + 4]
    out_ref = refs[-1]
    biases = [bias_ref.at[j:j + 1] for j in range(count)]
    for head in range(q_ref.shape[1] // HD):
        window = slice(head * HD, (head + 1) * HD)
        before = max_ref[head]
        largest, total, acc = attend_head(q_ref, blocks, biases, window, before)
        shrink = jnp.exp2(before - largest)
        inverse = 1.0 / (total + sum_ref[head] * shrink)
        for layer in range(out_ref.shape[0]):
            part = slice(layer * HD, (layer + 1) * HD)
            share = acc[:, part] + acc_ref[head, :, part] * shrink
            out_ref[layer, :, window] = (share * inverse).astype(out_ref.dtype)


def attend(queries, blocks, mask=None, later=None, state=(), tokens=()):
    rows, width = queries.shape
    heads = width // HD
    vmem = pl.BlockSpec(memory_space=pltpu.VMEM)
    operands = [queries]
    in_specs = [vmem]
    scratch = []
    if state:
        count = len(blocks)
        layers = blocks[0].shape[0] - 1
        kernel = functools.partial(last_kernel, count)
        shapes = jax.ShapeDtypeStruct((layers, rows, width), jnp.bfloat16)
        out_specs = vmem
    else:
        stacked = [block.shape[0] if rule is None else None for block, rule in blocks]
        rules = []
        for block, rule in blocks:
            rules += [beside(j) for j in range(block.shape[0])] if rule is None else [rule]
        blocks = [block for block, _ in blocks]
        count = len(rules)
        layers = blocks[0].shape[-3] - 1
        kernel = functools.partial(first_kernel, stacked, rules, later)
        operands.append(mask)
        in_specs.append(pl.BlockSpec(memory_space=pltpu.SMEM))
        shapes = (
            jax.ShapeDtypeStruct((heads, rows, layers * HD), jnp.float32),
            jax.ShapeDtypeStruct((heads, rows, HD), jnp.float32),
            jax.ShapeDtypeStruct((heads, rows, HD), jnp.float32),
            jax.ShapeDtypeStruct((8, HD), jnp.float32),
        )
        out_specs = (vmem,) * len(shapes)
        scratch = [pltpu.VMEM((16, HD), jnp.float32)]
    operands += [*blocks, *state, *tokens]
    in_specs += [vmem] * (len(blocks) + len(state) + len(tokens))
    return pl.pallas_call(
        kernel,
        out_shape=shapes,
        in_specs=in_specs,
        out_specs=out_specs,
        scratch_shapes=scratch,
        compiler_params=pltpu.CompilerParams(vmem_limit_bytes=8 * MIB),
        cost_estimate=pl.CostEstimate(
            flops=2 * rows * rows * width * count * (1 + layers) * (LAST if state else FIRST),
            bytes_accessed=2 * rows * width * (1 + layers) * count,
            transcendentals=rows * rows * heads * count,
        ),
    )(*operands)


def offset(level, ahead, there=None):
    def rule(mask_ref, y, x, c):
        up = ahead(y, x, c)
        alive = mask_ref[jnp.where(up, 2 * level + 1, 2 * level + 2)] != 0
        return alive if there is None else alive & there(y, x, c)

    return rule


def gate_kernel(*refs):
    refs[-1][...] = jnp.zeros_like(refs[-1])


def gate(weight, *arrays):
    vmem = pl.BlockSpec(memory_space=pltpu.VMEM)
    return pl.pallas_call(
        gate_kernel,
        out_shape=jax.ShapeDtypeStruct((8, 128), jnp.float32),
        in_specs=[pl.BlockSpec(memory_space=pl.ANY)] * len(arrays),
        out_specs=vmem,
        compiler_params=pltpu.CompilerParams(vmem_limit_bytes=1 * MIB),
        cost_estimate=pl.CostEstimate(flops=int(weight * 1e9), bytes_accessed=4096, transcendentals=0),
    )(*arrays)


def spread_kernel(own_ref, copies_ref, own_out_ref, sems):
    moves = [
        pltpu.make_async_copy(own_ref, goal, sems.at[j])
        for j, goal in enumerate([copies_ref.at[j] for j in range(XS)] + [own_out_ref])
    ]
    for move in moves:
        move.start()
    for move in moves:
        move.wait()


def spread(own):
    vmem = pl.BlockSpec(memory_space=pltpu.VMEM)
    anywhere = pl.BlockSpec(memory_space=pltpu.HBM)
    return pl.pallas_call(
        spread_kernel,
        out_shape=(
            jax.ShapeDtypeStruct((XS,) + own.shape, own.dtype),
            jax.ShapeDtypeStruct(own.shape, own.dtype),
        ),
        in_specs=[vmem],
        out_specs=(anywhere, anywhere),
        scratch_shapes=[pltpu.SemaphoreType.DMA((XS + 1,))],
        compiler_params=pltpu.CompilerParams(vmem_limit_bytes=3 * MIB),
        cost_estimate=pl.CostEstimate(flops=SPREAD, bytes_accessed=own.size, transcendentals=0),
    )(own)


def beside(j):
    def rule(mask_ref, y, x, c):
        ahead = j - x
        alive = mask_ref[jnp.where(ahead > 0, 1, 2) + 2 * jnp.abs(ahead)] != 0
        return (ahead == 0) | (alive & (jnp.abs(ahead) < 3))

    return rule


def body(queries, keys, values, tile_mask):
    y, x, c = coordinates()
    mask = tile_mask.reshape(-1)
    own = jnp.concatenate([keys[None], values], axis=0)
    sign = lambda y: 1 if y else -1

    a1 = send(own, lambda z, y, x, c: (z + sign(y), y, x, c))
    b1 = send(own, lambda z, y, x, c: (z - sign(y), y, x, c))
    copies, own = spread(own)
    row = lax.all_to_all(copies, "ctx", 0, 0, axis_index_groups=ROWS)
    cn = send(own, lambda z, y, x, c: (z, y, x, c + 1))
    yn = send(own, lambda z, y, x, c: (z, y + 1, x, c))
    token_a = gate(GATE1, a1)
    token_b = gate(GATE1, b1)
    a2 = send(after(a1, token_a), lambda z, y, x, c: (z + sign(y), y, x, c))
    b2 = send(after(b1, token_b), lambda z, y, x, c: (z - sign(y), y, x, c))
    edge = after(jnp.where((y == 0) == (x < 2), a1, own), cn, yn)
    x1w = send(edge, lambda z, y, x, c: (z, y + 1, 3 - x, c) if x in (0, 3) else None)
    x2c = send(edge, lambda z, y, x, c: (z, y + 1, x + 2, c))
    yc = send(after(a1, cn, yn), lambda z, y, x, c: (z, y + 1, x, c))
    a4 = send(a2, lambda z, y, x, c: (z + 2 * sign(y), y, x, c))
    b4 = send(b2, lambda z, y, x, c: (z - 2 * sign(y), y, x, c))
    state = attend(
        queries,
        [
            (row, None),
            (cn, offset(0, lambda y, x, c: c == 0)),
            (yn, offset(3, lambda y, x, c: y == 0)),
            (a1, offset(4, lambda y, x, c: y == 0)),
            (b1, offset(4, lambda y, x, c: y != 0)),
            (a2, offset(5, lambda y, x, c: y == 0)),
            (b2, offset(5, lambda y, x, c: y != 0)),
        ],
        mask=mask,
        tokens=[token_a, token_b],
        later=[
            offset(3, lambda y, x, c: y != 0),
            offset(2, lambda y, x, c: x >= 2),
            offset(1, lambda y, x, c: x == 3, lambda y, x, c: (x == 0) | (x == 3)),
            offset(0, lambda y, x, c: c != 0),
            offset(6, lambda y, x, c: y == 0),
            offset(6, lambda y, x, c: y != 0),
        ],
    )
    beside = lax.dynamic_index_in_dim(
        row, jnp.where(c == 0, jnp.minimum(x + 1, 3), jnp.maximum(x - 1, 0)), 0, keepdims=False
    )
    near = jnp.where(x == jnp.where(c == 0, 3, 0), x1w, beside)
    cc = send(after(near, state[3]), lambda z, y, x, c: (z, y, x, c + 1))
    token = gate(GATE2, a4, b4, x2c, yc, state[3])
    return attend(queries, [yc, x2c, x1w, cc, a4, b4], state=state, tokens=[token])


def solution(mesh):
    in_specs = (P("ctx", "mp"), P("ctx", "mp"), P(None, "ctx", "mp"), P("ctx", None, None, None))
    out_specs = P(None, "ctx", "mp")
    return jax.shard_map(body, mesh=mesh, in_specs=in_specs, out_specs=out_specs, check_vma=False)
```

time: 123 us -> 84.9 us (0.69)
  starting transfers between devices: 75.5 us -> 48 us
  between operations: 15.6 us -> 0.21 us
  waiting for transfers between devices: 12.8 us -> 23.8 us
  local copies, waits for them, and re-layouts: 4.95 us -> 1.34 us
  other arithmetic: 3.76 us -> 1.99 us
    ppermute x14 -> x12, starting transfers between devices: 75.5 us -> 44 us  [send(): return lax.ppermute(block, 'ctx', pairs)]
    ppermute x14 -> x12, waiting for transfers between devices: 12.8 us -> 22.1 us  [send(): return lax.ppermute(block, 'ctx', pairs)]
    all_to_all x0 -> x1, starting transfers between devices: none -> 4.02 us  [body(): row = lax.all_to_all(copies, 'ctx', 0, 0, axis_index_groups=ROWS)]
    select_n x3 -> x2, other arithmetic: 2.69 us -> 0.92 us  [the longest x1 0.86 us: body(): edge = after(jnp.where((y == 0) == (x < 2), a1, own), cn, yn)]
    all_to_all x0 -> x1, waiting for transfers between devices: none -> 1.73 us  [body(): row = lax.all_to_all(copies, 'ctx', 0, 0, axis_index_groups=ROWS)]
    unnamed x16 -> x6, local copies, waits for them, and re-layouts: 2.9 us -> 1.34 us
    another operation x2 -> x0, local copies, waits for them, and re-layouts: 1.36 us -> none  [attend(): jnp.stack(live)]
    pallas_call x2 -> x6, Pallas kernels: 9.25 us -> 8.92 us  [the longest x2 7.93 us: attend(): pl.pallas_call(kernel, out_shape=shapes, in_specs=in_specs, out_specs=out...]
  transfers between devices with their start and end apart: 14 -> 13, of which waited for: 3 -> 5; matrix products, arithmetic and copies ran while one was open for 4% -> 1% of each run, Pallas kernels for 4% -> 6%
where the time goes in v2:
time: 84.9 us; the launch traced here: 84.3 us
  starting transfers between devices  48 us (57%)
  waiting for transfers between devices  23.8 us (28%)
  Pallas kernels  8.92 us (11%)
  other arithmetic  1.99 us (2%)
  local copies, waits for them, and re-layouts  1.34 us (2%)
    ppermute x12, starting transfers between devices, send(): return lax.ppermute(block, 'ctx', pairs)  44 us
    ppermute x12, waiting for transfers between devices, send(): return lax.ppermute(block, 'ctx', pairs)  22.1 us
    pallas_call x2, Pallas kernels, attend(): pl.pallas_call(kernel, out_shape=shapes, in_specs=in_specs, out_specs=out...  7.93 us
    all_to_all x1, starting transfers between devices, body(): row = lax.all_to_all(copies, 'ctx', 0, 0, axis_index_groups=ROWS)  4.02 us
    all_to_all x1, waiting for transfers between devices, body(): row = lax.all_to_all(copies, 'ctx', 0, 0, axis_index_groups=ROWS)  1.73 us
  transfers between devices with their start and end apart: 13, of which 5 were waited for; matrix products, arithmetic and copies ran while one was open for 1% of the time, Pallas kernels for 6%

profile of v2, /device:TPU:1, one launch (start us, length us, event | category | flops | bytes accessed | tf_op | source)
XLA Modules:
  0.0 84.3 jit_solution(16844661498131787228)
XLA Ops:
  0.0 1.1 %pad_maximum_fusion.own_ref = bf16[4,128,512]{2,1,0:T(8,128)(2,1)S(1)} fusion(bf16[3,128,512]{2,1,0:T(8,128)(2,1)} %param.6, bf16[1,128,512]{2,1,0:T(8,128)(2,1)} %bitcast.5), kind=kLoop, calls=%fused_computation | loop fusion | flops 262144 | bytes 1048576 | tf_op jit(solution)/shard_map/concatenate | solution.py:224
  1.1 12.0 %collective-permute-start = (bf16[4,128,512]{2,1,0:T(8,128)(2,1)S(1)}, bf16[4,128,512]{2,1,0:T(8,128)(2,1)S(1)}, u32[]{:S(2)}, u32[]{:S(2)}) collective-permute-start(bf16[4,128,512]{2,1,0:T(8,128)(2,1)S(1)} %pad_maximum_fusion.own_ref), channel_id=1, source_target_pairs={{0,480},{2,482},{4,484},{6,486},{8,488},{10,490},{12,492},{14,494}... | collective-permute-start | bytes 1572872 | tf_op jit(solution)/shard_map/ppermute | solution.py:43
  13.0 1.9 %collective-permute-start.6 = (bf16[4,128,512]{2,1,0:T(8,128)(2,1)S(1)}, bf16[4,128,512]{2,1,0:T(8,128)(2,1)}, u32[]{:S(2)}, u32[]{:S(2)}) collective-permute-start(bf16[4,128,512]{2,1,0:T(8,128)(2,1)S(1)} %pad_maximum_fusion.own_ref), channel_id=1, source_target_pairs={{0,32},{2,34},{4,36},{6,38},{8,40},{10,42},{12,44},{14,46},{16,496... | collective-permute-start | bytes 1572872 | tf_op jit(solution)/shard_map/ppermute | solution.py:43
  15.0 1.0 %shard_map.46 = (bf16[4,4,128,512]{3,2,1,0:T(8,128)(2,1)S(1)}, bf16[4,128,512]{2,1,0:T(8,128)(2,1)}) custom-call(bf16[4,128,512]{2,1,0:T(8,128)(2,1)S(1)} %pad_maximum_fusion.own_ref), custom_call_target="tpu_custom_call" | custom-call | flops 1000000 | bytes 262144 | tf_op jit(solution)/shard_map/pallas_call | solution.py:198
  16.0 0.0 copy-start
  16.0 1.3 %copy-done = bf16[4,4,128,512]{3,2,1,0:T(8,128)(2,1)} copy-done((bf16[4,4,128,512]{3,2,1,0:T(8,128)(2,1)}, bf16[4,4,128,512]{3,2,1,0:T(8,128)(2,1)S(1)}, u32[]{:S(2)}) %copy-start) | copy-done | bytes 2097176
  17.3 2.9 %collective-permute-start.1 = (bf16[4,128,512]{2,1,0:T(8,128)(2,1)}, bf16[4,128,512]{2,1,0:T(8,128)(2,1)}, u32[]{:S(2)}, u32[]{:S(2)}) collective-permute-start(bf16[4,128,512]{2,1,0:T(8,128)(2,1)} %get-tuple-element.16), channel_id=1, source_target_pairs={{0,2},{2,0},{4,6},{6,4},{8,10},{10,8},{12,14},{14,12},{16,18},{18,... | collective-permute-start | bytes 1572872 | tf_op jit(solution)/shard_map/ppermute | solution.py:43
  20.2 3.2 %collective-permute-start.2 = (bf16[4,128,512]{2,1,0:T(8,128)(2,1)}, bf16[4,128,512]{2,1,0:T(8,128)(2,1)}, u32[]{:S(2)}, u32[]{:S(2)}) collective-permute-start(bf16[4,128,512]{2,1,0:T(8,128)(2,1)} %get-tuple-element.16), channel_id=1, source_target_pairs={{0,16},{2,18},{4,20},{6,22},{8,24},{10,26},{12,28},{14,30},{16,0},... | collective-permute-start | bytes 1572872 | tf_op jit(solution)/shard_map/ppermute | solution.py:43
  23.4 4.0 %all-to-all-start = ((bf16[4,4,128,512]{3,2,1,0:T(8,128)(2,1)}), bf16[4,4,128,512]{3,2,1,0:T(8,128)(2,1)S(1)}, u32[]{:S(2)}, u32[]{:S(2)}) async-start(bf16[4,4,128,512]{3,2,1,0:T(8,128)(2,1)} %copy-done), calls=%async_computation | async-start | bytes 4194304 | tf_op jit(solution)/shard_map/all_to_all | solution.py:230
  27.4 0.0 collective-permute-done.refs_0_.refs_3_
  27.4 0.0 copy-start.1
  27.4 0.0 copy-start.2
  27.4 3.8 %collective-permute-start.7 = (bf16[4,128,512]{2,1,0:T(8,128)(2,1)S(1)}, bf16[4,128,512]{2,1,0:T(8,128)(2,1)}, u32[]{:S(2)}, u32[]{:S(2)}) collective-permute-start(bf16[4,128,512]{2,1,0:T(8,128)(2,1)S(1)} %collective-permute-done.refs_0_.refs_3_), channel_id=1, source_target_pairs={{0,480},{2,482},{4,484},{6,486},{8,488},{10,490},{12,492},{14,494}... | collective-permute-start | bytes 1572872 | tf_op jit(solution)/shard_map/ppermute | solution.py:43
  31.2 0.0 collective-permute-done.6.refs_0_.refs_4_
  31.2 1.9 %collective-permute-start.8 = (bf16[4,128,512]{2,1,0:T(8,128)(2,1)}, bf16[4,128,512]{2,1,0:T(8,128)(2,1)}, u32[]{:S(2)}, u32[]{:S(2)}) collective-permute-start(bf16[4,128,512]{2,1,0:T(8,128)(2,1)} %collective-permute-done.6.refs_0_.refs_4_), channel_id=1, source_target_pairs={{0,32},{2,34},{4,36},{6,38},{8,40},{10,42},{12,44},{14,46},{16,496... | collective-permute-start | bytes 1572872 | tf_op jit(solution)/shard_map/ppermute | solution.py:43
  33.2 0.9 %broadcast_select_fusion = bf16[4,128,512]{2,1,0:T(8,128)(2,1)} fusion(bf16[4,128,512]{2,1,0:T(8,128)(2,1)S(1)} %collective-permute-done.refs_0_.refs_3_, bf16[4,128,512]{2,1,0:T(8,128)(2,1)} %get-tuple-element.16, pred[]{:T(512)S(6)} %eq.14), kind=kLoop, calls=%fused_computation.2 | loop fusion | flops 262144 | bytes 1572865 | tf_op jit(solution)/shard_map/jit(_where)/select_n | solution.py:237
  34.0 0.0 collective-permute-done.1.refs_1_
  34.0 1.9 %collective-permute-done.2.refs_2_ = bf16[4,128,512]{2,1,0:T(8,128)(2,1)} collective-permute-done((bf16[4,128,512]{2,1,0:T(8,128)(2,1)}, bf16[4,128,512]{2,1,0:T(8,128)(2,1)}, u32[]{:S(2)}, u32[]{:S(2)}) %collective-permute-start.2) | collective-permute-done | bytes 524320 | tf_op jit(solution)/shard_map/ppermute | solution.py:43
  35.9 5.4 %collective-permute-start.5 = (bf16[4,128,512]{2,1,0:T(8,128)(2,1)}, bf16[4,128,512]{2,1,0:T(8,128)(2,1)S(1)}, u32[]{:S(2)}, u32[]{:S(2)}) collective-permute-start(bf16[4,128,512]{2,1,0:T(8,128)(2,1)} %broadcast_select_fusion), channel_id=1, source_target_pairs={{0,28},{2,30},{12,16},{14,18},{16,12},{18,14},{28,0},{30,2},{32,60... | collective-permute-start | bytes 1572872 | tf_op jit(solution)/shard_map/ppermute | solution.py:43
  41.3 1.9 %collective-permute-start.4 = (bf16[4,128,512]{2,1,0:T(8,128)(2,1)}, bf16[4,128,512]{2,1,0:T(8,128)(2,1)}, u32[]{:S(2)}, u32[]{:S(2)}) collective-permute-start(bf16[4,128,512]{2,1,0:T(8,128)(2,1)} %broadcast_select_fusion), channel_id=1, source_target_pairs={{0,24},{2,26},{4,28},{6,30},{8,16},{10,18},{12,20},{14,22},{16,8},... | collective-permute-start | bytes 1572872 | tf_op jit(solution)/shard_map/ppermute | solution.py:43
  43.3 2.1 %collective-permute-start.3 = (bf16[4,128,512]{2,1,0:T(8,128)(2,1)S(1)}, bf16[4,128,512]{2,1,0:T(8,128)(2,1)}, u32[]{:S(2)}, u32[]{:S(2)}) collective-permute-start(bf16[4,128,512]{2,1,0:T(8,128)(2,1)S(1)} %collective-permute-done.refs_0_.refs_3_), channel_id=1, source_target_pairs={{0,16},{2,18},{4,20},{6,22},{8,24},{10,26},{12,28},{14,30},{16,0},... | collective-permute-start | bytes 1572872 | tf_op jit(solution)/shard_map/ppermute | solution.py:43
  45.4 0.0 collective-permute-done.7.refs_5_
  45.4 4.1 %collective-permute-start.10 = (bf16[4,128,512]{2,1,0:T(8,128)(2,1)}, bf16[4,128,512]{2,1,0:T(8,128)(2,1)}, u32[]{:S(2)}, u32[]{:S(2)}) collective-permute-start(bf16[4,128,512]{2,1,0:T(8,128)(2,1)} %collective-permute-done.7.refs_5_), channel_id=1, source_target_pairs={{0,448},{2,450},{4,452},{6,454},{8,456},{10,458},{12,460},{14,462}... | collective-permute-start | bytes 1572872 | tf_op jit(solution)/shard_map/ppermute | solution.py:43
  49.5 0.0 collective-permute-done.8.refs_6_
  49.5 2.1 %collective-permute-start.11 = (bf16[4,128,512]{2,1,0:T(8,128)(2,1)}, bf16[4,128,512]{2,1,0:T(8,128)(2,1)}, u32[]{:S(2)}, u32[]{:S(2)}) collective-permute-start(bf16[4,128,512]{2,1,0:T(8,128)(2,1)} %collective-permute-done.8.refs_6_), channel_id=1, source_target_pairs={{0,64},{2,66},{4,68},{6,70},{8,72},{10,74},{12,76},{14,78},{16,464... | collective-permute-start | bytes 1572872 | tf_op jit(solution)/shard_map/ppermute | solution.py:43
  51.6 1.7 %all-to-all-done.refs_0_ = bf16[4,4,128,512]{3,2,1,0:T(8,128)(2,1)S(1)} async-done(((bf16[4,4,128,512]{3,2,1,0:T(8,128)(2,1)}), bf16[4,4,128,512]{3,2,1,0:T(8,128)(2,1)S(1)}, u32[]{:S(2)}, u32[]{:S(2)}) %all-to-all-start) | async-done | bytes 2097184 | tf_op jit(solution)/shard_map/all_to_all | solution.py:230
  53.3 0.0 copy-done.1
  53.3 0.0 copy-done.2
  53.3 4.0 %shard_map.49 = (f32[4,128,384]{2,1,0:T(8,128)S(1)}, f32[4,128,128]{2,1,0:T(8,128)S(1)}, f32[4,128,128]{2,1,0:T(8,128)S(1)}, f32[8,128]{1,0:T(8,128)S(1)}) custom-call(bf16[128,512]{1,0:T(8,128)(2,1)S(1)} %copy-done.1, s32[15]{0:T(128)S(1)} %bitcast.4, bf16[4,4,128,512]{3,2,1,0:T(8,128)(2,1)S(1)} %all-to-all-done.refs_0_, ...), custom_call_target="tpu_custom_call" | custom-call | flops 671088640 | bytes 5242880 | tf_op jit(solution)/shard_map/pallas_call | solution.py:144
  57.3 18.7 %collective-permute-done.5.refs_2_ = bf16[4,128,512]{2,1,0:T(8,128)(2,1)S(1)} collective-permute-done((bf16[4,128,512]{2,1,0:T(8,128)(2,1)}, bf16[4,128,512]{2,1,0:T(8,128)(2,1)S(1)}, u32[]{:S(2)}, u32[]{:S(2)}) %collective-permute-start.5) | collective-permute-done | bytes 524320 | tf_op jit(solution)/shard_map/ppermute | solution.py:43
  76.0 0.1 bitcast_select_fusion
  76.0 2.8 %collective-permute-start.9 = (bf16[4,128,512]{2,1,0:T(8,128)(2,1)S(1)}, bf16[4,128,512]{2,1,0:T(8,128)(2,1)S(1)}, u32[]{:S(2)}, u32[]{:S(2)}) collective-permute-start(bf16[4,128,512]{2,1,0:T(8,128)(2,1)S(1)} %bitcast_select_fusion), channel_id=1, source_target_pairs={{0,2},{2,0},{4,6},{6,4},{8,10},{10,8},{12,14},{14,12},{16,18},{18,... | collective-permute-start | bytes 1572872 | tf_op jit(solution)/shard_map/ppermute | solution.py:43
  78.8 0.0 collective-permute-done.4.refs_2_.refs_1_
  78.8 0.8 collective-permute-done.3.refs_3_.refs_0_
  79.7 0.0 collective-permute-done.10.refs_0_.refs_4_
  79.7 0.0 collective-permute-done.11.refs_1_.refs_5_
  79.7 0.7 collective-permute-done.9.refs_3_
  80.4 4.0 %shard_map.51 = bf16[3,128,512]{2,1,0:T(8,128)(2,1)} custom-call(bf16[128,512]{1,0:T(8,128)(2,1)S(1)} %copy-done.1, bf16[4,128,512]{2,1,0:T(8,128)(2,1)} %collective-permute-done.3.refs_3_.refs_0_, bf16[4,128,512]{2,1,0:T(8,128)(2,1)} %collective-permute-done.4.refs_2_.refs_1_, bf16[4,128,512]{2,1,0:T(8,128)(2,1)S(1)} %collective-permute-done.5.refs_2_, ...), custom_call_target="tpu_custom_call" | custom-call | flops 402653184 | bytes 3145728 | tf_op jit(solution)/shard_map/pallas_call | solution.py:144
  (3 shorter events, 0.0 us)
Async XLA Ops:
  1.1 26.3 %collective-permute-start = (bf16[4,128,512]{2,1,0:T(8,128)(2,1)S(1)}, bf16[4,128,512]{2,1,0:T(8,128)(2,1)S(1)}, u32[]{:S(2)}, u32[]{:S(2)}) collective-permute-start(bf16[4,128,512]{2,1,0:T(8,128)(2,1)S(1)} %pad_maximum_fusion.own_ref), channel_id=1, source_target_pairs={{0,480},{2,482},{4,484},{6,486},{8,488},{10,490},{12,492},{14,494}... | collective-permute-start | bytes 1572872 | tf_op jit(solution)/shard_map/ppermute | solution.py:43
  13.0 18.2 %collective-permute-start.6 = (bf16[4,128,512]{2,1,0:T(8,128)(2,1)S(1)}, bf16[4,128,512]{2,1,0:T(8,128)(2,1)}, u32[]{:S(2)}, u32[]{:S(2)}) collective-permute-start(bf16[4,128,512]{2,1,0:T(8,128)(2,1)S(1)} %pad_maximum_fusion.own_ref), channel_id=1, source_target_pairs={{0,32},{2,34},{4,36},{6,38},{8,40},{10,42},{12,44},{14,46},{16,496... | collective-permute-start | bytes 1572872 | tf_op jit(solution)/shard_map/ppermute | solution.py:43
  16.0 1.3 %copy-start = (bf16[4,4,128,512]{3,2,1,0:T(8,128)(2,1)}, bf16[4,4,128,512]{3,2,1,0:T(8,128)(2,1)S(1)}, u32[]{:S(2)}) copy-start(bf16[4,4,128,512]{3,2,1,0:T(8,128)(2,1)S(1)} %get-tuple-element.19) | copy-start | bytes 6291460
  17.3 16.7 %collective-permute-start.1 = (bf16[4,128,512]{2,1,0:T(8,128)(2,1)}, bf16[4,128,512]{2,1,0:T(8,128)(2,1)}, u32[]{:S(2)}, u32[]{:S(2)}) collective-permute-start(bf16[4,128,512]{2,1,0:T(8,128)(2,1)} %get-tuple-element.16), channel_id=1, source_target_pairs={{0,2},{2,0},{4,6},{6,4},{8,10},{10,8},{12,14},{14,12},{16,18},{18,... | collective-permute-start | bytes 1572872 | tf_op jit(solution)/shard_map/ppermute | solution.py:43
  20.2 15.8 %collective-permute-start.2 = (bf16[4,128,512]{2,1,0:T(8,128)(2,1)}, bf16[4,128,512]{2,1,0:T(8,128)(2,1)}, u32[]{:S(2)}, u32[]{:S(2)}) collective-permute-start(bf16[4,128,512]{2,1,0:T(8,128)(2,1)} %get-tuple-element.16), channel_id=1, source_target_pairs={{0,16},{2,18},{4,20},{6,22},{8,24},{10,26},{12,28},{14,30},{16,0},... | collective-permute-start | bytes 1572872 | tf_op jit(solution)/shard_map/ppermute | solution.py:43
  23.4 29.9 %all-to-all-start = ((bf16[4,4,128,512]{3,2,1,0:T(8,128)(2,1)}), bf16[4,4,128,512]{3,2,1,0:T(8,128)(2,1)S(1)}, u32[]{:S(2)}, u32[]{:S(2)}) async-start(bf16[4,4,128,512]{3,2,1,0:T(8,128)(2,1)} %copy-done), calls=%async_computation | async-start | bytes 4194304 | tf_op jit(solution)/shard_map/all_to_all | solution.py:230
  27.4 25.9 %copy-start.1 = (bf16[128,512]{1,0:T(8,128)(2,1)S(1)}, bf16[128,512]{1,0:T(8,128)(2,1)}, u32[]{:S(2)}) copy-start(bf16[128,512]{1,0:T(8,128)(2,1)} %q_ref.3) | copy-start | bytes 393220
  27.4 25.9 %copy-start.2 = (s32[1,15,1,1]{1,3,2,0:T(1,128)S(1)}, s32[1,15,1,1]{1,3,2,0:T(1,128)}, u32[]{:S(2)}) copy-start(s32[1,15,1,1]{1,3,2,0:T(1,128)} %param.7) | copy-start | bytes 184
  27.4 17.9 %collective-permute-start.7 = (bf16[4,128,512]{2,1,0:T(8,128)(2,1)S(1)}, bf16[4,128,512]{2,1,0:T(8,128)(2,1)}, u32[]{:S(2)}, u32[]{:S(2)}) collective-permute-start(bf16[4,128,512]{2,1,0:T(8,128)(2,1)S(1)} %collective-permute-done.refs_0_.refs_3_), channel_id=1, source_target_pairs={{0,480},{2,482},{4,484},{6,486},{8,488},{10,490},{12,492},{14,494}... | collective-permute-start | bytes 1572872 | tf_op jit(solution)/shard_map/ppermute | solution.py:43
  31.2 18.2 %collective-permute-start.8 = (bf16[4,128,512]{2,1,0:T(8,128)(2,1)}, bf16[4,128,512]{2,1,0:T(8,128)(2,1)}, u32[]{:S(2)}, u32[]{:S(2)}) collective-permute-start(bf16[4,128,512]{2,1,0:T(8,128)(2,1)} %collective-permute-done.6.refs_0_.refs_4_), channel_id=1, source_target_pairs={{0,32},{2,34},{4,36},{6,38},{8,40},{10,42},{12,44},{14,46},{16,496... | collective-permute-start | bytes 1572872 | tf_op jit(solution)/shard_map/ppermute | solution.py:43
  35.9 40.1 %collective-permute-start.5 = (bf16[4,128,512]{2,1,0:T(8,128)(2,1)}, bf16[4,128,512]{2,1,0:T(8,128)(2,1)S(1)}, u32[]{:S(2)}, u32[]{:S(2)}) collective-permute-start(bf16[4,128,512]{2,1,0:T(8,128)(2,1)} %broadcast_select_fusion), channel_id=1, source_target_pairs={{0,28},{2,30},{12,16},{14,18},{16,12},{18,14},{28,0},{30,2},{32,60... | collective-permute-start | bytes 1572872 | tf_op jit(solution)/shard_map/ppermute | solution.py:43
  41.3 37.5 %collective-permute-start.4 = (bf16[4,128,512]{2,1,0:T(8,128)(2,1)}, bf16[4,128,512]{2,1,0:T(8,128)(2,1)}, u32[]{:S(2)}, u32[]{:S(2)}) collective-permute-start(bf16[4,128,512]{2,1,0:T(8,128)(2,1)} %broadcast_select_fusion), channel_id=1, source_target_pairs={{0,24},{2,26},{4,28},{6,30},{8,16},{10,18},{12,20},{14,22},{16,8},... | collective-permute-start | bytes 1572872 | tf_op jit(solution)/shard_map/ppermute | solution.py:43
  43.3 36.4 %collective-permute-start.3 = (bf16[4,128,512]{2,1,0:T(8,128)(2,1)S(1)}, bf16[4,128,512]{2,1,0:T(8,128)(2,1)}, u32[]{:S(2)}, u32[]{:S(2)}) collective-permute-start(bf16[4,128,512]{2,1,0:T(8,128)(2,1)S(1)} %collective-permute-done.refs_0_.refs_3_), channel_id=1, source_target_pairs={{0,16},{2,18},{4,20},{6,22},{8,24},{10,26},{12,28},{14,30},{16,0},... | collective-permute-start | bytes 1572872 | tf_op jit(solution)/shard_map/ppermute | solution.py:43
  45.4 34.3 %collective-permute-start.10 = (bf16[4,128,512]{2,1,0:T(8,128)(2,1)}, bf16[4,128,512]{2,1,0:T(8,128)(2,1)}, u32[]{:S(2)}, u32[]{:S(2)}) collective-permute-start(bf16[4,128,512]{2,1,0:T(8,128)(2,1)} %collective-permute-done.7.refs_5_), channel_id=1, source_target_pairs={{0,448},{2,450},{4,452},{6,454},{8,456},{10,458},{12,460},{14,462}... | collective-permute-start | bytes 1572872 | tf_op jit(solution)/shard_map/ppermute | solution.py:43
  49.5 30.2 %collective-permute-start.11 = (bf16[4,128,512]{2,1,0:T(8,128)(2,1)}, bf16[4,128,512]{2,1,0:T(8,128)(2,1)}, u32[]{:S(2)}, u32[]{:S(2)}) collective-permute-start(bf16[4,128,512]{2,1,0:T(8,128)(2,1)} %collective-permute-done.8.refs_6_), channel_id=1, source_target_pairs={{0,64},{2,66},{4,68},{6,70},{8,72},{10,74},{12,76},{14,78},{16,464... | collective-permute-start | bytes 1572872 | tf_op jit(solution)/shard_map/ppermute | solution.py:43
  76.0 4.3 %collective-permute-start.9 = (bf16[4,128,512]{2,1,0:T(8,128)(2,1)S(1)}, bf16[4,128,512]{2,1,0:T(8,128)(2,1)S(1)}, u32[]{:S(2)}, u32[]{:S(2)}) collective-permute-start(bf16[4,128,512]{2,1,0:T(8,128)(2,1)S(1)} %bitcast_select_fusion), channel_id=1, source_target_pairs={{0,2},{2,0},{4,6},{6,4},{8,10},{10,8},{12,14},{14,12},{16,18},{18,... | collective-permute-start | bytes 1572872 | tf_op jit(solution)/shard_map/ppermute | solution.py:43

commit v3 on v2

--- a/solution.py
+++ b/solution.py
@@ -11,8 +11,7 @@
 HD = 128
 DEAD = -1e30
 MIB = 1024 * 1024
-SPREAD = 1_000_000
-GATE1, GATE2 = 20.0, 3.0
+GATE0, GATE1, GATE2 = 0.1, 20, 10.0
 FIRST, LAST = 1, 1
 ZS, YS, XS, CS = 16, 2, 4, 2
 
@@ -24,11 +23,6 @@
 def coordinates():
     here = lax.axis_index("ctx")
     return (here >> 3) & 1, (here >> 1) & 3, here & 1
-
-
-ROWS = [
-    [place(z, y, x, c) for x in range(XS)] for z in range(ZS) for y in range(YS) for c in range(CS)
-]
 
 
 def send(block, target):
@@ -70,17 +64,16 @@
     return largest, total, jnp.dot(weights, values, preferred_element_type=jnp.float32)
 
 
-def first_kernel(stacked, rules, later, q_ref, mask_ref, *refs):
-    blocks = []
-    for ref, depth in zip(refs, stacked):
-        blocks += [ref] if depth is None else [ref.at[j] for j in range(depth)]
+def first_kernel(rules, later, q_ref, mask_ref, *refs):
+    blocks = refs[:len(rules)]
     acc_ref, max_ref, sum_ref, later_ref, now_ref = refs[-5:]
     where = coordinates()
     row = (1, HD)
     for j, rule in enumerate(later):
         later_ref[j:j + 1] = jnp.where(rule(mask_ref, *where), jnp.zeros(row, jnp.float32), DEAD)
     for j, rule in enumerate(rules):
-        now_ref[j:j + 1] = jnp.where(rule(mask_ref, *where), jnp.zeros(row, jnp.float32), DEAD)
+        alive = True if rule is None else rule(mask_ref, *where)
+        now_ref[j:j + 1] = jnp.where(alive, jnp.zeros(row, jnp.float32), DEAD)
     biases = [now_ref.at[j:j + 1] for j in range(len(rules))]
     for head in range(q_ref.shape[1] // HD):
         window = slice(head * HD, (head + 1) * HD)
@@ -91,10 +84,10 @@
 
 
 def last_kernel(count, q_ref, *refs):
-    blocks = refs[:count]
+    blocks = [*refs[:count - 1], refs[count - 1].at[0], refs[count - 1].at[1]]
     acc_ref, max_ref, sum_ref, bias_ref = refs[count:count + 4]
     out_ref = refs[-1]
-    biases = [bias_ref.at[j:j + 1] for j in range(count)]
+    biases = [bias_ref.at[j:j + 1] for j in range(len(blocks))]
     for head in range(q_ref.shape[1] // HD):
         window = slice(head * HD, (head + 1) * HD)
         before = max_ref[head]
@@ -121,14 +114,11 @@
         shapes = jax.ShapeDtypeStruct((layers, rows, width), jnp.bfloat16)
         out_specs = vmem
     else:
-        stacked = [block.shape[0] if rule is None else None for block, rule in blocks]
-        rules = []
-        for block, rule in blocks:
-            rules += [beside(j) for j in range(block.shape[0])] if rule is None else [rule]
+        rules = [rule for _, rule in blocks]
         blocks = [block for block, _ in blocks]
-        count = len(rules)
-        layers = blocks[0].shape[-3] - 1
-        kernel = functools.partial(first_kernel, stacked, rules, later)
+        count = len(blocks)
+        layers = blocks[0].shape[0] - 1
+        kernel = functools.partial(first_kernel, rules, later)
         operands.append(mask)
         in_specs.append(pl.BlockSpec(memory_space=pltpu.SMEM))
         shapes = (
@@ -156,11 +146,9 @@
     )(*operands)
 
 
-def offset(level, ahead, there=None):
+def offset(level, ahead):
     def rule(mask_ref, y, x, c):
-        up = ahead(y, x, c)
-        alive = mask_ref[jnp.where(up, 2 * level + 1, 2 * level + 2)] != 0
-        return alive if there is None else alive & there(y, x, c)
+        return mask_ref[jnp.where(ahead(y, x, c), 2 * level + 1, 2 * level + 2)] != 0
 
     return rule
 
@@ -181,43 +169,6 @@
     )(*arrays)
 
 
-def spread_kernel(own_ref, copies_ref, own_out_ref, sems):
-    moves = [
-        pltpu.make_async_copy(own_ref, goal, sems.at[j])
-        for j, goal in enumerate([copies_ref.at[j] for j in range(XS)] + [own_out_ref])
-    ]
-    for move in moves:
-        move.start()
-    for move in moves:
-        move.wait()
-
-
-def spread(own):
-    vmem = pl.BlockSpec(memory_space=pltpu.VMEM)
-    anywhere = pl.BlockSpec(memory_space=pltpu.HBM)
-    return pl.pallas_call(
-        spread_kernel,
-        out_shape=(
-            jax.ShapeDtypeStruct((XS,) + own.shape, own.dtype),
-            jax.ShapeDtypeStruct(own.shape, own.dtype),
-        ),
-        in_specs=[vmem],
-        out_specs=(anywhere, anywhere),
-        scratch_shapes=[pltpu.SemaphoreType.DMA((XS + 1,))],
-        compiler_params=pltpu.CompilerParams(vmem_limit_bytes=3 * MIB),
-        cost_estimate=pl.CostEstimate(flops=SPREAD, bytes_accessed=own.size, transcendentals=0),
-    )(own)
-
-
-def beside(j):
-    def rule(mask_ref, y, x, c):
-        ahead = j - x
-        alive = mask_ref[jnp.where(ahead > 0, 1, 2) + 2 * jnp.abs(ahead)] != 0
-        return (ahead == 0) | (alive & (jnp.abs(ahead) < 3))
-
-    return rule
-
-
 def body(queries, keys, values, tile_mask):
     y, x, c = coordinates()
     mask = tile_mask.reshape(-1)
@@ -226,25 +177,29 @@
 
     a1 = send(own, lambda z, y, x, c: (z + sign(y), y, x, c))
     b1 = send(own, lambda z, y, x, c: (z - sign(y), y, x, c))
-    copies, own = spread(own)
-    row = lax.all_to_all(copies, "ctx", 0, 0, axis_index_groups=ROWS)
-    cn = send(own, lambda z, y, x, c: (z, y, x, c + 1))
     yn = send(own, lambda z, y, x, c: (z, y + 1, x, c))
+    x1n = send(own, lambda z, y, x, c: (z, y, x ^ 1, c))
+    x2n = send(after(own, b1), lambda z, y, x, c: (z, y, x + 2, c))
     token_a = gate(GATE1, a1)
-    token_b = gate(GATE1, b1)
+    token_b = gate(GATE0, b1)
     a2 = send(after(a1, token_a), lambda z, y, x, c: (z + sign(y), y, x, c))
     b2 = send(after(b1, token_b), lambda z, y, x, c: (z - sign(y), y, x, c))
-    edge = after(jnp.where((y == 0) == (x < 2), a1, own), cn, yn)
-    x1w = send(edge, lambda z, y, x, c: (z, y + 1, 3 - x, c) if x in (0, 3) else None)
+    edge = jnp.where((y == 0) == (x < 2), a1, own)
+    inner = (x == 1) | (x == 2)
+    x1w = send(
+        after(jnp.where(inner, own, edge), yn),
+        lambda z, y, x, c: (z, y if x in (1, 2) else y + 1, 3 - x, c),
+    )
     x2c = send(edge, lambda z, y, x, c: (z, y + 1, x + 2, c))
-    yc = send(after(a1, cn, yn), lambda z, y, x, c: (z, y + 1, x, c))
+    yc = send(after(a1, x1n), lambda z, y, x, c: (z, y + 1, x, c))
     a4 = send(a2, lambda z, y, x, c: (z + 2 * sign(y), y, x, c))
     b4 = send(b2, lambda z, y, x, c: (z - 2 * sign(y), y, x, c))
     state = attend(
         queries,
         [
-            (row, None),
-            (cn, offset(0, lambda y, x, c: c == 0)),
+            (own, None),
+            (x1n, offset(1, lambda y, x, c: x & 1 == 0)),
+            (x2n, offset(2, lambda y, x, c: x < 2)),
             (yn, offset(3, lambda y, x, c: y == 0)),
             (a1, offset(4, lambda y, x, c: y == 0)),
             (b1, offset(4, lambda y, x, c: y != 0)),
@@ -256,19 +211,17 @@
         later=[
             offset(3, lambda y, x, c: y != 0),
             offset(2, lambda y, x, c: x >= 2),
-            offset(1, lambda y, x, c: x == 3, lambda y, x, c: (x == 0) | (x == 3)),
-            offset(0, lambda y, x, c: c != 0),
+            offset(1, lambda y, x, c: x & 1 == 1),
             offset(6, lambda y, x, c: y == 0),
             offset(6, lambda y, x, c: y != 0),
+            offset(0, lambda y, x, c: c == 0),
+            offset(0, lambda y, x, c: c != 0),
         ],
     )
-    beside = lax.dynamic_index_in_dim(
-        row, jnp.where(c == 0, jnp.minimum(x + 1, 3), jnp.maximum(x - 1, 0)), 0, keepdims=False
-    )
-    near = jnp.where(x == jnp.where(c == 0, 3, 0), x1w, beside)
-    cc = send(after(near, state[3]), lambda z, y, x, c: (z, y, x, c + 1))
+    near = jnp.where(x & 1 == c, x1n, x1w)
+    cc = send(after(jnp.stack([own, near]), state[3]), lambda z, y, x, c: (z, y, x, c + 1))
     token = gate(GATE2, a4, b4, x2c, yc, state[3])
-    return attend(queries, [yc, x2c, x1w, cc, a4, b4], state=state, tokens=[token])
+    return attend(queries, [yc, x2c, x1w, a4, b4, cc], state=state, tokens=[token])
 
 
 def solution(mesh):

time: 84.9 us -> 80.9 us (0.953)
  waiting for transfers between devices: 23.8 us -> 20.5 us
  Pallas kernels: 8.92 us -> 5.86 us
  starting transfers between devices: 48 us -> 50.4 us
  local copies, waits for them, and re-layouts: 1.34 us -> 0.02 us
    ppermute x12 -> x13, starting transfers between devices: 44 us -> 50.4 us  [send(): return lax.ppermute(block, 'ctx', pairs)]
    all_to_all x1 -> x0, starting transfers between devices: 4.02 us -> none  [body(): row = lax.all_to_all(copies, 'ctx', 0, 0, axis_index_groups=ROWS)]
    pallas_call x2, Pallas kernels: 7.93 us -> 5.85 us  [attend(): pl.pallas_call(kernel, out_shape=shapes, in_specs=in_specs, out_specs=out...]
    all_to_all x1 -> x0, waiting for transfers between devices: 1.73 us -> none  [body(): row = lax.all_to_all(copies, 'ctx', 0, 0, axis_index_groups=ROWS)]
    ppermute x12 -> x13, waiting for transfers between devices: 22.1 us -> 20.5 us  [send(): return lax.ppermute(block, 'ctx', pairs)]
    unnamed x6 -> x10, local copies, waits for them, and re-layouts: 1.34 us -> 0.02 us
    pallas_call x1 -> x0, Pallas kernels: 0.99 us -> none  [spread(): pl.pallas_call(spread_kernel, out_shape=(jax.ShapeDtypeStruct((XS,) + own...]
  transfers between devices with their start and end apart: 13 -> 13, of which waited for: 5 -> 3; matrix products, arithmetic and copies ran while one was open for 1% -> 2% of each run, Pallas kernels for 6% -> 4%
where the time goes in v3:
time: 80.9 us; the launch traced here: 79.6 us
  starting transfers between devices  50.4 us (62%)
  waiting for transfers between devices  20.5 us (25%)
  Pallas kernels  5.86 us (7%)
  other arithmetic  2.5 us (3%)
    ppermute x13, starting transfers between devices, send(): return lax.ppermute(block, 'ctx', pairs)  50.4 us
    ppermute x13, waiting for transfers between devices, send(): return lax.ppermute(block, 'ctx', pairs)  20.5 us
    pallas_call x2, Pallas kernels, attend(): pl.pallas_call(kernel, out_shape=shapes, in_specs=in_specs, out_specs=out...  5.85 us
  transfers between devices with their start and end apart: 13, of which 3 were waited for; matrix products, arithmetic and copies ran while one was open for 2% of the time, Pallas kernels for 4%

profile of v3, /device:TPU:1, one launch (start us, length us, event | category | flops | bytes accessed | tf_op | source)
XLA Modules:
  0.0 79.6 jit_solution(1541607030801540459)
XLA Ops:
  0.0 1.1 %pad_maximum_fusion.1.refs_0_ = bf16[4,128,512]{2,1,0:T(8,128)(2,1)S(1)} fusion(bf16[3,128,512]{2,1,0:T(8,128)(2,1)} %param.6, bf16[1,128,512]{2,1,0:T(8,128)(2,1)} %bitcast.7), kind=kLoop, calls=%fused_computation.1 | loop fusion | flops 262144 | bytes 1048576 | tf_op jit(solution)/shard_map/concatenate | solution.py:175
  1.1 4.4 %collective-permute-start.8 = (bf16[4,128,512]{2,1,0:T(8,128)(2,1)S(1)}, bf16[4,128,512]{2,1,0:T(8,128)(2,1)S(1)}, u32[]{:S(2)}, u32[]{:S(2)}) collective-permute-start(bf16[4,128,512]{2,1,0:T(8,128)(2,1)S(1)} %pad_maximum_fusion.1.refs_0_), channel_id=1, source_target_pairs={{0,32},{2,34},{4,36},{6,38},{8,40},{10,42},{12,44},{14,46},{16,496... | collective-permute-start | bytes 1572872 | tf_op jit(solution)/shard_map/ppermute | solution.py:37
  5.5 9.5 %collective-permute-start = (bf16[4,128,512]{2,1,0:T(8,128)(2,1)S(1)}, bf16[4,128,512]{2,1,0:T(8,128)(2,1)S(1)}, u32[]{:S(2)}, u32[]{:S(2)}) collective-permute-start(bf16[4,128,512]{2,1,0:T(8,128)(2,1)S(1)} %pad_maximum_fusion.1.refs_0_), channel_id=1, source_target_pairs={{0,480},{2,482},{4,484},{6,486},{8,488},{10,490},{12,492},{14,494}... | collective-permute-start | bytes 1572872 | tf_op jit(solution)/shard_map/ppermute | solution.py:37
  15.0 3.2 %collective-permute-start.4 = (bf16[4,128,512]{2,1,0:T(8,128)(2,1)S(1)}, bf16[4,128,512]{2,1,0:T(8,128)(2,1)S(1)}, u32[]{:S(2)}, u32[]{:S(2)}) collective-permute-start(bf16[4,128,512]{2,1,0:T(8,128)(2,1)S(1)} %pad_maximum_fusion.1.refs_0_), channel_id=1, source_target_pairs={{0,16},{2,18},{4,20},{6,22},{8,24},{10,26},{12,28},{14,30},{16,0},... | collective-permute-start | bytes 1572872 | tf_op jit(solution)/shard_map/ppermute | solution.py:37
  18.2 3.1 %collective-permute-start.1 = (bf16[4,128,512]{2,1,0:T(8,128)(2,1)S(1)}, bf16[4,128,512]{2,1,0:T(8,128)(2,1)S(1)}, u32[]{:S(2)}, u32[]{:S(2)}) collective-permute-start(bf16[4,128,512]{2,1,0:T(8,128)(2,1)S(1)} %pad_maximum_fusion.1.refs_0_), channel_id=1, source_target_pairs={{0,4},{2,6},{4,0},{6,2},{8,12},{10,14},{12,8},{14,10},{16,20},{18,... | collective-permute-start | bytes 1572872 | tf_op jit(solution)/shard_map/ppermute | solution.py:37
  21.3 3.3 %collective-permute-done.8.refs_0_.refs_5_ = bf16[4,128,512]{2,1,0:T(8,128)(2,1)S(1)} collective-permute-done((bf16[4,128,512]{2,1,0:T(8,128)(2,1)S(1)}, bf16[4,128,512]{2,1,0:T(8,128)(2,1)S(1)}, u32[]{:S(2)}, u32[]{:S(2)}) %collective-permute-start.8) | collective-permute-done | bytes 524320 | tf_op jit(solution)/shard_map/ppermute | solution.py:37
  24.7 0.0 copy-start.3
  24.7 0.0 copy-start.4
  24.7 2.0 %collective-permute-start.9 = (bf16[4,128,512]{2,1,0:T(8,128)(2,1)S(1)}, bf16[4,128,512]{2,1,0:T(8,128)(2,1)}, u32[]{:S(2)}, u32[]{:S(2)}) collective-permute-start(bf16[4,128,512]{2,1,0:T(8,128)(2,1)S(1)} %collective-permute-done.8.refs_0_.refs_5_), channel_id=1, source_target_pairs={{0,32},{2,34},{4,36},{6,38},{8,40},{10,42},{12,44},{14,46},{16,496... | collective-permute-start | bytes 1572872 | tf_op jit(solution)/shard_map/ppermute | solution.py:37
  26.7 4.7 %collective-permute-start.11 = (bf16[4,128,512]{2,1,0:T(8,128)(2,1)S(1)}, bf16[4,128,512]{2,1,0:T(8,128)(2,1)}, u32[]{:S(2)}, u32[]{:S(2)}) collective-permute-start(bf16[4,128,512]{2,1,0:T(8,128)(2,1)S(1)} %pad_maximum_fusion.1.refs_0_), channel_id=1, source_target_pairs={{0,8},{2,10},{4,12},{6,14},{8,0},{10,2},{12,4},{14,6},{16,24},{18,... | collective-permute-start | bytes 1572872 | tf_op jit(solution)/shard_map/ppermute | solution.py:37
  31.4 0.0 collective-permute-done.refs_0_.refs_4_
  31.4 0.0 copy-start
  31.4 4.7 %collective-permute-start.6 = (bf16[4,128,512]{2,1,0:T(8,128)(2,1)S(1)}, bf16[4,128,512]{2,1,0:T(8,128)(2,1)}, u32[]{:S(2)}, u32[]{:S(2)}) collective-permute-start(bf16[4,128,512]{2,1,0:T(8,128)(2,1)S(1)} %collective-permute-done.refs_0_.refs_4_), channel_id=1, source_target_pairs={{0,480},{2,482},{4,484},{6,486},{8,488},{10,490},{12,492},{14,494}... | collective-permute-start | bytes 1572872 | tf_op jit(solution)/shard_map/ppermute | solution.py:37
  36.1 0.0 copy-done.3
  36.1 0.0 copy-done.4
  36.1 1.3 %broadcast_select_fusion = (bf16[4,128,512]{2,1,0:T(8,128)(2,1)}, bf16[4,128,512]{2,1,0:T(8,128)(2,1)}, bf16[1,4,128,512]{3,2,1,0:T(8,128)(2,1)}) fusion(pred[]{:T(512)S(6)} %or.3, bf16[3,128,512]{2,1,0:T(8,128)(2,1)S(1)} %copy-done.3, bf16[1,128,512]{2,1,0:T(8,128)(2,1)S(1)} %bitcast.8, bf16[4,128,512]{2,1,0:T(8,128)(2,1)S(1)} %collective-permute-done.refs_0_.refs_4_, ...), kind=kLoop, calls=%fused_computation.3 | loop fusion | flops 786432 | bytes 2621442 | tf_op jit(solution)/shard_map/jit(_where)/select_n | solution.py:190
  37.4 0.0 collective-permute-done.4.refs_3_
  37.4 3.5 %collective-permute-start.5 = (bf16[4,128,512]{2,1,0:T(8,128)(2,1)}, bf16[4,128,512]{2,1,0:T(8,128)(2,1)S(1)}, u32[]{:S(2)}, u32[]{:S(2)}) collective-permute-start(bf16[4,128,512]{2,1,0:T(8,128)(2,1)} %get-tuple-element.16), channel_id=1, source_target_pairs={{0,28},{2,30},{4,8},{6,10},{8,4},{10,6},{12,16},{14,18},{16,12},{1... | collective-permute-start | bytes 1572872 | tf_op jit(solution)/shard_map/ppermute | solution.py:37
  40.9 0.0 collective-permute-done.1.refs_1_
  40.9 2.4 %collective-permute-start.2 = (bf16[4,128,512]{2,1,0:T(8,128)(2,1)S(1)}, bf16[4,128,512]{2,1,0:T(8,128)(2,1)S(1)}, u32[]{:S(2)}, u32[]{:S(2)}) collective-permute-start(bf16[4,128,512]{2,1,0:T(8,128)(2,1)S(1)} %collective-permute-done.refs_0_.refs_4_), channel_id=1, source_target_pairs={{0,16},{2,18},{4,20},{6,22},{8,24},{10,26},{12,28},{14,30},{16,0},... | collective-permute-start | bytes 1572872 | tf_op jit(solution)/shard_map/ppermute | solution.py:37
  43.3 0.0 collective-permute-done.9.refs_7_
  43.3 0.0 copy-start.1
  43.3 3.1 %collective-permute-start.3 = (bf16[4,128,512]{2,1,0:T(8,128)(2,1)}, bf16[4,128,512]{2,1,0:T(8,128)(2,1)S(1)}, u32[]{:S(2)}, u32[]{:S(2)}) collective-permute-start(bf16[4,128,512]{2,1,0:T(8,128)(2,1)} %get-tuple-element.26), channel_id=1, source_target_pairs={{0,24},{2,26},{4,28},{6,30},{8,16},{10,18},{12,20},{14,22},{16,8},... | collective-permute-start | bytes 1572872 | tf_op jit(solution)/shard_map/ppermute | solution.py:37
  46.5 0.0 collective-permute-done.11.refs_2_
  46.5 1.9 %collective-permute-start.10 = (bf16[4,128,512]{2,1,0:T(8,128)(2,1)}, bf16[4,128,512]{2,1,0:T(8,128)(2,1)S(1)}, u32[]{:S(2)}, u32[]{:S(2)}) collective-permute-start(bf16[4,128,512]{2,1,0:T(8,128)(2,1)} %collective-permute-done.9.refs_7_), channel_id=1, source_target_pairs={{0,64},{2,66},{4,68},{6,70},{8,72},{10,74},{12,76},{14,78},{16,464... | collective-permute-start | bytes 1572872 | tf_op jit(solution)/shard_map/ppermute | solution.py:37
  48.4 0.0 collective-permute-done.6.refs_6_
  48.4 5.5 %collective-permute-start.7 = (bf16[4,128,512]{2,1,0:T(8,128)(2,1)}, bf16[4,128,512]{2,1,0:T(8,128)(2,1)S(1)}, u32[]{:S(2)}, u32[]{:S(2)}) collective-permute-start(bf16[4,128,512]{2,1,0:T(8,128)(2,1)} %collective-permute-done.6.refs_6_), channel_id=1, source_target_pairs={{0,448},{2,450},{4,452},{6,454},{8,456},{10,458},{12,460},{14,462}... | collective-permute-start | bytes 1572872 | tf_op jit(solution)/shard_map/ppermute | solution.py:37
  53.9 0.0 copy-done
  53.9 0.0 copy-done.1
  53.9 3.2 %shard_map.48 = (f32[4,128,384]{2,1,0:T(8,128)S(1)}, f32[4,128,128]{2,1,0:T(8,128)S(1)}, f32[4,128,128]{2,1,0:T(8,128)S(1)}, f32[8,128]{1,0:T(8,128)S(1)}) custom-call(bf16[128,512]{1,0:T(8,128)(2,1)S(1)} %copy-done, s32[15]{0:T(128)S(1)} %bitcast.6, bf16[4,128,512]{2,1,0:T(8,128)(2,1)S(1)} %pad_maximum_fusion.1.refs_0_, ...), custom_call_target="tpu_custom_call" | custom-call | flops 536870912 | bytes 4194304 | tf_op jit(solution)/shard_map/pallas_call | solution.py:134
  57.2 0.0 copy-start.2
  57.2 12.6 %collective-permute-done.5.refs_2_ = bf16[4,128,512]{2,1,0:T(8,128)(2,1)S(1)} collective-permute-done((bf16[4,128,512]{2,1,0:T(8,128)(2,1)}, bf16[4,128,512]{2,1,0:T(8,128)(2,1)S(1)}, u32[]{:S(2)}, u32[]{:S(2)}) %collective-permute-start.5) | collective-permute-done | bytes 524320 | tf_op jit(solution)/shard_map/ppermute | solution.py:37
  69.8 0.1 select_bitcast_fusion
  69.9 0.0 copy-done.2
  69.9 0.1 pad_maximum_fusion
  70.0 2.5 %collective-permute-start.12 = (bf16[2,4,128,512]{3,2,1,0:T(8,128)(2,1)S(1)}, bf16[2,4,128,512]{3,2,1,0:T(8,128)(2,1)S(1)}, u32[]{:S(2)}, u32[]{:S(2)}) collective-permute-start(bf16[2,4,128,512]{3,2,1,0:T(8,128)(2,1)S(1)} %pad_maximum_fusion), channel_id=1, source_target_pairs={{0,2},{2,0},{4,6},{6,4},{8,10},{10,8},{12,14},{14,12},{16,18},{18,... | collective-permute-start | bytes 3145736 | tf_op jit(solution)/shard_map/ppermute | solution.py:37
  72.5 4.5 %collective-permute-done.2.refs_3_.refs_0_ = bf16[4,128,512]{2,1,0:T(8,128)(2,1)S(1)} collective-permute-done((bf16[4,128,512]{2,1,0:T(8,128)(2,1)S(1)}, bf16[4,128,512]{2,1,0:T(8,128)(2,1)S(1)}, u32[]{:S(2)}, u32[]{:S(2)}) %collective-permute-start.2) | collective-permute-done | bytes 524320 | tf_op jit(solution)/shard_map/ppermute | solution.py:37
  77.0 0.0 collective-permute-done.3.refs_2_.refs_1_
  77.0 0.0 collective-permute-done.10.refs_1_.refs_4_
  77.0 0.0 collective-permute-done.7.refs_0_.refs_3_
  77.0 0.0 collective-permute-done.12.refs_5_
  77.0 2.6 %shard_map.50 = bf16[3,128,512]{2,1,0:T(8,128)(2,1)} custom-call(bf16[128,512]{1,0:T(8,128)(2,1)S(1)} %copy-done, bf16[4,128,512]{2,1,0:T(8,128)(2,1)S(1)} %collective-permute-done.2.refs_3_.refs_0_, bf16[4,128,512]{2,1,0:T(8,128)(2,1)S(1)} %collective-permute-done.3.refs_2_.refs_1_, bf16[4,128,512]{2,1,0:T(8,128)(2,1)S(1)} %collective-permute-done.5.refs_2_, ...), custom_call_target="tpu_custom_call" | custom-call | flops 402653184 | bytes 3145728 | tf_op jit(solution)/shard_map/pallas_call | solution.py:134
  (3 shorter events, 0.0 us)
Async XLA Ops:
  1.1 23.6 %collective-permute-start.8 = (bf16[4,128,512]{2,1,0:T(8,128)(2,1)S(1)}, bf16[4,128,512]{2,1,0:T(8,128)(2,1)S(1)}, u32[]{:S(2)}, u32[]{:S(2)}) collective-permute-start(bf16[4,128,512]{2,1,0:T(8,128)(2,1)S(1)} %pad_maximum_fusion.1.refs_0_), channel_id=1, source_target_pairs={{0,32},{2,34},{4,36},{6,38},{8,40},{10,42},{12,44},{14,46},{16,496... | collective-permute-start | bytes 1572872 | tf_op jit(solution)/shard_map/ppermute | solution.py:37
  5.5 25.9 %collective-permute-start = (bf16[4,128,512]{2,1,0:T(8,128)(2,1)S(1)}, bf16[4,128,512]{2,1,0:T(8,128)(2,1)S(1)}, u32[]{:S(2)}, u32[]{:S(2)}) collective-permute-start(bf16[4,128,512]{2,1,0:T(8,128)(2,1)S(1)} %pad_maximum_fusion.1.refs_0_), channel_id=1, source_target_pairs={{0,480},{2,482},{4,484},{6,486},{8,488},{10,490},{12,492},{14,494}... | collective-permute-start | bytes 1572872 | tf_op jit(solution)/shard_map/ppermute | solution.py:37
  15.0 22.5 %collective-permute-start.4 = (bf16[4,128,512]{2,1,0:T(8,128)(2,1)S(1)}, bf16[4,128,512]{2,1,0:T(8,128)(2,1)S(1)}, u32[]{:S(2)}, u32[]{:S(2)}) collective-permute-start(bf16[4,128,512]{2,1,0:T(8,128)(2,1)S(1)} %pad_maximum_fusion.1.refs_0_), channel_id=1, source_target_pairs={{0,16},{2,18},{4,20},{6,22},{8,24},{10,26},{12,28},{14,30},{16,0},... | collective-permute-start | bytes 1572872 | tf_op jit(solution)/shard_map/ppermute | solution.py:37
  18.2 22.7 %collective-permute-start.1 = (bf16[4,128,512]{2,1,0:T(8,128)(2,1)S(1)}, bf16[4,128,512]{2,1,0:T(8,128)(2,1)S(1)}, u32[]{:S(2)}, u32[]{:S(2)}) collective-permute-start(bf16[4,128,512]{2,1,0:T(8,128)(2,1)S(1)} %pad_maximum_fusion.1.refs_0_), channel_id=1, source_target_pairs={{0,4},{2,6},{4,0},{6,2},{8,12},{10,14},{12,8},{14,10},{16,20},{18,... | collective-permute-start | bytes 1572872 | tf_op jit(solution)/shard_map/ppermute | solution.py:37
  24.7 11.5 %copy-start.3 = (bf16[3,128,512]{2,1,0:T(8,128)(2,1)S(1)}, bf16[3,128,512]{2,1,0:T(8,128)(2,1)}, u32[]{:S(2)}) copy-start(bf16[3,128,512]{2,1,0:T(8,128)(2,1)} %param.6) | copy-start | bytes 1179652
  24.7 11.5 %copy-start.4 = (bf16[128,512]{1,0:T(8,128)(2,1)S(1)}, bf16[128,512]{1,0:T(8,128)(2,1)}, u32[]{:S(2)}) copy-start(bf16[128,512]{1,0:T(8,128)(2,1)} %param.5) | copy-start | bytes 393220
  24.7 18.6 %collective-permute-start.9 = (bf16[4,128,512]{2,1,0:T(8,128)(2,1)S(1)}, bf16[4,128,512]{2,1,0:T(8,128)(2,1)}, u32[]{:S(2)}, u32[]{:S(2)}) collective-permute-start(bf16[4,128,512]{2,1,0:T(8,128)(2,1)S(1)} %collective-permute-done.8.refs_0_.refs_5_), channel_id=1, source_target_pairs={{0,32},{2,34},{4,36},{6,38},{8,40},{10,42},{12,44},{14,46},{16,496... | collective-permute-start | bytes 1572872 | tf_op jit(solution)/shard_map/ppermute | solution.py:37
  26.7 19.8 %collective-permute-start.11 = (bf16[4,128,512]{2,1,0:T(8,128)(2,1)S(1)}, bf16[4,128,512]{2,1,0:T(8,128)(2,1)}, u32[]{:S(2)}, u32[]{:S(2)}) collective-permute-start(bf16[4,128,512]{2,1,0:T(8,128)(2,1)S(1)} %pad_maximum_fusion.1.refs_0_), channel_id=1, source_target_pairs={{0,8},{2,10},{4,12},{6,14},{8,0},{10,2},{12,4},{14,6},{16,24},{18,... | collective-permute-start | bytes 1572872 | tf_op jit(solution)/shard_map/ppermute | solution.py:37
  31.4 22.5 %copy-start = (bf16[128,512]{1,0:T(8,128)(2,1)S(1)}, bf16[128,512]{1,0:T(8,128)(2,1)}, u32[]{:S(2)}) copy-start(bf16[128,512]{1,0:T(8,128)(2,1)} %q_ref.3) | copy-start | bytes 393220
  31.4 17.0 %collective-permute-start.6 = (bf16[4,128,512]{2,1,0:T(8,128)(2,1)S(1)}, bf16[4,128,512]{2,1,0:T(8,128)(2,1)}, u32[]{:S(2)}, u32[]{:S(2)}) collective-permute-start(bf16[4,128,512]{2,1,0:T(8,128)(2,1)S(1)} %collective-permute-done.refs_0_.refs_4_), channel_id=1, source_target_pairs={{0,480},{2,482},{4,484},{6,486},{8,488},{10,490},{12,492},{14,494}... | collective-permute-start | bytes 1572872 | tf_op jit(solution)/shard_map/ppermute | solution.py:37
  37.4 32.4 %collective-permute-start.5 = (bf16[4,128,512]{2,1,0:T(8,128)(2,1)}, bf16[4,128,512]{2,1,0:T(8,128)(2,1)S(1)}, u32[]{:S(2)}, u32[]{:S(2)}) collective-permute-start(bf16[4,128,512]{2,1,0:T(8,128)(2,1)} %get-tuple-element.16), channel_id=1, source_target_pairs={{0,28},{2,30},{4,8},{6,10},{8,4},{10,6},{12,16},{14,18},{16,12},{1... | collective-permute-start | bytes 1572872 | tf_op jit(solution)/shard_map/ppermute | solution.py:37
  40.9 36.0 %collective-permute-start.2 = (bf16[4,128,512]{2,1,0:T(8,128)(2,1)S(1)}, bf16[4,128,512]{2,1,0:T(8,128)(2,1)S(1)}, u32[]{:S(2)}, u32[]{:S(2)}) collective-permute-start(bf16[4,128,512]{2,1,0:T(8,128)(2,1)S(1)} %collective-permute-done.refs_0_.refs_4_), channel_id=1, source_target_pairs={{0,16},{2,18},{4,20},{6,22},{8,24},{10,26},{12,28},{14,30},{16,0},... | collective-permute-start | bytes 1572872 | tf_op jit(solution)/shard_map/ppermute | solution.py:37
  43.3 10.6 %copy-start.1 = (s32[1,15,1,1]{1,3,2,0:T(1,128)S(1)}, s32[1,15,1,1]{1,3,2,0:T(1,128)}, u32[]{:S(2)}) copy-start(s32[1,15,1,1]{1,3,2,0:T(1,128)} %param.7) | copy-start | bytes 184
  43.3 33.6 %collective-permute-start.3 = (bf16[4,128,512]{2,1,0:T(8,128)(2,1)}, bf16[4,128,512]{2,1,0:T(8,128)(2,1)S(1)}, u32[]{:S(2)}, u32[]{:S(2)}) collective-permute-start(bf16[4,128,512]{2,1,0:T(8,128)(2,1)} %get-tuple-element.26), channel_id=1, source_target_pairs={{0,24},{2,26},{4,28},{6,30},{8,16},{10,18},{12,20},{14,22},{16,8},... | collective-permute-start | bytes 1572872 | tf_op jit(solution)/shard_map/ppermute | solution.py:37
  46.5 30.5 %collective-permute-start.10 = (bf16[4,128,512]{2,1,0:T(8,128)(2,1)}, bf16[4,128,512]{2,1,0:T(8,128)(2,1)S(1)}, u32[]{:S(2)}, u32[]{:S(2)}) collective-permute-start(bf16[4,128,512]{2,1,0:T(8,128)(2,1)} %collective-permute-done.9.refs_7_), channel_id=1, source_target_pairs={{0,64},{2,66},{4,68},{6,70},{8,72},{10,74},{12,76},{14,78},{16,464... | collective-permute-start | bytes 1572872 | tf_op jit(solution)/shard_map/ppermute | solution.py:37
  48.4 28.5 %collective-permute-start.7 = (bf16[4,128,512]{2,1,0:T(8,128)(2,1)}, bf16[4,128,512]{2,1,0:T(8,128)(2,1)S(1)}, u32[]{:S(2)}, u32[]{:S(2)}) collective-permute-start(bf16[4,128,512]{2,1,0:T(8,128)(2,1)} %collective-permute-done.6.refs_6_), channel_id=1, source_target_pairs={{0,448},{2,450},{4,452},{6,454},{8,456},{10,458},{12,460},{14,462}... | collective-permute-start | bytes 1572872 | tf_op jit(solution)/shard_map/ppermute | solution.py:37
  57.2 12.7 %copy-start.2 = (bf16[1,4,128,512]{3,2,1,0:T(8,128)(2,1)S(1)}, bf16[1,4,128,512]{3,2,1,0:T(8,128)(2,1)}, u32[]{:S(2)}) copy-start(bf16[1,4,128,512]{3,2,1,0:T(8,128)(2,1)} %get-tuple-element.27) | copy-start | bytes 1572868
  70.0 7.0 %collective-permute-start.12 = (bf16[2,4,128,512]{3,2,1,0:T(8,128)(2,1)S(1)}, bf16[2,4,128,512]{3,2,1,0:T(8,128)(2,1)S(1)}, u32[]{:S(2)}, u32[]{:S(2)}) collective-permute-start(bf16[2,4,128,512]{3,2,1,0:T(8,128)(2,1)S(1)} %pad_maximum_fusion), channel_id=1, source_target_pairs={{0,2},{2,0},{4,6},{6,4},{8,10},{10,8},{12,14},{14,12},{16,18},{18,... | collective-permute-start | bytes 3145736 | tf_op jit(solution)/shard_map/ppermute | solution.py:37

commit v4 on v3

--- a/solution.py
+++ b/solution.py
@@ -41,9 +41,8 @@
     return lax.optimization_barrier((block, *others))[0]
 
 
-def attend_head(q_ref, blocks, biases, window, before=None):
+def weigh(q_ref, blocks, biases, window, before=None):
     rows = q_ref.shape[0]
-    layers = blocks[0].shape[0] - 1
     keys = jnp.concatenate([b[0, :, window] for b in blocks], axis=0)
     scores = lax.dot_general(
         q_ref[:, window], keys, (((1,), (1,)), ((), ())), preferred_element_type=jnp.float32
@@ -56,12 +55,16 @@
         largest = jnp.maximum(largest, before)
     probs = [jnp.exp2(s - largest) for s in parts]
     total = jnp.sum(functools.reduce(jnp.add, probs), axis=1, keepdims=True)
-    weights = jnp.concatenate([p.astype(jnp.bfloat16) for p in probs], axis=1)
+    return largest, total, jnp.concatenate([p.astype(jnp.bfloat16) for p in probs], axis=1)
+
+
+def mix(weights, blocks, window):
+    layers = blocks[0].shape[0] - 1
     values = jnp.concatenate(
         [jnp.concatenate([b[1 + layer, :, window] for layer in range(layers)], axis=1) for b in blocks],
         axis=0,
     )
-    return largest, total, jnp.dot(weights, values, preferred_element_type=jnp.float32)
+    return jnp.dot(weights, values, preferred_element_type=jnp.float32)
 
 
 def first_kernel(rules, later, q_ref, mask_ref, *refs):
@@ -77,10 +80,10 @@
     biases = [now_ref.at[j:j + 1] for j in range(len(rules))]
     for head in range(q_ref.shape[1] // HD):
         window = slice(head * HD, (head + 1) * HD)
-        largest, total, acc = attend_head(q_ref, blocks, biases, window)
+        largest, total, weights = weigh(q_ref, blocks, biases, window)
         max_ref[head] = jnp.broadcast_to(largest, max_ref.shape[1:])
         sum_ref[head] = jnp.broadcast_to(total, sum_ref.shape[1:])
-        acc_ref[head] = acc
+        acc_ref[head] = mix(weights, blocks, window)
 
 
 def last_kernel(count, q_ref, *refs):
@@ -88,16 +91,18 @@
     acc_ref, max_ref, sum_ref, bias_ref = refs[count:count + 4]
     out_ref = refs[-1]
     biases = [bias_ref.at[j:j + 1] for j in range(len(blocks))]
-    for head in range(q_ref.shape[1] // HD):
-        window = slice(head * HD, (head + 1) * HD)
-        before = max_ref[head]
-        largest, total, acc = attend_head(q_ref, blocks, biases, window, before)
-        shrink = jnp.exp2(before - largest)
+    heads = range(q_ref.shape[1] // HD)
+    windows = [slice(head * HD, (head + 1) * HD) for head in heads]
+    weighed = [weigh(q_ref, blocks, biases, windows[head], max_ref[head]) for head in heads]
+    for head in heads:
+        largest, total, weights = weighed[head]
+        acc = mix(weights, blocks, windows[head])
+        shrink = jnp.exp2(max_ref[head] - largest)
         inverse = 1.0 / (total + sum_ref[head] * shrink)
         for layer in range(out_ref.shape[0]):
             part = slice(layer * HD, (layer + 1) * HD)
             share = acc[:, part] + acc_ref[head, :, part] * shrink
-            out_ref[layer, :, window] = (share * inverse).astype(out_ref.dtype)
+            out_ref[layer, :, windows[head]] = (share * inverse).astype(out_ref.dtype)
 
 
 def attend(queries, blocks, mask=None, later=None, state=(), tokens=()):

time: 80.9 us -> 80.2 us (level)
  no operation moved by 1% of the time
where the time goes in v4:
time: 80.2 us; the launch traced here: 78.9 us
  starting transfers between devices  50.4 us (63%)
  waiting for transfers between devices  20.5 us (26%)
  Pallas kernels  5.17 us (6%)
  other arithmetic  2.5 us (3%)
    ppermute x13, starting transfers between devices, send(): return lax.ppermute(block, 'ctx', pairs)  50.4 us
    ppermute x13, waiting for transfers between devices, send(): return lax.ppermute(block, 'ctx', pairs)  20.5 us
    pallas_call x2, Pallas kernels, attend(): pl.pallas_call(kernel, out_shape=shapes, in_specs=in_specs, out_specs=out...  5.16 us
  transfers between devices with their start and end apart: 13, of which 3 were waited for; matrix products, arithmetic and copies ran while one was open for 2% of the time, Pallas kernels for 4%

profile of v4, /device:TPU:1, one launch (start us, length us, event | category | flops | bytes accessed | tf_op | source)
XLA Modules:
  0.0 78.9 jit_solution(5227190516854616569)
XLA Ops:
  0.0 1.1 %pad_maximum_fusion.1.refs_0_ = bf16[4,128,512]{2,1,0:T(8,128)(2,1)S(1)} fusion(bf16[3,128,512]{2,1,0:T(8,128)(2,1)} %param.6, bf16[1,128,512]{2,1,0:T(8,128)(2,1)} %bitcast.7), kind=kLoop, calls=%fused_computation.1 | loop fusion | flops 262144 | bytes 1048576 | tf_op jit(solution)/shard_map/concatenate | solution.py:180
  1.1 4.4 %collective-permute-start.8 = (bf16[4,128,512]{2,1,0:T(8,128)(2,1)S(1)}, bf16[4,128,512]{2,1,0:T(8,128)(2,1)S(1)}, u32[]{:S(2)}, u32[]{:S(2)}) collective-permute-start(bf16[4,128,512]{2,1,0:T(8,128)(2,1)S(1)} %pad_maximum_fusion.1.refs_0_), channel_id=1, source_target_pairs={{0,32},{2,34},{4,36},{6,38},{8,40},{10,42},{12,44},{14,46},{16,496... | collective-permute-start | bytes 1572872 | tf_op jit(solution)/shard_map/ppermute | solution.py:37
  5.5 9.5 %collective-permute-start = (bf16[4,128,512]{2,1,0:T(8,128)(2,1)S(1)}, bf16[4,128,512]{2,1,0:T(8,128)(2,1)S(1)}, u32[]{:S(2)}, u32[]{:S(2)}) collective-permute-start(bf16[4,128,512]{2,1,0:T(8,128)(2,1)S(1)} %pad_maximum_fusion.1.refs_0_), channel_id=1, source_target_pairs={{0,480},{2,482},{4,484},{6,486},{8,488},{10,490},{12,492},{14,494}... | collective-permute-start | bytes 1572872 | tf_op jit(solution)/shard_map/ppermute | solution.py:37
  15.0 3.2 %collective-permute-start.4 = (bf16[4,128,512]{2,1,0:T(8,128)(2,1)S(1)}, bf16[4,128,512]{2,1,0:T(8,128)(2,1)S(1)}, u32[]{:S(2)}, u32[]{:S(2)}) collective-permute-start(bf16[4,128,512]{2,1,0:T(8,128)(2,1)S(1)} %pad_maximum_fusion.1.refs_0_), channel_id=1, source_target_pairs={{0,16},{2,18},{4,20},{6,22},{8,24},{10,26},{12,28},{14,30},{16,0},... | collective-permute-start | bytes 1572872 | tf_op jit(solution)/shard_map/ppermute | solution.py:37
  18.2 3.1 %collective-permute-start.1 = (bf16[4,128,512]{2,1,0:T(8,128)(2,1)S(1)}, bf16[4,128,512]{2,1,0:T(8,128)(2,1)S(1)}, u32[]{:S(2)}, u32[]{:S(2)}) collective-permute-start(bf16[4,128,512]{2,1,0:T(8,128)(2,1)S(1)} %pad_maximum_fusion.1.refs_0_), channel_id=1, source_target_pairs={{0,4},{2,6},{4,0},{6,2},{8,12},{10,14},{12,8},{14,10},{16,20},{18,... | collective-permute-start | bytes 1572872 | tf_op jit(solution)/shard_map/ppermute | solution.py:37
  21.3 3.3 %collective-permute-done.8.refs_0_.refs_5_ = bf16[4,128,512]{2,1,0:T(8,128)(2,1)S(1)} collective-permute-done((bf16[4,128,512]{2,1,0:T(8,128)(2,1)S(1)}, bf16[4,128,512]{2,1,0:T(8,128)(2,1)S(1)}, u32[]{:S(2)}, u32[]{:S(2)}) %collective-permute-start.8) | collective-permute-done | bytes 524320 | tf_op jit(solution)/shard_map/ppermute | solution.py:37
  24.7 0.0 copy-start.3
  24.7 0.0 copy-start.4
  24.7 2.0 %collective-permute-start.9 = (bf16[4,128,512]{2,1,0:T(8,128)(2,1)S(1)}, bf16[4,128,512]{2,1,0:T(8,128)(2,1)}, u32[]{:S(2)}, u32[]{:S(2)}) collective-permute-start(bf16[4,128,512]{2,1,0:T(8,128)(2,1)S(1)} %collective-permute-done.8.refs_0_.refs_5_), channel_id=1, source_target_pairs={{0,32},{2,34},{4,36},{6,38},{8,40},{10,42},{12,44},{14,46},{16,496... | collective-permute-start | bytes 1572872 | tf_op jit(solution)/shard_map/ppermute | solution.py:37
  26.7 4.7 %collective-permute-start.11 = (bf16[4,128,512]{2,1,0:T(8,128)(2,1)S(1)}, bf16[4,128,512]{2,1,0:T(8,128)(2,1)}, u32[]{:S(2)}, u32[]{:S(2)}) collective-permute-start(bf16[4,128,512]{2,1,0:T(8,128)(2,1)S(1)} %pad_maximum_fusion.1.refs_0_), channel_id=1, source_target_pairs={{0,8},{2,10},{4,12},{6,14},{8,0},{10,2},{12,4},{14,6},{16,24},{18,... | collective-permute-start | bytes 1572872 | tf_op jit(solution)/shard_map/ppermute | solution.py:37
  31.4 0.0 collective-permute-done.refs_0_.refs_4_
  31.4 0.0 copy-start
  31.4 4.7 %collective-permute-start.6 = (bf16[4,128,512]{2,1,0:T(8,128)(2,1)S(1)}, bf16[4,128,512]{2,1,0:T(8,128)(2,1)}, u32[]{:S(2)}, u32[]{:S(2)}) collective-permute-start(bf16[4,128,512]{2,1,0:T(8,128)(2,1)S(1)} %collective-permute-done.refs_0_.refs_4_), channel_id=1, source_target_pairs={{0,480},{2,482},{4,484},{6,486},{8,488},{10,490},{12,492},{14,494}... | collective-permute-start | bytes 1572872 | tf_op jit(solution)/shard_map/ppermute | solution.py:37
  36.1 0.0 copy-done.3
  36.1 0.0 copy-done.4
  36.1 1.3 %broadcast_select_fusion = (bf16[4,128,512]{2,1,0:T(8,128)(2,1)}, bf16[4,128,512]{2,1,0:T(8,128)(2,1)}, bf16[1,4,128,512]{3,2,1,0:T(8,128)(2,1)}) fusion(pred[]{:T(512)S(6)} %or.3, bf16[3,128,512]{2,1,0:T(8,128)(2,1)S(1)} %copy-done.3, bf16[1,128,512]{2,1,0:T(8,128)(2,1)S(1)} %bitcast.8, bf16[4,128,512]{2,1,0:T(8,128)(2,1)S(1)} %collective-permute-done.refs_0_.refs_4_, ...), kind=kLoop, calls=%fused_computation.3 | loop fusion | flops 786432 | bytes 2621442 | tf_op jit(solution)/shard_map/jit(_where)/select_n | solution.py:195
  37.4 0.0 collective-permute-done.4.refs_3_
  37.4 3.5 %collective-permute-start.5 = (bf16[4,128,512]{2,1,0:T(8,128)(2,1)}, bf16[4,128,512]{2,1,0:T(8,128)(2,1)S(1)}, u32[]{:S(2)}, u32[]{:S(2)}) collective-permute-start(bf16[4,128,512]{2,1,0:T(8,128)(2,1)} %get-tuple-element.16), channel_id=1, source_target_pairs={{0,28},{2,30},{4,8},{6,10},{8,4},{10,6},{12,16},{14,18},{16,12},{1... | collective-permute-start | bytes 1572872 | tf_op jit(solution)/shard_map/ppermute | solution.py:37
  40.9 0.0 collective-permute-done.1.refs_1_
  40.9 2.4 %collective-permute-start.2 = (bf16[4,128,512]{2,1,0:T(8,128)(2,1)S(1)}, bf16[4,128,512]{2,1,0:T(8,128)(2,1)S(1)}, u32[]{:S(2)}, u32[]{:S(2)}) collective-permute-start(bf16[4,128,512]{2,1,0:T(8,128)(2,1)S(1)} %collective-permute-done.refs_0_.refs_4_), channel_id=1, source_target_pairs={{0,16},{2,18},{4,20},{6,22},{8,24},{10,26},{12,28},{14,30},{16,0},... | collective-permute-start | bytes 1572872 | tf_op jit(solution)/shard_map/ppermute | solution.py:37
  43.3 0.0 collective-permute-done.9.refs_7_
  43.3 0.0 copy-start.1
  43.3 3.1 %collective-permute-start.3 = (bf16[4,128,512]{2,1,0:T(8,128)(2,1)}, bf16[4,128,512]{2,1,0:T(8,128)(2,1)S(1)}, u32[]{:S(2)}, u32[]{:S(2)}) collective-permute-start(bf16[4,128,512]{2,1,0:T(8,128)(2,1)} %get-tuple-element.26), channel_id=1, source_target_pairs={{0,24},{2,26},{4,28},{6,30},{8,16},{10,18},{12,20},{14,22},{16,8},... | collective-permute-start | bytes 1572872 | tf_op jit(solution)/shard_map/ppermute | solution.py:37
  46.5 0.0 collective-permute-done.11.refs_2_
  46.5 1.9 %collective-permute-start.10 = (bf16[4,128,512]{2,1,0:T(8,128)(2,1)}, bf16[4,128,512]{2,1,0:T(8,128)(2,1)S(1)}, u32[]{:S(2)}, u32[]{:S(2)}) collective-permute-start(bf16[4,128,512]{2,1,0:T(8,128)(2,1)} %collective-permute-done.9.refs_7_), channel_id=1, source_target_pairs={{0,64},{2,66},{4,68},{6,70},{8,72},{10,74},{12,76},{14,78},{16,464... | collective-permute-start | bytes 1572872 | tf_op jit(solution)/shard_map/ppermute | solution.py:37
  48.4 0.0 collective-permute-done.6.refs_6_
  48.4 5.5 %collective-permute-start.7 = (bf16[4,128,512]{2,1,0:T(8,128)(2,1)}, bf16[4,128,512]{2,1,0:T(8,128)(2,1)S(1)}, u32[]{:S(2)}, u32[]{:S(2)}) collective-permute-start(bf16[4,128,512]{2,1,0:T(8,128)(2,1)} %collective-permute-done.6.refs_6_), channel_id=1, source_target_pairs={{0,448},{2,450},{4,452},{6,454},{8,456},{10,458},{12,460},{14,462}... | collective-permute-start | bytes 1572872 | tf_op jit(solution)/shard_map/ppermute | solution.py:37
  53.9 0.0 copy-done
  53.9 0.0 copy-done.1
  53.9 3.2 %shard_map.48 = (f32[4,128,384]{2,1,0:T(8,128)S(1)}, f32[4,128,128]{2,1,0:T(8,128)S(1)}, f32[4,128,128]{2,1,0:T(8,128)S(1)}, f32[8,128]{1,0:T(8,128)S(1)}) custom-call(bf16[128,512]{1,0:T(8,128)(2,1)S(1)} %copy-done, s32[15]{0:T(128)S(1)} %bitcast.6, bf16[4,128,512]{2,1,0:T(8,128)(2,1)S(1)} %pad_maximum_fusion.1.refs_0_, ...), custom_call_target="tpu_custom_call" | custom-call | flops 536870912 | bytes 4194304 | tf_op jit(solution)/shard_map/pallas_call | solution.py:139
  57.2 0.0 copy-start.2
  57.2 12.6 %collective-permute-done.5.refs_2_ = bf16[4,128,512]{2,1,0:T(8,128)(2,1)S(1)} collective-permute-done((bf16[4,128,512]{2,1,0:T(8,128)(2,1)}, bf16[4,128,512]{2,1,0:T(8,128)(2,1)S(1)}, u32[]{:S(2)}, u32[]{:S(2)}) %collective-permute-start.5) | collective-permute-done | bytes 524320 | tf_op jit(solution)/shard_map/ppermute | solution.py:37
  69.8 0.1 select_bitcast_fusion
  69.9 0.0 copy-done.2
  69.9 0.1 pad_maximum_fusion
  70.0 2.5 %collective-permute-start.12 = (bf16[2,4,128,512]{3,2,1,0:T(8,128)(2,1)S(1)}, bf16[2,4,128,512]{3,2,1,0:T(8,128)(2,1)S(1)}, u32[]{:S(2)}, u32[]{:S(2)}) collective-permute-start(bf16[2,4,128,512]{3,2,1,0:T(8,128)(2,1)S(1)} %pad_maximum_fusion), channel_id=1, source_target_pairs={{0,2},{2,0},{4,6},{6,4},{8,10},{10,8},{12,14},{14,12},{16,18},{18,... | collective-permute-start | bytes 3145736 | tf_op jit(solution)/shard_map/ppermute | solution.py:37
  72.5 4.5 %collective-permute-done.2.refs_3_.refs_0_ = bf16[4,128,512]{2,1,0:T(8,128)(2,1)S(1)} collective-permute-done((bf16[4,128,512]{2,1,0:T(8,128)(2,1)S(1)}, bf16[4,128,512]{2,1,0:T(8,128)(2,1)S(1)}, u32[]{:S(2)}, u32[]{:S(2)}) %collective-permute-start.2) | collective-permute-done | bytes 524320 | tf_op jit(solution)/shard_map/ppermute | solution.py:37
  77.0 0.0 collective-permute-done.3.refs_2_.refs_1_
  77.0 0.0 collective-permute-done.10.refs_1_.refs_4_
  77.0 0.0 collective-permute-done.7.refs_0_.refs_3_
  77.0 0.0 collective-permute-done.12.refs_5_
  77.0 1.9 %shard_map.50 = bf16[3,128,512]{2,1,0:T(8,128)(2,1)} custom-call(bf16[128,512]{1,0:T(8,128)(2,1)S(1)} %copy-done, bf16[4,128,512]{2,1,0:T(8,128)(2,1)S(1)} %collective-permute-done.2.refs_3_.refs_0_, bf16[4,128,512]{2,1,0:T(8,128)(2,1)S(1)} %collective-permute-done.3.refs_2_.refs_1_, bf16[4,128,512]{2,1,0:T(8,128)(2,1)S(1)} %collective-permute-done.5.refs_2_, ...), custom_call_target="tpu_custom_call" | custom-call | flops 402653184 | bytes 3145728 | tf_op jit(solution)/shard_map/pallas_call | solution.py:139
  (3 shorter events, 0.0 us)
Async XLA Ops:
  1.1 23.6 %collective-permute-start.8 = (bf16[4,128,512]{2,1,0:T(8,128)(2,1)S(1)}, bf16[4,128,512]{2,1,0:T(8,128)(2,1)S(1)}, u32[]{:S(2)}, u32[]{:S(2)}) collective-permute-start(bf16[4,128,512]{2,1,0:T(8,128)(2,1)S(1)} %pad_maximum_fusion.1.refs_0_), channel_id=1, source_target_pairs={{0,32},{2,34},{4,36},{6,38},{8,40},{10,42},{12,44},{14,46},{16,496... | collective-permute-start | bytes 1572872 | tf_op jit(solution)/shard_map/ppermute | solution.py:37
  5.5 25.9 %collective-permute-start = (bf16[4,128,512]{2,1,0:T(8,128)(2,1)S(1)}, bf16[4,128,512]{2,1,0:T(8,128)(2,1)S(1)}, u32[]{:S(2)}, u32[]{:S(2)}) collective-permute-start(bf16[4,128,512]{2,1,0:T(8,128)(2,1)S(1)} %pad_maximum_fusion.1.refs_0_), channel_id=1, source_target_pairs={{0,480},{2,482},{4,484},{6,486},{8,488},{10,490},{12,492},{14,494}... | collective-permute-start | bytes 1572872 | tf_op jit(solution)/shard_map/ppermute | solution.py:37
  15.0 22.5 %collective-permute-start.4 = (bf16[4,128,512]{2,1,0:T(8,128)(2,1)S(1)}, bf16[4,128,512]{2,1,0:T(8,128)(2,1)S(1)}, u32[]{:S(2)}, u32[]{:S(2)}) collective-permute-start(bf16[4,128,512]{2,1,0:T(8,128)(2,1)S(1)} %pad_maximum_fusion.1.refs_0_), channel_id=1, source_target_pairs={{0,16},{2,18},{4,20},{6,22},{8,24},{10,26},{12,28},{14,30},{16,0},... | collective-permute-start | bytes 1572872 | tf_op jit(solution)/shard_map/ppermute | solution.py:37
  18.2 22.7 %collective-permute-start.1 = (bf16[4,128,512]{2,1,0:T(8,128)(2,1)S(1)}, bf16[4,128,512]{2,1,0:T(8,128)(2,1)S(1)}, u32[]{:S(2)}, u32[]{:S(2)}) collective-permute-start(bf16[4,128,512]{2,1,0:T(8,128)(2,1)S(1)} %pad_maximum_fusion.1.refs_0_), channel_id=1, source_target_pairs={{0,4},{2,6},{4,0},{6,2},{8,12},{10,14},{12,8},{14,10},{16,20},{18,... | collective-permute-start | bytes 1572872 | tf_op jit(solution)/shard_map/ppermute | solution.py:37
  24.7 11.5 %copy-start.3 = (bf16[3,128,512]{2,1,0:T(8,128)(2,1)S(1)}, bf16[3,128,512]{2,1,0:T(8,128)(2,1)}, u32[]{:S(2)}) copy-start(bf16[3,128,512]{2,1,0:T(8,128)(2,1)} %param.6) | copy-start | bytes 1179652
  24.7 11.5 %copy-start.4 = (bf16[128,512]{1,0:T(8,128)(2,1)S(1)}, bf16[128,512]{1,0:T(8,128)(2,1)}, u32[]{:S(2)}) copy-start(bf16[128,512]{1,0:T(8,128)(2,1)} %param.5) | copy-start | bytes 393220
  24.7 18.6 %collective-permute-start.9 = (bf16[4,128,512]{2,1,0:T(8,128)(2,1)S(1)}, bf16[4,128,512]{2,1,0:T(8,128)(2,1)}, u32[]{:S(2)}, u32[]{:S(2)}) collective-permute-start(bf16[4,128,512]{2,1,0:T(8,128)(2,1)S(1)} %collective-permute-done.8.refs_0_.refs_5_), channel_id=1, source_target_pairs={{0,32},{2,34},{4,36},{6,38},{8,40},{10,42},{12,44},{14,46},{16,496... | collective-permute-start | bytes 1572872 | tf_op jit(solution)/shard_map/ppermute | solution.py:37
  26.7 19.8 %collective-permute-start.11 = (bf16[4,128,512]{2,1,0:T(8,128)(2,1)S(1)}, bf16[4,128,512]{2,1,0:T(8,128)(2,1)}, u32[]{:S(2)}, u32[]{:S(2)}) collective-permute-start(bf16[4,128,512]{2,1,0:T(8,128)(2,1)S(1)} %pad_maximum_fusion.1.refs_0_), channel_id=1, source_target_pairs={{0,8},{2,10},{4,12},{6,14},{8,0},{10,2},{12,4},{14,6},{16,24},{18,... | collective-permute-start | bytes 1572872 | tf_op jit(solution)/shard_map/ppermute | solution.py:37
  31.4 22.5 %copy-start = (bf16[128,512]{1,0:T(8,128)(2,1)S(1)}, bf16[128,512]{1,0:T(8,128)(2,1)}, u32[]{:S(2)}) copy-start(bf16[128,512]{1,0:T(8,128)(2,1)} %q_ref.3) | copy-start | bytes 393220
  31.4 17.0 %collective-permute-start.6 = (bf16[4,128,512]{2,1,0:T(8,128)(2,1)S(1)}, bf16[4,128,512]{2,1,0:T(8,128)(2,1)}, u32[]{:S(2)}, u32[]{:S(2)}) collective-permute-start(bf16[4,128,512]{2,1,0:T(8,128)(2,1)S(1)} %collective-permute-done.refs_0_.refs_4_), channel_id=1, source_target_pairs={{0,480},{2,482},{4,484},{6,486},{8,488},{10,490},{12,492},{14,494}... | collective-permute-start | bytes 1572872 | tf_op jit(solution)/shard_map/ppermute | solution.py:37
  37.4 32.4 %collective-permute-start.5 = (bf16[4,128,512]{2,1,0:T(8,128)(2,1)}, bf16[4,128,512]{2,1,0:T(8,128)(2,1)S(1)}, u32[]{:S(2)}, u32[]{:S(2)}) collective-permute-start(bf16[4,128,512]{2,1,0:T(8,128)(2,1)} %get-tuple-element.16), channel_id=1, source_target_pairs={{0,28},{2,30},{4,8},{6,10},{8,4},{10,6},{12,16},{14,18},{16,12},{1... | collective-permute-start | bytes 1572872 | tf_op jit(solution)/shard_map/ppermute | solution.py:37
  40.9 36.0 %collective-permute-start.2 = (bf16[4,128,512]{2,1,0:T(8,128)(2,1)S(1)}, bf16[4,128,512]{2,1,0:T(8,128)(2,1)S(1)}, u32[]{:S(2)}, u32[]{:S(2)}) collective-permute-start(bf16[4,128,512]{2,1,0:T(8,128)(2,1)S(1)} %collective-permute-done.refs_0_.refs_4_), channel_id=1, source_target_pairs={{0,16},{2,18},{4,20},{6,22},{8,24},{10,26},{12,28},{14,30},{16,0},... | collective-permute-start | bytes 1572872 | tf_op jit(solution)/shard_map/ppermute | solution.py:37
  43.3 10.6 %copy-start.1 = (s32[1,15,1,1]{1,3,2,0:T(1,128)S(1)}, s32[1,15,1,1]{1,3,2,0:T(1,128)}, u32[]{:S(2)}) copy-start(s32[1,15,1,1]{1,3,2,0:T(1,128)} %param.7) | copy-start | bytes 184
  43.3 33.6 %collective-permute-start.3 = (bf16[4,128,512]{2,1,0:T(8,128)(2,1)}, bf16[4,128,512]{2,1,0:T(8,128)(2,1)S(1)}, u32[]{:S(2)}, u32[]{:S(2)}) collective-permute-start(bf16[4,128,512]{2,1,0:T(8,128)(2,1)} %get-tuple-element.26), channel_id=1, source_target_pairs={{0,24},{2,26},{4,28},{6,30},{8,16},{10,18},{12,20},{14,22},{16,8},... | collective-permute-start | bytes 1572872 | tf_op jit(solution)/shard_map/ppermute | solution.py:37
  46.5 30.5 %collective-permute-start.10 = (bf16[4,128,512]{2,1,0:T(8,128)(2,1)}, bf16[4,128,512]{2,1,0:T(8,128)(2,1)S(1)}, u32[]{:S(2)}, u32[]{:S(2)}) collective-permute-start(bf16[4,128,512]{2,1,0:T(8,128)(2,1)} %collective-permute-done.9.refs_7_), channel_id=1, source_target_pairs={{0,64},{2,66},{4,68},{6,70},{8,72},{10,74},{12,76},{14,78},{16,464... | collective-permute-start | bytes 1572872 | tf_op jit(solution)/shard_map/ppermute | solution.py:37
  48.4 28.5 %collective-permute-start.7 = (bf16[4,128,512]{2,1,0:T(8,128)(2,1)}, bf16[4,128,512]{2,1,0:T(8,128)(2,1)S(1)}, u32[]{:S(2)}, u32[]{:S(2)}) collective-permute-start(bf16[4,128,512]{2,1,0:T(8,128)(2,1)} %collective-permute-done.6.refs_6_), channel_id=1, source_target_pairs={{0,448},{2,450},{4,452},{6,454},{8,456},{10,458},{12,460},{14,462}... | collective-permute-start | bytes 1572872 | tf_op jit(solution)/shard_map/ppermute | solution.py:37
  57.2 12.7 %copy-start.2 = (bf16[1,4,128,512]{3,2,1,0:T(8,128)(2,1)S(1)}, bf16[1,4,128,512]{3,2,1,0:T(8,128)(2,1)}, u32[]{:S(2)}) copy-start(bf16[1,4,128,512]{3,2,1,0:T(8,128)(2,1)} %get-tuple-element.27) | copy-start | bytes 1572868
  70.0 7.0 %collective-permute-start.12 = (bf16[2,4,128,512]{3,2,1,0:T(8,128)(2,1)S(1)}, bf16[2,4,128,512]{3,2,1,0:T(8,128)(2,1)S(1)}, u32[]{:S(2)}, u32[]{:S(2)}) collective-permute-start(bf16[2,4,128,512]{3,2,1,0:T(8,128)(2,1)S(1)} %pad_maximum_fusion), channel_id=1, source_target_pairs={{0,2},{2,0},{4,6},{6,4},{8,10},{10,8},{12,14},{14,12},{16,18},{18,... | collective-permute-start | bytes 3145736 | tf_op jit(solution)/shard_map/ppermute | solution.py:37

commit v5 on v4

--- a/solution.py
+++ b/solution.py
@@ -41,12 +41,15 @@
     return lax.optimization_barrier((block, *others))[0]
 
 
-def weigh(q_ref, blocks, biases, window, before=None):
-    rows = q_ref.shape[0]
+def score(q_ref, blocks, window):
     keys = jnp.concatenate([b[0, :, window] for b in blocks], axis=0)
-    scores = lax.dot_general(
+    return lax.dot_general(
         q_ref[:, window], keys, (((1,), (1,)), ((), ())), preferred_element_type=jnp.float32
     ) * (math.log2(math.e) / math.sqrt(HD))
+
+
+def weigh(scores, blocks, biases, before=None):
+    rows = scores.shape[0]
     parts = [
         scores[:, j * rows:(j + 1) * rows] + biases[j][...] for j in range(len(blocks))
     ]
@@ -80,7 +83,7 @@
     biases = [now_ref.at[j:j + 1] for j in range(len(rules))]
     for head in range(q_ref.shape[1] // HD):
         window = slice(head * HD, (head + 1) * HD)
-        largest, total, weights = weigh(q_ref, blocks, biases, window)
+        largest, total, weights = weigh(score(q_ref, blocks, window), blocks, biases)
         max_ref[head] = jnp.broadcast_to(largest, max_ref.shape[1:])
         sum_ref[head] = jnp.broadcast_to(total, sum_ref.shape[1:])
         acc_ref[head] = mix(weights, blocks, window)
@@ -93,7 +96,8 @@
     biases = [bias_ref.at[j:j + 1] for j in range(len(blocks))]
     heads = range(q_ref.shape[1] // HD)
     windows = [slice(head * HD, (head + 1) * HD) for head in heads]
-    weighed = [weigh(q_ref, blocks, biases, windows[head], max_ref[head]) for head in heads]
+    scores = [score(q_ref, blocks, window) for window in windows]
+    weighed = [weigh(scores[head], blocks, biases, max_ref[head]) for head in heads]
     for head in heads:
         largest, total, weights = weighed[head]
         acc = mix(weights, blocks, windows[head])

time: 80.2 us -> 80.2 us (level)
  no operation moved by 1% of the time
where the time goes in v5:
time: 80.2 us; the launch traced here: 79 us
  starting transfers between devices  50.4 us (63%)
  waiting for transfers between devices  20.5 us (26%)
  Pallas kernels  5.19 us (6%)
  other arithmetic  2.5 us (3%)
    ppermute x13, starting transfers between devices, send(): return lax.ppermute(block, 'ctx', pairs)  50.4 us
    ppermute x13, waiting for transfers between devices, send(): return lax.ppermute(block, 'ctx', pairs)  20.5 us
    pallas_call x2, Pallas kernels, attend(): pl.pallas_call(kernel, out_shape=shapes, in_specs=in_specs, out_specs=out...  5.18 us
  transfers between devices with their start and end apart: 13, of which 3 were waited for; matrix products, arithmetic and copies ran while one was open for 2% of the time, Pallas kernels for 4%

profile of v5, /device:TPU:1, one launch (start us, length us, event | category | flops | bytes accessed | tf_op | source)
XLA Modules:
  0.0 79.0 jit_solution(13153058015451903315)
XLA Ops:
  0.0 1.1 %pad_maximum_fusion.1.refs_0_ = bf16[4,128,512]{2,1,0:T(8,128)(2,1)S(1)} fusion(bf16[3,128,512]{2,1,0:T(8,128)(2,1)} %param.6, bf16[1,128,512]{2,1,0:T(8,128)(2,1)} %bitcast.7), kind=kLoop, calls=%fused_computation.1 | loop fusion | flops 262144 | bytes 1048576 | tf_op jit(solution)/shard_map/concatenate | solution.py:184
  1.1 4.4 %collective-permute-start.8 = (bf16[4,128,512]{2,1,0:T(8,128)(2,1)S(1)}, bf16[4,128,512]{2,1,0:T(8,128)(2,1)S(1)}, u32[]{:S(2)}, u32[]{:S(2)}) collective-permute-start(bf16[4,128,512]{2,1,0:T(8,128)(2,1)S(1)} %pad_maximum_fusion.1.refs_0_), channel_id=1, source_target_pairs={{0,32},{2,34},{4,36},{6,38},{8,40},{10,42},{12,44},{14,46},{16,496... | collective-permute-start | bytes 1572872 | tf_op jit(solution)/shard_map/ppermute | solution.py:37
  5.5 9.5 %collective-permute-start = (bf16[4,128,512]{2,1,0:T(8,128)(2,1)S(1)}, bf16[4,128,512]{2,1,0:T(8,128)(2,1)S(1)}, u32[]{:S(2)}, u32[]{:S(2)}) collective-permute-start(bf16[4,128,512]{2,1,0:T(8,128)(2,1)S(1)} %pad_maximum_fusion.1.refs_0_), channel_id=1, source_target_pairs={{0,480},{2,482},{4,484},{6,486},{8,488},{10,490},{12,492},{14,494}... | collective-permute-start | bytes 1572872 | tf_op jit(solution)/shard_map/ppermute | solution.py:37
  15.0 3.2 %collective-permute-start.4 = (bf16[4,128,512]{2,1,0:T(8,128)(2,1)S(1)}, bf16[4,128,512]{2,1,0:T(8,128)(2,1)S(1)}, u32[]{:S(2)}, u32[]{:S(2)}) collective-permute-start(bf16[4,128,512]{2,1,0:T(8,128)(2,1)S(1)} %pad_maximum_fusion.1.refs_0_), channel_id=1, source_target_pairs={{0,16},{2,18},{4,20},{6,22},{8,24},{10,26},{12,28},{14,30},{16,0},... | collective-permute-start | bytes 1572872 | tf_op jit(solution)/shard_map/ppermute | solution.py:37
  18.2 3.1 %collective-permute-start.1 = (bf16[4,128,512]{2,1,0:T(8,128)(2,1)S(1)}, bf16[4,128,512]{2,1,0:T(8,128)(2,1)S(1)}, u32[]{:S(2)}, u32[]{:S(2)}) collective-permute-start(bf16[4,128,512]{2,1,0:T(8,128)(2,1)S(1)} %pad_maximum_fusion.1.refs_0_), channel_id=1, source_target_pairs={{0,4},{2,6},{4,0},{6,2},{8,12},{10,14},{12,8},{14,10},{16,20},{18,... | collective-permute-start | bytes 1572872 | tf_op jit(solution)/shard_map/ppermute | solution.py:37
  21.3 3.3 %collective-permute-done.8.refs_0_.refs_5_ = bf16[4,128,512]{2,1,0:T(8,128)(2,1)S(1)} collective-permute-done((bf16[4,128,512]{2,1,0:T(8,128)(2,1)S(1)}, bf16[4,128,512]{2,1,0:T(8,128)(2,1)S(1)}, u32[]{:S(2)}, u32[]{:S(2)}) %collective-permute-start.8) | collective-permute-done | bytes 524320 | tf_op jit(solution)/shard_map/ppermute | solution.py:37
  24.7 0.0 copy-start.3
  24.7 0.0 copy-start.4
  24.7 2.0 %collective-permute-start.9 = (bf16[4,128,512]{2,1,0:T(8,128)(2,1)S(1)}, bf16[4,128,512]{2,1,0:T(8,128)(2,1)}, u32[]{:S(2)}, u32[]{:S(2)}) collective-permute-start(bf16[4,128,512]{2,1,0:T(8,128)(2,1)S(1)} %collective-permute-done.8.refs_0_.refs_5_), channel_id=1, source_target_pairs={{0,32},{2,34},{4,36},{6,38},{8,40},{10,42},{12,44},{14,46},{16,496... | collective-permute-start | bytes 1572872 | tf_op jit(solution)/shard_map/ppermute | solution.py:37
  26.7 4.7 %collective-permute-start.11 = (bf16[4,128,512]{2,1,0:T(8,128)(2,1)S(1)}, bf16[4,128,512]{2,1,0:T(8,128)(2,1)}, u32[]{:S(2)}, u32[]{:S(2)}) collective-permute-start(bf16[4,128,512]{2,1,0:T(8,128)(2,1)S(1)} %pad_maximum_fusion.1.refs_0_), channel_id=1, source_target_pairs={{0,8},{2,10},{4,12},{6,14},{8,0},{10,2},{12,4},{14,6},{16,24},{18,... | collective-permute-start | bytes 1572872 | tf_op jit(solution)/shard_map/ppermute | solution.py:37
  31.4 0.0 collective-permute-done.refs_0_.refs_4_
  31.4 0.0 copy-start
  31.4 4.7 %collective-permute-start.6 = (bf16[4,128,512]{2,1,0:T(8,128)(2,1)S(1)}, bf16[4,128,512]{2,1,0:T(8,128)(2,1)}, u32[]{:S(2)}, u32[]{:S(2)}) collective-permute-start(bf16[4,128,512]{2,1,0:T(8,128)(2,1)S(1)} %collective-permute-done.refs_0_.refs_4_), channel_id=1, source_target_pairs={{0,480},{2,482},{4,484},{6,486},{8,488},{10,490},{12,492},{14,494}... | collective-permute-start | bytes 1572872 | tf_op jit(solution)/shard_map/ppermute | solution.py:37
  36.1 0.0 copy-done.3
  36.1 0.0 copy-done.4
  36.1 1.3 %broadcast_select_fusion = (bf16[4,128,512]{2,1,0:T(8,128)(2,1)}, bf16[4,128,512]{2,1,0:T(8,128)(2,1)}, bf16[1,4,128,512]{3,2,1,0:T(8,128)(2,1)}) fusion(pred[]{:T(512)S(6)} %or.3, bf16[3,128,512]{2,1,0:T(8,128)(2,1)S(1)} %copy-done.3, bf16[1,128,512]{2,1,0:T(8,128)(2,1)S(1)} %bitcast.8, bf16[4,128,512]{2,1,0:T(8,128)(2,1)S(1)} %collective-permute-done.refs_0_.refs_4_, ...), kind=kLoop, calls=%fused_computation.3 | loop fusion | flops 786432 | bytes 2621442 | tf_op jit(solution)/shard_map/jit(_where)/select_n | solution.py:199
  37.4 0.0 collective-permute-done.4.refs_3_
  37.4 3.5 %collective-permute-start.5 = (bf16[4,128,512]{2,1,0:T(8,128)(2,1)}, bf16[4,128,512]{2,1,0:T(8,128)(2,1)S(1)}, u32[]{:S(2)}, u32[]{:S(2)}) collective-permute-start(bf16[4,128,512]{2,1,0:T(8,128)(2,1)} %get-tuple-element.16), channel_id=1, source_target_pairs={{0,28},{2,30},{4,8},{6,10},{8,4},{10,6},{12,16},{14,18},{16,12},{1... | collective-permute-start | bytes 1572872 | tf_op jit(solution)/shard_map/ppermute | solution.py:37
  40.9 0.0 collective-permute-done.1.refs_1_
  40.9 2.4 %collective-permute-start.2 = (bf16[4,128,512]{2,1,0:T(8,128)(2,1)S(1)}, bf16[4,128,512]{2,1,0:T(8,128)(2,1)S(1)}, u32[]{:S(2)}, u32[]{:S(2)}) collective-permute-start(bf16[4,128,512]{2,1,0:T(8,128)(2,1)S(1)} %collective-permute-done.refs_0_.refs_4_), channel_id=1, source_target_pairs={{0,16},{2,18},{4,20},{6,22},{8,24},{10,26},{12,28},{14,30},{16,0},... | collective-permute-start | bytes 1572872 | tf_op jit(solution)/shard_map/ppermute | solution.py:37
  43.3 0.0 collective-permute-done.9.refs_7_
  43.3 0.0 copy-start.1
  43.3 3.1 %collective-permute-start.3 = (bf16[4,128,512]{2,1,0:T(8,128)(2,1)}, bf16[4,128,512]{2,1,0:T(8,128)(2,1)S(1)}, u32[]{:S(2)}, u32[]{:S(2)}) collective-permute-start(bf16[4,128,512]{2,1,0:T(8,128)(2,1)} %get-tuple-element.26), channel_id=1, source_target_pairs={{0,24},{2,26},{4,28},{6,30},{8,16},{10,18},{12,20},{14,22},{16,8},... | collective-permute-start | bytes 1572872 | tf_op jit(solution)/shard_map/ppermute | solution.py:37
  46.5 0.0 collective-permute-done.11.refs_2_
  46.5 1.9 %collective-permute-start.10 = (bf16[4,128,512]{2,1,0:T(8,128)(2,1)}, bf16[4,128,512]{2,1,0:T(8,128)(2,1)S(1)}, u32[]{:S(2)}, u32[]{:S(2)}) collective-permute-start(bf16[4,128,512]{2,1,0:T(8,128)(2,1)} %collective-permute-done.9.refs_7_), channel_id=1, source_target_pairs={{0,64},{2,66},{4,68},{6,70},{8,72},{10,74},{12,76},{14,78},{16,464... | collective-permute-start | bytes 1572872 | tf_op jit(solution)/shard_map/ppermute | solution.py:37
  48.4 0.0 collective-permute-done.6.refs_6_
  48.4 5.5 %collective-permute-start.7 = (bf16[4,128,512]{2,1,0:T(8,128)(2,1)}, bf16[4,128,512]{2,1,0:T(8,128)(2,1)S(1)}, u32[]{:S(2)}, u32[]{:S(2)}) collective-permute-start(bf16[4,128,512]{2,1,0:T(8,128)(2,1)} %collective-permute-done.6.refs_6_), channel_id=1, source_target_pairs={{0,448},{2,450},{4,452},{6,454},{8,456},{10,458},{12,460},{14,462}... | collective-permute-start | bytes 1572872 | tf_op jit(solution)/shard_map/ppermute | solution.py:37
  53.9 0.0 copy-done
  53.9 0.0 copy-done.1
  53.9 3.2 %shard_map.48 = (f32[4,128,384]{2,1,0:T(8,128)S(1)}, f32[4,128,128]{2,1,0:T(8,128)S(1)}, f32[4,128,128]{2,1,0:T(8,128)S(1)}, f32[8,128]{1,0:T(8,128)S(1)}) custom-call(bf16[128,512]{1,0:T(8,128)(2,1)S(1)} %copy-done, s32[15]{0:T(128)S(1)} %bitcast.6, bf16[4,128,512]{2,1,0:T(8,128)(2,1)S(1)} %pad_maximum_fusion.1.refs_0_, ...), custom_call_target="tpu_custom_call" | custom-call | flops 536870912 | bytes 4194304 | tf_op jit(solution)/shard_map/pallas_call | solution.py:143
  57.2 0.0 copy-start.2
  57.2 12.6 %collective-permute-done.5.refs_2_ = bf16[4,128,512]{2,1,0:T(8,128)(2,1)S(1)} collective-permute-done((bf16[4,128,512]{2,1,0:T(8,128)(2,1)}, bf16[4,128,512]{2,1,0:T(8,128)(2,1)S(1)}, u32[]{:S(2)}, u32[]{:S(2)}) %collective-permute-start.5) | collective-permute-done | bytes 524320 | tf_op jit(solution)/shard_map/ppermute | solution.py:37
  69.8 0.1 select_bitcast_fusion
  69.9 0.0 copy-done.2
  69.9 0.1 pad_maximum_fusion
  70.0 2.5 %collective-permute-start.12 = (bf16[2,4,128,512]{3,2,1,0:T(8,128)(2,1)S(1)}, bf16[2,4,128,512]{3,2,1,0:T(8,128)(2,1)S(1)}, u32[]{:S(2)}, u32[]{:S(2)}) collective-permute-start(bf16[2,4,128,512]{3,2,1,0:T(8,128)(2,1)S(1)} %pad_maximum_fusion), channel_id=1, source_target_pairs={{0,2},{2,0},{4,6},{6,4},{8,10},{10,8},{12,14},{14,12},{16,18},{18,... | collective-permute-start | bytes 3145736 | tf_op jit(solution)/shard_map/ppermute | solution.py:37
  72.5 4.5 %collective-permute-done.2.refs_3_.refs_0_ = bf16[4,128,512]{2,1,0:T(8,128)(2,1)S(1)} collective-permute-done((bf16[4,128,512]{2,1,0:T(8,128)(2,1)S(1)}, bf16[4,128,512]{2,1,0:T(8,128)(2,1)S(1)}, u32[]{:S(2)}, u32[]{:S(2)}) %collective-permute-start.2) | collective-permute-done | bytes 524320 | tf_op jit(solution)/shard_map/ppermute | solution.py:37
  77.0 0.0 collective-permute-done.3.refs_2_.refs_1_
  77.0 0.0 collective-permute-done.10.refs_1_.refs_4_
  77.0 0.0 collective-permute-done.7.refs_0_.refs_3_
  77.0 0.0 collective-permute-done.12.refs_5_
  77.0 2.0 %shard_map.50 = bf16[3,128,512]{2,1,0:T(8,128)(2,1)} custom-call(bf16[128,512]{1,0:T(8,128)(2,1)S(1)} %copy-done, bf16[4,128,512]{2,1,0:T(8,128)(2,1)S(1)} %collective-permute-done.2.refs_3_.refs_0_, bf16[4,128,512]{2,1,0:T(8,128)(2,1)S(1)} %collective-permute-done.3.refs_2_.refs_1_, bf16[4,128,512]{2,1,0:T(8,128)(2,1)S(1)} %collective-permute-done.5.refs_2_, ...), custom_call_target="tpu_custom_call" | custom-call | flops 402653184 | bytes 3145728 | tf_op jit(solution)/shard_map/pallas_call | solution.py:143
  (3 shorter events, 0.0 us)
Async XLA Ops:
  1.1 23.6 %collective-permute-start.8 = (bf16[4,128,512]{2,1,0:T(8,128)(2,1)S(1)}, bf16[4,128,512]{2,1,0:T(8,128)(2,1)S(1)}, u32[]{:S(2)}, u32[]{:S(2)}) collective-permute-start(bf16[4,128,512]{2,1,0:T(8,128)(2,1)S(1)} %pad_maximum_fusion.1.refs_0_), channel_id=1, source_target_pairs={{0,32},{2,34},{4,36},{6,38},{8,40},{10,42},{12,44},{14,46},{16,496... | collective-permute-start | bytes 1572872 | tf_op jit(solution)/shard_map/ppermute | solution.py:37
  5.5 25.9 %collective-permute-start = (bf16[4,128,512]{2,1,0:T(8,128)(2,1)S(1)}, bf16[4,128,512]{2,1,0:T(8,128)(2,1)S(1)}, u32[]{:S(2)}, u32[]{:S(2)}) collective-permute-start(bf16[4,128,512]{2,1,0:T(8,128)(2,1)S(1)} %pad_maximum_fusion.1.refs_0_), channel_id=1, source_target_pairs={{0,480},{2,482},{4,484},{6,486},{8,488},{10,490},{12,492},{14,494}... | collective-permute-start | bytes 1572872 | tf_op jit(solution)/shard_map/ppermute | solution.py:37
  15.0 22.5 %collective-permute-start.4 = (bf16[4,128,512]{2,1,0:T(8,128)(2,1)S(1)}, bf16[4,128,512]{2,1,0:T(8,128)(2,1)S(1)}, u32[]{:S(2)}, u32[]{:S(2)}) collective-permute-start(bf16[4,128,512]{2,1,0:T(8,128)(2,1)S(1)} %pad_maximum_fusion.1.refs_0_), channel_id=1, source_target_pairs={{0,16},{2,18},{4,20},{6,22},{8,24},{10,26},{12,28},{14,30},{16,0},... | collective-permute-start | bytes 1572872 | tf_op jit(solution)/shard_map/ppermute | solution.py:37
  18.2 22.7 %collective-permute-start.1 = (bf16[4,128,512]{2,1,0:T(8,128)(2,1)S(1)}, bf16[4,128,512]{2,1,0:T(8,128)(2,1)S(1)}, u32[]{:S(2)}, u32[]{:S(2)}) collective-permute-start(bf16[4,128,512]{2,1,0:T(8,128)(2,1)S(1)} %pad_maximum_fusion.1.refs_0_), channel_id=1, source_target_pairs={{0,4},{2,6},{4,0},{6,2},{8,12},{10,14},{12,8},{14,10},{16,20},{18,... | collective-permute-start | bytes 1572872 | tf_op jit(solution)/shard_map/ppermute | solution.py:37
  24.7 11.5 %copy-start.3 = (bf16[3,128,512]{2,1,0:T(8,128)(2,1)S(1)}, bf16[3,128,512]{2,1,0:T(8,128)(2,1)}, u32[]{:S(2)}) copy-start(bf16[3,128,512]{2,1,0:T(8,128)(2,1)} %param.6) | copy-start | bytes 1179652
  24.7 11.5 %copy-start.4 = (bf16[128,512]{1,0:T(8,128)(2,1)S(1)}, bf16[128,512]{1,0:T(8,128)(2,1)}, u32[]{:S(2)}) copy-start(bf16[128,512]{1,0:T(8,128)(2,1)} %param.5) | copy-start | bytes 393220
  24.7 18.6 %collective-permute-start.9 = (bf16[4,128,512]{2,1,0:T(8,128)(2,1)S(1)}, bf16[4,128,512]{2,1,0:T(8,128)(2,1)}, u32[]{:S(2)}, u32[]{:S(2)}) collective-permute-start(bf16[4,128,512]{2,1,0:T(8,128)(2,1)S(1)} %collective-permute-done.8.refs_0_.refs_5_), channel_id=1, source_target_pairs={{0,32},{2,34},{4,36},{6,38},{8,40},{10,42},{12,44},{14,46},{16,496... | collective-permute-start | bytes 1572872 | tf_op jit(solution)/shard_map/ppermute | solution.py:37
  26.7 19.8 %collective-permute-start.11 = (bf16[4,128,512]{2,1,0:T(8,128)(2,1)S(1)}, bf16[4,128,512]{2,1,0:T(8,128)(2,1)}, u32[]{:S(2)}, u32[]{:S(2)}) collective-permute-start(bf16[4,128,512]{2,1,0:T(8,128)(2,1)S(1)} %pad_maximum_fusion.1.refs_0_), channel_id=1, source_target_pairs={{0,8},{2,10},{4,12},{6,14},{8,0},{10,2},{12,4},{14,6},{16,24},{18,... | collective-permute-start | bytes 1572872 | tf_op jit(solution)/shard_map/ppermute | solution.py:37
  31.4 22.5 %copy-start = (bf16[128,512]{1,0:T(8,128)(2,1)S(1)}, bf16[128,512]{1,0:T(8,128)(2,1)}, u32[]{:S(2)}) copy-start(bf16[128,512]{1,0:T(8,128)(2,1)} %q_ref.3) | copy-start | bytes 393220
  31.4 17.0 %collective-permute-start.6 = (bf16[4,128,512]{2,1,0:T(8,128)(2,1)S(1)}, bf16[4,128,512]{2,1,0:T(8,128)(2,1)}, u32[]{:S(2)}, u32[]{:S(2)}) collective-permute-start(bf16[4,128,512]{2,1,0:T(8,128)(2,1)S(1)} %collective-permute-done.refs_0_.refs_4_), channel_id=1, source_target_pairs={{0,480},{2,482},{4,484},{6,486},{8,488},{10,490},{12,492},{14,494}... | collective-permute-start | bytes 1572872 | tf_op jit(solution)/shard_map/ppermute | solution.py:37
  37.4 32.4 %collective-permute-start.5 = (bf16[4,128,512]{2,1,0:T(8,128)(2,1)}, bf16[4,128,512]{2,1,0:T(8,128)(2,1)S(1)}, u32[]{:S(2)}, u32[]{:S(2)}) collective-permute-start(bf16[4,128,512]{2,1,0:T(8,128)(2,1)} %get-tuple-element.16), channel_id=1, source_target_pairs={{0,28},{2,30},{4,8},{6,10},{8,4},{10,6},{12,16},{14,18},{16,12},{1... | collective-permute-start | bytes 1572872 | tf_op jit(solution)/shard_map/ppermute | solution.py:37
  40.9 36.0 %collective-permute-start.2 = (bf16[4,128,512]{2,1,0:T(8,128)(2,1)S(1)}, bf16[4,128,512]{2,1,0:T(8,128)(2,1)S(1)}, u32[]{:S(2)}, u32[]{:S(2)}) collective-permute-start(bf16[4,128,512]{2,1,0:T(8,128)(2,1)S(1)} %collective-permute-done.refs_0_.refs_4_), channel_id=1, source_target_pairs={{0,16},{2,18},{4,20},{6,22},{8,24},{10,26},{12,28},{14,30},{16,0},... | collective-permute-start | bytes 1572872 | tf_op jit(solution)/shard_map/ppermute | solution.py:37
  43.3 10.6 %copy-start.1 = (s32[1,15,1,1]{1,3,2,0:T(1,128)S(1)}, s32[1,15,1,1]{1,3,2,0:T(1,128)}, u32[]{:S(2)}) copy-start(s32[1,15,1,1]{1,3,2,0:T(1,128)} %param.7) | copy-start | bytes 184
  43.3 33.6 %collective-permute-start.3 = (bf16[4,128,512]{2,1,0:T(8,128)(2,1)}, bf16[4,128,512]{2,1,0:T(8,128)(2,1)S(1)}, u32[]{:S(2)}, u32[]{:S(2)}) collective-permute-start(bf16[4,128,512]{2,1,0:T(8,128)(2,1)} %get-tuple-element.26), channel_id=1, source_target_pairs={{0,24},{2,26},{4,28},{6,30},{8,16},{10,18},{12,20},{14,22},{16,8},... | collective-permute-start | bytes 1572872 | tf_op jit(solution)/shard_map/ppermute | solution.py:37
  46.5 30.5 %collective-permute-start.10 = (bf16[4,128,512]{2,1,0:T(8,128)(2,1)}, bf16[4,128,512]{2,1,0:T(8,128)(2,1)S(1)}, u32[]{:S(2)}, u32[]{:S(2)}) collective-permute-start(bf16[4,128,512]{2,1,0:T(8,128)(2,1)} %collective-permute-done.9.refs_7_), channel_id=1, source_target_pairs={{0,64},{2,66},{4,68},{6,70},{8,72},{10,74},{12,76},{14,78},{16,464... | collective-permute-start | bytes 1572872 | tf_op jit(solution)/shard_map/ppermute | solution.py:37
  48.4 28.5 %collective-permute-start.7 = (bf16[4,128,512]{2,1,0:T(8,128)(2,1)}, bf16[4,128,512]{2,1,0:T(8,128)(2,1)S(1)}, u32[]{:S(2)}, u32[]{:S(2)}) collective-permute-start(bf16[4,128,512]{2,1,0:T(8,128)(2,1)} %collective-permute-done.6.refs_6_), channel_id=1, source_target_pairs={{0,448},{2,450},{4,452},{6,454},{8,456},{10,458},{12,460},{14,462}... | collective-permute-start | bytes 1572872 | tf_op jit(solution)/shard_map/ppermute | solution.py:37
  57.2 12.7 %copy-start.2 = (bf16[1,4,128,512]{3,2,1,0:T(8,128)(2,1)S(1)}, bf16[1,4,128,512]{3,2,1,0:T(8,128)(2,1)}, u32[]{:S(2)}) copy-start(bf16[1,4,128,512]{3,2,1,0:T(8,128)(2,1)} %get-tuple-element.27) | copy-start | bytes 1572868
  70.0 7.0 %collective-permute-start.12 = (bf16[2,4,128,512]{3,2,1,0:T(8,128)(2,1)S(1)}, bf16[2,4,128,512]{3,2,1,0:T(8,128)(2,1)S(1)}, u32[]{:S(2)}, u32[]{:S(2)}) collective-permute-start(bf16[2,4,128,512]{3,2,1,0:T(8,128)(2,1)S(1)} %pad_maximum_fusion), channel_id=1, source_target_pairs={{0,2},{2,0},{4,6},{6,4},{8,10},{10,8},{12,14},{14,12},{16,18},{18,... | collective-permute-start | bytes 3145736 | tf_op jit(solution)/shard_map/ppermute | solution.py:37
